TPU v7x, 128 devices: a whole 4x4x4 slice. The times are simulated.
128 devices in a mesh: row: 8 (over y, core), col: 16 (over x, z).
Axes of the slice: x: 4, y: 4, z: 4, core: 2. Of those that a mesh axis runs over, the one named last changes fastest.
Arguments:
- features: bfloat16 [65536, 64], P(('row', 'col')), may hold values from -12 to 12
- task_id: int32 [65536], P(('row', 'col')), may hold values from 0 to 255
- task_count: int32 [256], replicated, may hold values from 103 to 409, as said below
- task_rank: int32 [65536], P(('row', 'col')), may hold values from 0 to 408, as said below
- probes: bfloat16 [65536, 32], P(('row', 'col')), may hold values from -6 to 6
- net_w: bfloat16 [64, 64], replicated, may hold values from -0.75 to 0.75
- net_b: float32 [64], replicated, may hold values from -3 to 3
- inv_scale: float32 [64], replicated, may hold values from 0.2 to 0.7
- task_mix: float32 [256, 4], replicated, may hold values from -3 to 3
- task_diag: float32 [256], replicated, may hold values from 0.2 to 1
- task_noise: float32 [256], replicated, may hold values from 0.05 to 0.5
Outputs:
- residual: float32 [65536, 32], P(('row', 'col'))
- direction: float32 [65536, 32], P(('row', 'col'))
- step_length: float32 [32], replicated
- update_weight: float32 [32], replicated
Inputs may be any that keep to these rules, and one draw needn't show every extreme that they name: Task t holds exactly task_count[t] observations; their task_rank values are 0 to task_count[t] - 1, each once. `task_rank`: every device holds exactly 4 observations whose sorted position falls in each device's block of 512 positions.
All inputs are finite; a program needn't handle non-finite values.
Results may differ from a plain program's by a relative error of at most 0.0044.
The roundings to bfloat16 on the way count: a program that leaves them out, or rounds other values in their place, can miss the bound.
Values may be sent and summed in bfloat16 or wider, within the bound.
No kernel may reach another device: no remote copies, remote signals or barrier semaphores. Data moves between devices by JAX's collectives and lax.ppermute only.
A program may use at most 64 MiB of HBM per device.

v0:
```python
import math

import jax
import jax.numpy as jnp
from jax import lax
from jax.sharding import PartitionSpec as P


def lookup(tasks, table):
    onehot = (tasks[:, None] == jnp.arange(table.shape[0], dtype=jnp.int32)[None, :]).astype(
        jnp.float32
    )
    return jnp.dot(onehot, table, precision=lax.Precision.HIGHEST)


def permute_rows(placing, values):
    return jnp.dot(placing.astype(jnp.bfloat16), values, preferred_element_type=jnp.float32).astype(
        jnp.bfloat16
    )


def permute_ints(placing, values):
    return jnp.sum(jnp.where(placing, values[None, :], 0), axis=1).astype(jnp.int32)


def make_scaled(values, weights):
    count = values.shape[0]
    spread = weights[:, :, None] * values.astype(jnp.float32)[:, None, :]
    return jnp.concatenate([spread.reshape(count, -1).astype(jnp.bfloat16), values], axis=1)


def body(
    features,
    task_id,
    task_count,
    task_rank,
    probes,
    net_w,
    net_b,
    inv_scale,
    task_mix,
    task_diag,
    task_noise,
):
    rows_dev = features.shape[0]
    n_col = lax.axis_size("col")
    ntask = task_count.shape[0]
    rank_q = task_mix.shape[1]
    width = probes.shape[1]
    offsets = jnp.cumsum(task_count) - task_count
    hit = task_id[:, None] == jnp.arange(ntask, dtype=jnp.int32)[None, :]
    position = jnp.sum(jnp.where(hit, offsets[None, :], 0), axis=1) + task_rank
    hidden = jnp.tanh(jnp.dot(features, net_w, preferred_element_type=jnp.float32) + net_b)
    latent = (hidden * inv_scale).astype(jnp.bfloat16)
    order = jnp.sum((position[None, :] < position[:, None]).astype(jnp.int32), axis=1)
    placing = order[None, :] == jnp.arange(rows_dev, dtype=jnp.int32)[:, None]
    packed_z = permute_rows(placing, latent)
    packed_v = permute_rows(placing, probes)
    packed_t = permute_ints(placing, task_id)
    packed_p = permute_ints(placing, position)
    got_z, got_v, got_t, got_p = (
        lax.all_to_all(packed_z, ("row", "col"), split_axis=0, concat_axis=0, tiled=True),
        lax.all_to_all(packed_v, ("row", "col"), split_axis=0, concat_axis=0, tiled=True),
        lax.all_to_all(packed_t, ("row", "col"), split_axis=0, concat_axis=0, tiled=True),
        lax.all_to_all(packed_p, ("row", "col"), split_axis=0, concat_axis=0, tiled=True),
    )
    flat_index = lax.axis_index("row") * n_col + lax.axis_index("col")
    local_place = got_p - flat_index * rows_dev
    sorting = local_place[None, :] == jnp.arange(rows_dev, dtype=jnp.int32)[:, None]
    sorted_z = permute_rows(sorting, got_z)
    sorted_v = permute_rows(sorting, got_v)
    sorted_t = permute_ints(sorting, got_t)
    table = jnp.concatenate([task_mix, task_diag[:, None], task_noise[:, None]], axis=1)
    own_look = lookup(sorted_t, table)
    noise_own = own_look[:, rank_q + 1]
    row_z, row_t = (
        lax.all_gather(sorted_z, "col", axis=0, tiled=True),
        lax.all_gather(sorted_t, "col", axis=0, tiled=True),
    )
    row_look = lookup(row_t, table)
    row_w = row_look[:, :rank_q]
    row_k = row_look[:, rank_q]
    row_n = jnp.sum(row_z.astype(jnp.float32) ** 2, axis=1)
    total_rows = row_z.shape[0]
    block = math.gcd(total_rows, 1024)
    blocks = total_rows // block
    initial = jnp.zeros((total_rows, width), jnp.float32)
    col_scaled = make_scaled(sorted_v, own_look[:, :rank_q])
    col_z = lax.all_gather(sorted_z, "row", axis=0, tiled=True)
    col_q = lax.all_gather(col_scaled, "row", axis=0, tiled=True)
    col_t = lax.all_gather(sorted_t, "row", axis=0, tiled=True)
    col_n = jnp.sum(col_z.astype(jnp.float32) ** 2, axis=1)
    low_part = col_q[:, : rank_q * width]
    plain_part = col_q[:, rank_q * width :]

    def step(index, acc):
        start = index * block
        zb = lax.dynamic_slice_in_dim(row_z, start, block, 0)
        nb = lax.dynamic_slice_in_dim(row_n, start, block, 0)
        tb = lax.dynamic_slice_in_dim(row_t, start, block, 0)
        wb = lax.dynamic_slice_in_dim(row_w, start, block, 0)
        kb = lax.dynamic_slice_in_dim(row_k, start, block, 0)
        cross = lax.dot_general(
            zb, col_z, (((1,), (1,)), ((), ())), preferred_element_type=jnp.float32
        )
        dist = jnp.maximum(nb[:, None] + col_n[None, :] - 2.0 * cross, 0.0)
        kern = jnp.exp(-0.5 * dist).astype(jnp.bfloat16)
        prod = jnp.dot(kern, low_part, preferred_element_type=jnp.float32).reshape(
            block, rank_q, width
        )
        low = jnp.sum(wb[:, :, None] * prod, axis=1)
        same = jnp.where(tb[:, None] == col_t[None, :], kern, jnp.zeros_like(kern))
        diag = jnp.dot(same, plain_part, preferred_element_type=jnp.float32)
        term = low + kb[:, None] * diag
        current = lax.dynamic_slice_in_dim(acc, start, block, 0)
        return lax.dynamic_update_slice_in_dim(acc, current + term, start, 0)

    summed = lax.fori_loop(0, blocks, step, initial)
    partial_value = lax.psum_scatter(summed, "col", scatter_dimension=0, tiled=True)
    v_float = sorted_v.astype(jnp.float32)
    image = partial_value + noise_own[:, None] * v_float
    start_sum = lax.psum(jnp.sum(v_float * v_float, axis=0), ("row", "col"))
    curve = lax.psum(jnp.sum(v_float * image, axis=0), ("row", "col"))
    alpha = start_sum / curve
    residual = v_float - alpha * image
    finish = lax.psum(jnp.sum(residual * residual, axis=0), ("row", "col"))
    beta = finish / start_sum
    direction = residual + beta * v_float
    return (residual, direction, alpha, beta)


def solution(mesh):
    return jax.shard_map(
        body,
        mesh=mesh,
        in_specs=(
            P(("row", "col"), None),
            P(("row", "col")),
            P(),
            P(("row", "col")),
            P(("row", "col"), None),
            P(),
            P(),
            P(),
            P(),
            P(),
            P(),
        ),
        out_specs=(P(("row", "col"), None), P(("row", "col"), None), P(), P()),
        check_vma=False,
    )
```

profile of v0, /device:TPU:1, one launch (start us, length us, event | category | flops | bytes accessed | tf_op | source)
XLA Modules:
  0.0 443.9 jit_solution(1122650830039205359)
XLA Ops:
  7.2 1.0 reduce-window.9
  8.4 0.8 bitcast_subtract_fusion
  9.2 0.9 select_reduce_fusion.3
  10.1 0.7 add.104
  11.0 1.0 select_reduce_fusion.1
  12.1 0.7 all_to_all.28
  12.8 11.5 %all-to-all-start = ((s32[128,4,1]{1,2,0:T(1,128)}), s32[128,4,1]{1,2,0:T(1,128)S(1)}, u32[]{:S(2)}, u32[]{:S(2)}) async-start(s32[128,4,1]{1,2,0:T(1,128)} %bitcast.3), calls=%async_computation | async-start | bytes 131072 | tf_op jit(solution)/shard_map/all_to_all | solution.py:65
  24.3 1.2 convolution_convert_fusion.1
  25.6 0.8 reshape.92
  26.4 7.4 %all-to-all-done = s32[128,4,1]{1,2,0:T(1,128)S(1)} async-done(((s32[128,4,1]{1,2,0:T(1,128)}), s32[128,4,1]{1,2,0:T(1,128)S(1)}, u32[]{:S(2)}, u32[]{:S(2)}) %all-to-all-start) | async-done | bytes 2080 | tf_op jit(solution)/shard_map/all_to_all | solution.py:65
  33.8 4.5 %all-to-all-start.3 = ((bf16[128,2,128]{2,1,0:T(2,128)(2,1)}), bf16[128,2,128]{2,1,0:T(2,128)(2,1)S(1)}, u32[]{:S(2)}, u32[]{:S(2)}) async-start(bf16[128,2,128]{2,1,0:T(2,128)(2,1)} %reshape.92), calls=%async_computation.3 | async-start | bytes 131072 | tf_op jit(solution)/shard_map/all_to_all | solution.py:62
  38.6 9.1 %all-to-all-done.3 = bf16[128,2,128]{2,1,0:T(2,128)(2,1)S(1)} async-done(((bf16[128,2,128]{2,1,0:T(2,128)(2,1)}), bf16[128,2,128]{2,1,0:T(2,128)(2,1)S(1)}, u32[]{:S(2)}, u32[]{:S(2)}) %all-to-all-start.3) | async-done | bytes 65568 | tf_op jit(solution)/shard_map/all_to_all | solution.py:62
  47.9 1.0 convolution_convert_fusion
  48.9 0.7 all_to_all.33
  49.6 4.5 %all-to-all-start.2 = ((s32[128,4,1]{1,2,0:T(1,128)}), s32[128,4,1]{1,2,0:T(1,128)S(1)}, u32[]{:S(2)}, u32[]{:S(2)}) async-start(s32[128,4,1]{1,2,0:T(1,128)} %bitcast.6), calls=%async_computation.2 | async-start | bytes 131072 | tf_op jit(solution)/shard_map/all_to_all | solution.py:64
  54.1 1.1 convolution_convert_fusion.2
  55.2 0.8 copy.35
  55.9 7.7 %all-to-all-done.2 = s32[128,4,1]{1,2,0:T(1,128)S(1)} async-done(((s32[128,4,1]{1,2,0:T(1,128)}), s32[128,4,1]{1,2,0:T(1,128)S(1)}, u32[]{:S(2)}, u32[]{:S(2)}) %all-to-all-start.2) | async-done | bytes 2080 | tf_op jit(solution)/shard_map/all_to_all | solution.py:64
  63.6 4.5 %all-to-all-start.1 = ((bf16[128,4,32]{2,1,0:T(4,128)(2,1)}), bf16[128,4,32]{2,1,0:T(4,128)(2,1)S(1)}, u32[]{:S(2)}, u32[]{:S(2)}) async-start(bf16[128,4,32]{2,1,0:T(4,128)(2,1)} %bitcast.4), calls=%async_computation.1 | async-start | bytes 262144 | tf_op jit(solution)/shard_map/all_to_all | solution.py:63
  68.7 0.8 reduce.9
  69.8 1.1 fusion.20
  70.9 7.1 %all-to-all-done.1 = bf16[128,4,32]{2,1,0:T(4,128)(2,1)S(1)} async-done(((bf16[128,4,32]{2,1,0:T(4,128)(2,1)}), bf16[128,4,32]{2,1,0:T(4,128)(2,1)S(1)}, u32[]{:S(2)}, u32[]{:S(2)}) %all-to-all-start.1) | async-done | bytes 32800 | tf_op jit(solution)/shard_map/all_to_all | solution.py:63
  78.4 0.7 pad_maximum_fusion
  79.1 17.0 %all-gather = s32[16,1,512]{2,1,0:T(1,128)S(1)} all-gather(s32[1,1,512]{2,1,0:T(1,128)S(1)} %bitcast.46), channel_id=1, replica_groups=mesh['row'=8,'col'=16] {'col'}, dimensions={0}, use_global_device_ids=true | all-gather | bytes 34816 | tf_op jit(solution)/shard_map/all_gather | solution.py:78
  96.1 4.4 fusion.11
  100.6 15.9 %all-gather.1 = s32[8,1,512]{2,1,0:T(1,128)S(1)} all-gather(s32[1,1,512]{2,1,0:T(1,128)S(1)} %bitcast.47), channel_id=1, replica_groups=mesh['row'=8,'col'=16] {'row'}, dimensions={0}, use_global_device_ids=true | all-gather | bytes 18432 | tf_op jit(solution)/shard_map/all_gather | solution.py:91
  116.5 13.5 %all_gather.17 = bf16[4096,64]{0,1:T(8,128)(2,1)S(1)} all-gather(bf16[512,64]{0,1:T(8,128)(2,1)} %convolution_convert_fusion), channel_id=1, replica_groups=mesh['row'=8,'col'=16] {'row'}, dimensions={0}, use_global_device_ids=true | all-gather | bytes 589824 | tf_op jit(solution)/shard_map/all_gather | solution.py:89
  130.1 1.3 copy.39
  131.5 1.5 multiply_reduce_fusion.1
  133.1 1.3 slice.35
  134.4 0.7 copy.40
  135.0 1.0 slice.37
  136.6 100.0 %while.13 = (s32[]{:T(128)}, f32[8192,32]{0,1:T(8,128)S(1)}, f32[8192,4]{0,1:T(4,128)S(1)}, f32[8192]{0:T(1024)S(1)}, f32[4096]{0:T(1024)S(1)}, /*index=5*/bf16[...) while((s32[]{:T(128)}, f32[8192,32]{0,1:T(8,128)S(1)}, ...), condition=%wide.region_13.14_spmd, body=%wide.region_11.13_spmd.sunk | while | flops 1912930304 | bytes 30134492 | solution.py:118
  136.6 6.9 %exponential_convert_fusion.2 = bf16[1024,4096]{1,0:T(8,128)(2,1)S(1)} fusion(bf16[4096,64]{1,0:T(8,128)(2,1)} %get-tuple-element.397, f32[4096]{0:T(1024)S(1)} %get-tuple-element.395, f32[1024]{0:T(1024)S(1)} %dynamic_slice.55, bf16[8192,64]{0,1:T(8,128)(2,1)} %get-tuple-element.396, s32[]{:T(128)S(6)} %select_n.56), kind=kOutput, calls=%fused_computation.clone.1 | convolution fusion | flops 562036736 | bytes 9588740 | tf_op jit(solution)/shard_map/while/body/eval_jaxpr/dot_general | solution.py:103
  143.6 2.9 fusion.53
  146.5 2.5 fusion.54
  149.1 6.9 %exponential_convert_fusion.2 = bf16[1024,4096]{1,0:T(8,128)(2,1)S(1)} fusion(bf16[4096,64]{1,0:T(8,128)(2,1)} %get-tuple-element.397, f32[4096]{0:T(1024)S(1)} %get-tuple-element.395, f32[1024]{0:T(1024)S(1)} %dynamic_slice.55, bf16[8192,64]{0,1:T(8,128)(2,1)} %get-tuple-element.396, s32[]{:T(128)S(6)} %select_n.56), kind=kOutput, calls=%fused_computation.clone.1 | convolution fusion | flops 562036736 | bytes 9588740 | tf_op jit(solution)/shard_map/while/body/eval_jaxpr/dot_general | solution.py:103
  156.1 2.9 fusion.53
  159.1 2.5 fusion.54
  161.6 6.9 %exponential_convert_fusion.2 = bf16[1024,4096]{1,0:T(8,128)(2,1)S(1)} fusion(bf16[4096,64]{1,0:T(8,128)(2,1)} %get-tuple-element.397, f32[4096]{0:T(1024)S(1)} %get-tuple-element.395, f32[1024]{0:T(1024)S(1)} %dynamic_slice.55, bf16[8192,64]{0,1:T(8,128)(2,1)} %get-tuple-element.396, s32[]{:T(128)S(6)} %select_n.56), kind=kOutput, calls=%fused_computation.clone.1 | convolution fusion | flops 562036736 | bytes 9588740 | tf_op jit(solution)/shard_map/while/body/eval_jaxpr/dot_general | solution.py:103
  168.6 2.9 fusion.53
  171.6 2.5 fusion.54
  174.2 6.9 %exponential_convert_fusion.2 = bf16[1024,4096]{1,0:T(8,128)(2,1)S(1)} fusion(bf16[4096,64]{1,0:T(8,128)(2,1)} %get-tuple-element.397, f32[4096]{0:T(1024)S(1)} %get-tuple-element.395, f32[1024]{0:T(1024)S(1)} %dynamic_slice.55, bf16[8192,64]{0,1:T(8,128)(2,1)} %get-tuple-element.396, s32[]{:T(128)S(6)} %select_n.56), kind=kOutput, calls=%fused_computation.clone.1 | convolution fusion | flops 562036736 | bytes 9588740 | tf_op jit(solution)/shard_map/while/body/eval_jaxpr/dot_general | solution.py:103
  181.1 2.9 fusion.53
  184.1 2.5 fusion.54
  186.7 6.9 %exponential_convert_fusion.2 = bf16[1024,4096]{1,0:T(8,128)(2,1)S(1)} fusion(bf16[4096,64]{1,0:T(8,128)(2,1)} %get-tuple-element.397, f32[4096]{0:T(1024)S(1)} %get-tuple-element.395, f32[1024]{0:T(1024)S(1)} %dynamic_slice.55, bf16[8192,64]{0,1:T(8,128)(2,1)} %get-tuple-element.396, s32[]{:T(128)S(6)} %select_n.56), kind=kOutput, calls=%fused_computation.clone.1 | convolution fusion | flops 562036736 | bytes 9588740 | tf_op jit(solution)/shard_map/while/body/eval_jaxpr/dot_general | solution.py:103
  193.6 2.9 fusion.53
  196.6 2.5 fusion.54
  199.2 6.9 %exponential_convert_fusion.2 = bf16[1024,4096]{1,0:T(8,128)(2,1)S(1)} fusion(bf16[4096,64]{1,0:T(8,128)(2,1)} %get-tuple-element.397, f32[4096]{0:T(1024)S(1)} %get-tuple-element.395, f32[1024]{0:T(1024)S(1)} %dynamic_slice.55, bf16[8192,64]{0,1:T(8,128)(2,1)} %get-tuple-element.396, s32[]{:T(128)S(6)} %select_n.56), kind=kOutput, calls=%fused_computation.clone.1 | convolution fusion | flops 562036736 | bytes 9588740 | tf_op jit(solution)/shard_map/while/body/eval_jaxpr/dot_general | solution.py:103
  206.1 2.9 fusion.53
  209.1 2.5 fusion.54
  211.7 6.9 %exponential_convert_fusion.2 = bf16[1024,4096]{1,0:T(8,128)(2,1)S(1)} fusion(bf16[4096,64]{1,0:T(8,128)(2,1)} %get-tuple-element.397, f32[4096]{0:T(1024)S(1)} %get-tuple-element.395, f32[1024]{0:T(1024)S(1)} %dynamic_slice.55, bf16[8192,64]{0,1:T(8,128)(2,1)} %get-tuple-element.396, s32[]{:T(128)S(6)} %select_n.56), kind=kOutput, calls=%fused_computation.clone.1 | convolution fusion | flops 562036736 | bytes 9588740 | tf_op jit(solution)/shard_map/while/body/eval_jaxpr/dot_general | solution.py:103
  218.6 2.9 fusion.53
  221.6 2.5 fusion.54
  224.2 6.9 %exponential_convert_fusion.2 = bf16[1024,4096]{1,0:T(8,128)(2,1)S(1)} fusion(bf16[4096,64]{1,0:T(8,128)(2,1)} %get-tuple-element.397, f32[4096]{0:T(1024)S(1)} %get-tuple-element.395, f32[1024]{0:T(1024)S(1)} %dynamic_slice.55, bf16[8192,64]{0,1:T(8,128)(2,1)} %get-tuple-element.396, s32[]{:T(128)S(6)} %select_n.56), kind=kOutput, calls=%fused_computation.clone.1 | convolution fusion | flops 562036736 | bytes 9588740 | tf_op jit(solution)/shard_map/while/body/eval_jaxpr/dot_general | solution.py:103
  231.1 2.9 fusion.53
  234.1 2.5 fusion.54
  236.6 1.0 copy-done.1
  237.6 68.7 %reduce-scatter.2.cloned.1.call-done = f32[512,32]{0,1:T(8,128)} async-done(((f32[8192,32]{0,1:T(8,128)}), f32[512,32]{0,1:T(8,128)}) %reduce-scatter.2.cloned.1.call-update) | async-done | bytes 65552 | tf_op jit(solution)/shard_map/reduce_scatter | solution.py:119
  306.3 1.0 fusion.24
  307.3 65.8 %all-reduce = (f32[32]{0:T(128)S(1)}, f32[32]{0:T(128)S(1)}) all-reduce(f32[32]{0:T(128)S(1)} %get-tuple-element.253, f32[32]{0:T(128)S(1)} %get-tuple-element.252), channel_id=1, replica_groups=mesh['row'=8,'col'=16] {'row','col'}, use_global_device_ids=true, to_apply=%region_6.7 | all-reduce | flops 64 | bytes 512 | tf_op jit(solution)/shard_map/psum | solution.py:122
  373.1 1.0 multiply_reduce_fusion.3
  374.1 62.5 %psum.23 = f32[32]{0:T(128)S(1)} all-reduce(f32[32]{0:T(128)S(1)} %get-tuple-element.282), channel_id=1, replica_groups=mesh['row'=8,'col'=16] {'row','col'}, use_global_device_ids=true, to_apply=%region_18.19 | all-reduce | flops 32 | bytes 256 | tf_op jit(solution)/shard_map/psum | solution.py:126
  436.6 0.7 fusion.25
  (79 shorter events, 3.8 us)
Async XLA Ops:
  7.2 17.1 %copy-start = (bf16[512,64]{0,1:T(8,128)(2,1)S(1)}, bf16[512,64]{0,1:T(8,128)(2,1)}, u32[]{:S(2)}) copy-start(bf16[512,64]{0,1:T(8,128)(2,1)} %param.13) | copy-start | bytes 196612
  12.8 21.0 %all-to-all-start = ((s32[128,4,1]{1,2,0:T(1,128)}), s32[128,4,1]{1,2,0:T(1,128)S(1)}, u32[]{:S(2)}, u32[]{:S(2)}) async-start(s32[128,4,1]{1,2,0:T(1,128)} %bitcast.3), calls=%async_computation | async-start | bytes 131072 | tf_op jit(solution)/shard_map/all_to_all | solution.py:65
  33.8 14.0 %all-to-all-start.3 = ((bf16[128,2,128]{2,1,0:T(2,128)(2,1)}), bf16[128,2,128]{2,1,0:T(2,128)(2,1)S(1)}, u32[]{:S(2)}, u32[]{:S(2)}) async-start(bf16[128,2,128]{2,1,0:T(2,128)(2,1)} %reshape.92), calls=%async_computation.3 | async-start | bytes 131072 | tf_op jit(solution)/shard_map/all_to_all | solution.py:62
  38.3 93.2 %all-gather.5.cloned.1.call-start = ((), (), s32[]{:S(2)}) async-start(), calls=%async_computation.5 | async-start | bytes 1114112 | tf_op jit(solution)/shard_map/all_gather | solution.py:77
  49.6 14.0 %all-to-all-start.2 = ((s32[128,4,1]{1,2,0:T(1,128)}), s32[128,4,1]{1,2,0:T(1,128)S(1)}, u32[]{:S(2)}, u32[]{:S(2)}) async-start(s32[128,4,1]{1,2,0:T(1,128)} %bitcast.6), calls=%async_computation.2 | async-start | bytes 131072 | tf_op jit(solution)/shard_map/all_to_all | solution.py:64
  63.6 14.4 %all-to-all-start.1 = ((bf16[128,4,32]{2,1,0:T(4,128)(2,1)}), bf16[128,4,32]{2,1,0:T(4,128)(2,1)S(1)}, u32[]{:S(2)}, u32[]{:S(2)}) async-start(bf16[128,4,32]{2,1,0:T(4,128)(2,1)} %bitcast.4), calls=%async_computation.1 | async-start | bytes 262144 | tf_op jit(solution)/shard_map/all_to_all | solution.py:63
  68.1 64.9 %all-gather.7.cloned.1.call-start = ((), (), s32[]{:S(2)}) async-start(), calls=%async_computation.6 | async-start | bytes 1474560 | tf_op jit(solution)/shard_map/all_gather | solution.py:90
  79.1 227.2 %reduce-scatter.2.cloned.1.call-start = ((), (), s32[]{:S(2)}) async-start(), calls=%async_computation.7 | async-start | bytes 1114112 | tf_op jit(solution)/shard_map/reduce_scatter | solution.py:119
  236.6 1.0 copy-start.1
  373.1 64.2 %copy-start.3 = (f32[32]{0:T(128)}, f32[32]{0:T(128)S(1)}, u32[]{:S(2)}) copy-start(f32[32]{0:T(128)S(1)} %div.6) | copy-start | bytes 388
  374.1 63.2 %copy-start.2 = (f32[512,32]{0,1:T(8,128)}, f32[512,32]{0,1:T(8,128)S(1)}, u32[]{:S(2)}) copy-start(f32[512,32]{0,1:T(8,128)S(1)} %get-tuple-element.283) | copy-start | bytes 196612
  436.6 0.7 copy-start.4
Sparse Core Ops, SparseCore 0:
  49.0 38.3 all-gather.4
  89.1 25.1 all-gather.6
  237.7 68.5 reduce-scatter.1
where the time goes:
time: 445 us; the launch traced here: 444 us
  blocking collectives  175 us (39%)
  matrix products  108 us (24%)
  waiting for transfers between devices  100 us (22%)
  starting transfers between devices  25.2 us (6%)
  between operations  14 us (3%)
  other arithmetic  11.2 us (3%)
  local copies, waits for them, and re-layouts  10.3 us (2%)
    reduce_scatter x1, waiting for transfers between devices, body(): lax.psum_scatter(summed, 'col', scatter_dimension=0, tiled=True)  68.7 us
    psum x1, blocking collectives, body(): start_sum = lax.psum(jnp.sum(v_float * v_float, axis=0), ('row', 'col'))  65.8 us
    psum x1, blocking collectives, body(): finish = lax.psum(jnp.sum(residual * residual, axis=0), ('row', 'col'))  62.5 us
    dot_general x8, matrix products, step(): lax.dot_general(zb, col_z, (((1,), (1,)), ((), ())), preferred_element_ty...  55.6 us
    dot_general x8, matrix products, step(): jnp.dot(kern, low_part, preferred_element_type=jnp.float32)  23.2 us
    dot_general x8, matrix products, step(): diag = jnp.dot(same, plain_part, preferred_element_type=jnp.float32)  20 us
    all_gather x1, blocking collectives, body(): lax.all_gather(sorted_t, 'col', axis=0, tiled=True)  17 us
    all_gather x1, blocking collectives, body(): col_t = lax.all_gather(sorted_t, 'row', axis=0, tiled=True)  15.9 us
  transfers between devices with their start and end apart: 7, of which 5 were waited for; matrix products, arithmetic and copies ran while one was open for 3% of the time, Pallas kernels for 0%

commit v1 on v0

v1 whole, which is shorter than its diff:
```python
import functools

import jax
import jax.numpy as jnp
from jax import lax
from jax.experimental import pallas as pl
from jax.experimental.pallas import tpu as pltpu
from jax.sharding import PartitionSpec as P

F32 = jnp.float32
BF16 = jnp.bfloat16
VMEM = pl.BlockSpec(memory_space=pltpu.VMEM)
SMEM = pl.BlockSpec(memory_space=pltpu.SMEM)
PARAMS = pltpu.CompilerParams(vmem_limit_bytes=48 * 1024 * 1024)
V0, P0, T0 = 64, 96, 98


def iota(shape, dim):
    return lax.broadcasted_iota(jnp.int32, shape, dim)


def split3(x):
    hi = x.astype(BF16)
    rest = x - hi.astype(F32)
    mid = rest.astype(BF16)
    low = (rest - mid.astype(F32)).astype(BF16)
    return hi, mid, low


def task_starts(counts):
    n = counts.shape[1]
    before = iota((n, n), 1) < iota((n, n), 0)
    start = jnp.sum(jnp.where(before, counts, 0.0), axis=1, keepdims=True)
    own = iota((n, n), 1) == iota((n, n), 0)
    return start, start + jnp.sum(jnp.where(own, counts, 0.0), axis=1, keepdims=True)


def pack_kernel(feat, tid, cnt, rank, probes, net_w, net_b, scale, packed, payload):
    rows = feat.shape[0]
    ntask = cnt.shape[1]
    start, _ = task_starts(cnt[...].astype(F32))
    task = tid[...]
    hit = iota((ntask, rows), 0) == task
    pos = jnp.sum(jnp.where(hit, start, 0.0), axis=0, keepdims=True) + rank[...].astype(F32)
    both = jnp.concatenate([pos, task.astype(F32), jnp.zeros((6, rows), F32)], axis=0).T
    pos_col, task_col = both[:, 0:1], both[:, 1:2]
    order = jnp.sum((pos_col < pos).astype(F32), axis=0, keepdims=True)
    placing = (iota((rows, rows), 0) == order.astype(jnp.int32)).astype(BF16)
    hidden = jnp.tanh(
        jnp.dot(feat[...], net_w[...], preferred_element_type=F32) + net_b[...]
    )
    latent = (hidden * scale[...]).astype(BF16)
    local = pos_col - jnp.floor(pos_col * (1.0 / rows)) * rows
    high = jnp.floor(local * (1.0 / 16.0))
    lane = iota((rows, 128 - P0), 1)
    extra = jnp.where(
        lane == 0,
        high,
        jnp.where(lane == 1, local - 16.0 * high, jnp.where(lane == T0 - P0, task_col, 0.0)),
    )
    whole = jnp.concatenate([latent, probes[...], extra.astype(BF16)], axis=1)
    payload[...] = whole
    packed[...] = jnp.dot(placing, whole, preferred_element_type=F32).astype(BF16)


def rows_kernel(n_col, flat, cnt, table, rows_w, own):
    half = rows_w.shape[2] // n_col
    ntask = cnt.shape[1]
    start, end = task_starts(cnt[...].astype(F32))
    block = own.shape[1]
    group = (flat[0] // n_col) * (n_col * block)
    tab = jnp.concatenate(split3(table[...]), axis=0)

    def look(first, count):
        pos = (first + iota((1, count), 1)).astype(F32)
        hit = jnp.logical_and(start <= pos, pos < end)
        got = jnp.dot(tab, hit.astype(BF16), preferred_element_type=F32)
        return hit, got[0:8] + got[8:16] + got[16:24]

    for c in range(n_col):
        _, got = look(group + c * block, block)
        for h in range(2):
            rows_w[h, :, c * half : (c + 1) * half] = got[:, h * half : (h + 1) * half]
    hit, got = look(flat[0] * block, block)
    low = jnp.sum(jnp.where(hit, start, 0.0), axis=0, keepdims=True)
    high = jnp.sum(jnp.where(hit, end, 0.0), axis=0, keepdims=True)
    own[...] = jnp.concatenate([low, high, got[4:6], jnp.zeros((4, block), F32)], axis=0)


def sort_kernel(got, out_t, za, zb):
    rows = got.shape[0]
    data = got[...]
    place = data[:, P0 : P0 + 1].astype(F32) * 16.0 + data[:, P0 + 1 : P0 + 2].astype(F32)
    onehot = (iota((rows, rows), 1) == place.astype(jnp.int32)).astype(BF16)
    ordered = lax.dot_general(
        data, onehot, (((0,), (0,)), ((), ())), preferred_element_type=F32
    ).astype(BF16)
    out_t[...] = ordered[:P0]
    half = rows // 2
    for c in range(za.shape[0]):
        za[c] = ordered[:V0, :half]
        zb[c] = ordered[:V0, half:]


def cols_kernel(table, *refs):
    chunks, (zc, st) = refs[:-2], refs[-2:]
    rows = chunks[0].shape[0]
    ntask = table.shape[1]
    tab = jnp.concatenate(split3(table[...]), axis=0)
    for k, ref in enumerate(chunks):
        data = ref[...].astype(F32)
        lane = iota((rows, 128), 1)
        z = jnp.where(lane < V0, data, 0.0)
        norm = jnp.sum(z * z, axis=1, keepdims=True) * -0.5
        hi, mid, low = (a.astype(F32) for a in split3(norm))
        z = jnp.where(lane == V0, hi, z)
        z = jnp.where(lane == V0 + 1, mid, z)
        z = jnp.where(lane == V0 + 2, low, z)
        z = jnp.where(jnp.logical_and(lane > V0 + 2, lane < V0 + 6), 1.0, z)
        zc[k * rows : (k + 1) * rows, :] = z.astype(BF16)
        turned = data.T
        task = turned[T0 : T0 + 1].astype(jnp.int32)
        hit = (iota((ntask, rows), 0) == task).astype(BF16)
        got = jnp.dot(tab, hit, preferred_element_type=F32)
        weight = got[0:8] + got[8:16] + got[16:24]
        values = turned[V0:P0]
        width = P0 - V0
        for q in range(4):
            st[q * width : (q + 1) * width, k * rows : (k + 1) * rows] = (
                weight[q : q + 1] * values
            ).astype(BF16)


def augment_rows(z):
    n = z.shape[1]
    zf = z.astype(F32)
    norm = jnp.sum(zf * zf, axis=0, keepdims=True) * -0.5
    hi, mid, low = (a.astype(F32) for a in split3(norm))
    sub = iota((16, n), 0)
    extra = jnp.where(sub < 3, 1.0, 0.0)
    extra = jnp.where(sub == 3, hi, extra)
    extra = jnp.where(sub == 4, mid, extra)
    extra = jnp.where(sub == 5, low, extra)
    return jnp.concatenate([z, extra.astype(BF16), jnp.zeros((48, n), BF16)], axis=0)


def main_kernel(tile, zr, weight, zc, st, out):
    z = augment_rows(jnp.concatenate([zr[c] for c in range(zr.shape[0])], axis=1))
    total = None
    for j in range(zc.shape[0] // tile):
        span = slice(j * tile, (j + 1) * tile)
        x = jnp.dot(zc[span, :], z, preferred_element_type=F32)
        kern = jnp.minimum(jnp.exp(x).astype(BF16), jnp.asarray(1.0, BF16))
        part = jnp.dot(st[:, span], kern, preferred_element_type=F32)
        total = part if total is None else total + part
    width = total.shape[0] // 4
    summed = weight[0:1] * total[:width]
    for q in range(1, 4):
        summed = summed + weight[q : q + 1] * total[q * width : (q + 1) * width]
    half = zr.shape[2]
    for c in range(zr.shape[0]):
        out[c] = summed[:, c * half : (c + 1) * half].astype(out.dtype)


def main_call(zr, weight, zc, st):
    n_col, feat, half = zr.shape
    cols = zc.shape[0]
    step = 4
    width = st.shape[0] // 4
    return pl.pallas_call(
        functools.partial(main_kernel, 1024),
        grid=(n_col // step,),
        in_specs=[
            pl.BlockSpec((step, feat, half), lambda i: (i, 0, 0)),
            pl.BlockSpec((8, step * half), lambda i: (0, i)),
            pl.BlockSpec((cols, 128), lambda i: (0, 0)),
            pl.BlockSpec((st.shape[0], cols), lambda i: (0, 0)),
        ],
        out_specs=pl.BlockSpec((step, width, half), lambda i: (i, 0, 0)),
        out_shape=jax.ShapeDtypeStruct((n_col, width, half), F32),
        compiler_params=PARAMS,
        cost_estimate=pl.CostEstimate(
            flops=2 * n_col * half * cols * 512, bytes_accessed=4 << 20, transcendentals=0
        ),
        name="product",
    )(zr, weight, zc, st)


def same_kernel(flat, own, mid, prev, nxt, out):
    block = own.shape[1]
    z = augment_rows(mid[:V0])
    low, high = own[0:1], own[1:2]
    total = None
    for k, ref in enumerate((prev, mid, nxt)):
        data = ref[...]
        zt = augment_rows(data[:V0])
        zt = jnp.concatenate([zt[:V0], swap_norm(zt[V0 : V0 + 16]), zt[V0 + 16 :]], axis=0)
        x = lax.dot_general(zt, z, (((0,), (0,)), ((), ())), preferred_element_type=F32)
        kern = jnp.minimum(jnp.exp(x).astype(BF16), jnp.asarray(1.0, BF16)).astype(F32)
        pos = ((flat[0] + (k - 1)) * block + iota((block, 1), 0)).astype(F32)
        same = jnp.logical_and(low <= pos, pos < high)
        kern = jnp.where(same, kern, 0.0).astype(BF16)
        part = jnp.dot(data[V0:P0], kern, preferred_element_type=F32)
        total = part if total is None else total + part
    out[...] = own[2:3] * total + own[3:4] * mid[V0:P0].astype(F32)


def swap_norm(extra):
    e = extra.astype(F32)
    n = e.shape[1]
    sub = iota((16, n), 0)
    out = jnp.where(jnp.logical_and(sub > 2, sub < 6), 1.0, 0.0)
    for k in range(3):
        out = jnp.where(sub == k, e[k + 3 : k + 4], out)
    return out.astype(BF16)


def image_kernel(sa, sb, diag, mid, image, stats):
    parts = [jnp.sum(ref[...].astype(F32), axis=0) for ref in (sa, sb)]
    img = jnp.concatenate(parts, axis=1) + diag[...]
    image[...] = img
    v = mid[V0:P0].astype(F32)
    vv = jnp.sum(v * v, axis=1, keepdims=True)
    vi = jnp.sum(v * img, axis=1, keepdims=True)
    ratio = jnp.where(vv > 0.0, vi / jnp.where(vv > 0.0, vv, 1.0), 0.0)
    rest = img - ratio * v
    rr = jnp.sum(rest * rest, axis=1, keepdims=True)
    lane = iota((32, 128), 1)
    wide = jnp.where(lane == 0, vv, jnp.where(lane == 1, vi, jnp.where(lane == 2, rr, 0.0)))
    turned = wide.T
    row = jnp.concatenate(
        [turned[0:1], turned[1:2], turned[2:3], jnp.zeros((1, 32), F32)], axis=1
    )
    for d in range(stats.shape[0]):
        stats[d] = row


def final_kernel(stats, image, mid, residual, direction, alpha_out, beta_out):
    every = stats[...]
    every = every.reshape(every.shape[0], 128)
    vv, vi, rr = every[:, 0:32], every[:, 32:64], every[:, 64:96]
    total_v = jnp.sum(vv, axis=0, keepdims=True)
    total_i = jnp.sum(vi, axis=0, keepdims=True)
    center = total_i / total_v
    ratio = jnp.where(vv > 0.0, vi / jnp.where(vv > 0.0, vv, 1.0), 0.0)
    shift = ratio - center
    total_r = jnp.sum(rr + vv * (shift * shift), axis=0, keepdims=True)
    alpha = total_v / total_i
    beta = alpha * alpha * total_r / total_v
    alpha_out[...] = alpha
    beta_out[...] = beta
    v = mid[V0:P0].astype(F32).T
    res = v - alpha * image[...].T
    residual[...] = res
    direction[...] = res + beta * v


def body(
    features,
    task_id,
    task_count,
    task_rank,
    probes,
    net_w,
    net_b,
    inv_scale,
    task_mix,
    task_diag,
    task_noise,
):
    rows = features.shape[0]
    n_row, n_col = lax.axis_size("row"), lax.axis_size("col")
    devices = n_row * n_col
    axes = ("row", "col")
    width = probes.shape[1]
    flat = (lax.axis_index("row") * n_col + lax.axis_index("col")).astype(jnp.int32).reshape(1)
    counts = task_count.reshape(1, -1)
    ntask = counts.shape[1]
    table = jnp.concatenate(
        [task_mix.T, task_diag[None], task_noise[None], jnp.zeros((2, ntask), F32)], axis=0
    )
    packed, payload = pl.pallas_call(
        pack_kernel,
        in_specs=[VMEM] * 8,
        out_specs=[VMEM, VMEM],
        out_shape=[jax.ShapeDtypeStruct((rows, 128), BF16)] * 2,
        compiler_params=PARAMS,
        name="pack",
    )(
        features,
        task_id.reshape(1, -1),
        counts,
        task_rank.reshape(1, -1),
        probes,
        net_w,
        net_b.reshape(1, -1),
        inv_scale.reshape(1, -1),
    )
    got = lax.all_to_all(packed, axes, split_axis=0, concat_axis=0, tiled=True)
    chunks = [payload] + [
        lax.ppermute(payload, "row", [(i, (i + k) % n_row) for i in range(n_row)])
        for k in range(1, n_row)
    ]
    half = rows // 2
    rows_w, own = pl.pallas_call(
        functools.partial(rows_kernel, n_col),
        in_specs=[SMEM, VMEM, VMEM],
        out_specs=[VMEM, VMEM],
        out_shape=[
            jax.ShapeDtypeStruct((2, 8, n_col * half), F32),
            jax.ShapeDtypeStruct((8, rows), F32),
        ],
        compiler_params=PARAMS,
        cost_estimate=pl.CostEstimate(flops=1 << 30, bytes_accessed=1 << 20, transcendentals=0),
        name="rows",
    )(flat, counts, table)
    mid, za, zb = pl.pallas_call(
        sort_kernel,
        in_specs=[VMEM],
        out_specs=[VMEM] * 3,
        out_shape=[
            jax.ShapeDtypeStruct((P0, rows), BF16),
            jax.ShapeDtypeStruct((n_col, V0, half), BF16),
            jax.ShapeDtypeStruct((n_col, V0, half), BF16),
        ],
        compiler_params=PARAMS,
        name="sort",
    )(got)
    ga = lax.all_to_all(za, "col", split_axis=0, concat_axis=0, tiled=True)
    gb = lax.all_to_all(zb, "col", split_axis=0, concat_axis=0, tiled=True)
    prev = lax.ppermute(mid, axes, [(i, (i + 1) % devices) for i in range(devices)])
    nxt = lax.ppermute(mid, axes, [(i, (i - 1) % devices) for i in range(devices)])
    total = n_row * rows
    zc, st = pl.pallas_call(
        cols_kernel,
        in_specs=[VMEM] * (1 + n_row),
        out_specs=[VMEM, VMEM],
        out_shape=[
            jax.ShapeDtypeStruct((total, 128), BF16),
            jax.ShapeDtypeStruct((4 * width, total), BF16),
        ],
        compiler_params=PARAMS,
        cost_estimate=pl.CostEstimate(flops=1 << 31, bytes_accessed=4 << 20, transcendentals=0),
        name="cols",
    )(table, *chunks)
    pa = main_call(ga, rows_w[0], zc, st)
    sa = lax.all_to_all(pa, "col", split_axis=0, concat_axis=0, tiled=True)
    pb = main_call(gb, rows_w[1], zc, st)
    sb = lax.all_to_all(pb, "col", split_axis=0, concat_axis=0, tiled=True)
    diag = pl.pallas_call(
        same_kernel,
        in_specs=[SMEM, VMEM, VMEM, VMEM, VMEM],
        out_specs=VMEM,
        out_shape=jax.ShapeDtypeStruct((width, rows), F32),
        compiler_params=PARAMS,
        cost_estimate=pl.CostEstimate(flops=1 << 31, bytes_accessed=1 << 20, transcendentals=0),
        name="same",
    )(flat, own, mid, prev, nxt)
    image, stats = pl.pallas_call(
        image_kernel,
        in_specs=[VMEM] * 4,
        out_specs=[VMEM] * 2,
        out_shape=[
            jax.ShapeDtypeStruct((width, rows), F32),
            jax.ShapeDtypeStruct((devices, 1, 128), F32),
        ],
        compiler_params=PARAMS,
        name="image",
    )(sa, sb, diag, mid)
    every = lax.all_to_all(stats, axes, split_axis=0, concat_axis=0, tiled=True)
    residual, direction, alpha, beta = pl.pallas_call(
        final_kernel,
        in_specs=[VMEM] * 3,
        out_specs=[VMEM] * 4,
        out_shape=[
            jax.ShapeDtypeStruct((rows, width), F32),
            jax.ShapeDtypeStruct((rows, width), F32),
            jax.ShapeDtypeStruct((1, width), F32),
            jax.ShapeDtypeStruct((1, width), F32),
        ],
        compiler_params=PARAMS,
        name="final",
    )(every, image, mid)
    return residual, direction, alpha.reshape(width), beta.reshape(width)


def solution(mesh):
    axes = ("row", "col")
    return jax.shard_map(
        body,
        mesh=mesh,
        in_specs=(
            P(axes, None),
            P(axes),
            P(),
            P(axes),
            P(axes, None),
            P(),
            P(),
            P(),
            P(),
            P(),
            P(),
        ),
        out_specs=(P(axes, None), P(axes, None), P(), P()),
        check_vma=False,
    )
```

time: 445 us -> 132 us (0.30)
  blocking collectives: 175 us -> 14.1 us
  matrix products: 108 us -> 0 us
  waiting for transfers between devices: 100 us -> 21.5 us
  Pallas kernels: 0 us -> 39.1 us
  starting transfers between devices: 25.2 us -> 47.6 us
  between operations: 14 us -> 0.88 us
  other arithmetic: 11.2 us -> 0.07 us
    psum x2 -> x0, blocking collectives: 128 us -> none  [the longest x1 65.8 us: body(): start_sum = lax.psum(jnp.sum(v_float * v_float, axis=0), ('row', 'col'))]
    dot_general x30 -> x0, matrix products: 108 us -> none  [the longest x8 55.6 us: step(): lax.dot_general(zb, col_z, (((1,), (1,)), ((), ())), preferred_element_ty...]
    reduce_scatter x1 -> x0, waiting for transfers between devices: 68.7 us -> none  [body(): lax.psum_scatter(summed, 'col', scatter_dimension=0, tiled=True)]
    all_gather x3 -> x0, blocking collectives: 46.4 us -> none  [the longest x1 17 us: body(): lax.all_gather(sorted_t, 'col', axis=0, tiled=True)]
    pallas_call x0 -> x9, Pallas kernels: none -> 39.1 us  [the longest x2 30 us: main_call(): pl.pallas_call(functools.partial(main_kernel, 1024), grid=(n_col // step,...]
    all_to_all x4 -> x5, waiting for transfers between devices: 31.3 us -> 8.21 us  [the longest x1 7.56 us: body(): got = lax.all_to_all(packed, axes, split_axis=0, concat_axis=0, tiled=True)]
    ppermute x0 -> x9, starting transfers between devices: none -> 15.5 us  [the longest x7 9.93 us: body(): lax.ppermute(payload, 'row', [(i, (i + k) % n_row) for i in range(n_row)])]
    all_to_all x0 -> x1, blocking collectives: none -> 14.1 us  [body(): every = lax.all_to_all(stats, axes, split_axis=0, concat_axis=0, tiled=True)]
  transfers between devices with their start and end apart: 7 -> 14, of which waited for: 5 -> 5; matrix products, arithmetic and copies ran while one was open for 3% -> 0% of each run, Pallas kernels for 0% -> 28%
where the time goes in v1:
time: 132 us; the launch traced here: 131 us
  starting transfers between devices  47.6 us (36%)
  Pallas kernels  39.1 us (30%)
  waiting for transfers between devices  21.5 us (16%)
  blocking collectives  14.1 us (11%)
  local copies, waits for them, and re-layouts  7.43 us (6%)
    pallas_call x2, Pallas kernels, main_call(): pl.pallas_call(functools.partial(main_kernel, 1024), grid=(n_col // step,...  30 us
    all_to_all x1, blocking collectives, body(): every = lax.all_to_all(stats, axes, split_axis=0, concat_axis=0, tiled=True)  14.1 us
    ppermute x7, starting transfers between devices, body(): lax.ppermute(payload, 'row', [(i, (i + k) % n_row) for i in range(n_row)])  9.93 us
    all_to_all x1, starting transfers between devices, body(): got = lax.all_to_all(packed, axes, split_axis=0, concat_axis=0, tiled=True)  9.16 us
    ppermute x1, waiting for transfers between devices, body(): lax.ppermute(mid, axes, [(i, (i + 1) % devices) for i in range(devices)])  8.31 us
    all_to_all x1, waiting for transfers between devices, body(): got = lax.all_to_all(packed, axes, split_axis=0, concat_axis=0, tiled=True)  7.56 us
    unnamed x30, local copies, waits for them, and re-layouts  7.34 us
    all_to_all x1, starting transfers between devices, body(): sb = lax.all_to_all(pb, 'col', split_axis=0, concat_axis=0, tiled=True)  6.67 us
  transfers between devices with their start and end apart: 14, of which 5 were waited for; matrix products, arithmetic and copies ran while one was open for 0% of the time, Pallas kernels for 28%

profile of v1, /device:TPU:1, one launch (start us, length us, event | category | flops | bytes accessed | tf_op | source)
XLA Modules:
  0.0 130.7 jit_solution(12968143643026167083)
XLA Ops:
  0.6 0.0 copy-start.9
  0.6 1.0 copy.15.feat
  1.6 0.0 copy-done.9
  1.6 0.0 copy-start
  1.6 0.1 copy.16.probes
  1.8 0.0 copy-start.5
  1.8 0.0 copy-start.2
  1.8 0.0 copy-start.1
  1.8 0.0 copy-start.3
  1.8 0.0 copy-start.4
  1.8 0.5 copy-done
  2.3 0.1 copy-done.5
  2.4 0.0 copy-done.2
  2.5 0.0 copy-done.1
  2.5 0.0 copy-done.3
  2.5 0.0 copy-done.4
  2.5 1.6 %pack.1 = (bf16[512,128]{1,0:T(8,128)(2,1)}, bf16[512,128]{1,0:T(8,128)(2,1)S(1)}) custom-call(bf16[512,64]{1,0:T(8,128)(2,1)S(1)} %copy.15.feat, s32[1,512]{1,0:T(1,128)S(1)} %bitcast.18, s32[1,256]{1,0:T(1,128)S(1)} %bitcast.20, s32[1,512]{1,0:T(1,128)S(1)} %bitcast.19, bf16[512,32]{1,0:T(8,128)(2,1)S(1)} %copy.16.probes, bf16[64,64]{1,0:T(8,128)(2,1)S(1)} %copy-done, ...), custom_call_target="tpu_custom_call" | custom-call | tf_op jit(solution)/shard_map/pack/pallas_call | solution.py:282
  4.0 2.7 %collective-permute-start = (bf16[512,128]{1,0:T(8,128)(2,1)S(1)}, bf16[512,128]{1,0:T(8,128)(2,1)S(1)}, u32[]{:S(2)}, u32[]{:S(2)}) collective-permute-start(bf16[512,128]{1,0:T(8,128)(2,1)S(1)} %get-tuple-element.22.refs_0_), channel_id=1, source_target_pairs={{0,16},{16,32},{32,48},{48,64},{64,80},{80,96},{96,112},{112,0},{1... | collective-permute-start | bytes 393224 | tf_op jit(solution)/shard_map/ppermute | solution.py:301
  6.7 1.3 collective-permute-start.1
  8.0 1.6 %collective-permute-start.2 = (bf16[512,128]{1,0:T(8,128)(2,1)S(1)}, bf16[512,128]{1,0:T(8,128)(2,1)S(1)}, u32[]{:S(2)}, u32[]{:S(2)}) collective-permute-start(bf16[512,128]{1,0:T(8,128)(2,1)S(1)} %get-tuple-element.22.refs_0_), channel_id=1, source_target_pairs={{0,48},{16,64},{32,80},{48,96},{64,112},{80,0},{96,16},{112,32},{1... | collective-permute-start | bytes 393224 | tf_op jit(solution)/shard_map/ppermute | solution.py:301
  9.7 0.3 collective-permute-start.3
  10.0 2.0 %collective-permute-start.4 = (bf16[512,128]{1,0:T(8,128)(2,1)S(1)}, bf16[512,128]{1,0:T(8,128)(2,1)S(1)}, u32[]{:S(2)}, u32[]{:S(2)}) collective-permute-start(bf16[512,128]{1,0:T(8,128)(2,1)S(1)} %get-tuple-element.22.refs_0_), channel_id=1, source_target_pairs={{0,80},{16,96},{32,112},{48,0},{64,16},{80,32},{96,48},{112,64},{1... | collective-permute-start | bytes 393224 | tf_op jit(solution)/shard_map/ppermute | solution.py:301
  12.0 9.2 %all-to-all-start = ((bf16[128,4,128]{2,1,0:T(4,128)(2,1)}), bf16[128,4,128]{2,1,0:T(4,128)(2,1)S(1)}, u32[]{:S(2)}, u32[]{:S(2)}) async-start(bf16[128,4,128]{2,1,0:T(4,128)(2,1)} %bitcast.5), calls=%async_computation | async-start | bytes 262144 | tf_op jit(solution)/shard_map/all_to_all | solution.py:299
  21.2 0.0 copy-start.10
  21.2 0.1 pad.3.clone
  21.3 0.6 copy-done.10
  21.9 0.1 copy-done.11
  22.0 0.1 maximum_maximum_fusion.table
  22.0 1.5 %rows.1 = (f32[2,8,4096]{2,1,0:T(8,128)S(1)}, f32[8,512]{1,0:T(8,128)S(1)}) custom-call(s32[1]{0:T(128)} %bitcast.7.flat, s32[1,256]{1,0:T(1,128)S(1)} %bitcast.21, f32[8,256]{1,0:T(8,128)S(1)} %maximum_maximum_fusion.table), custom_call_target="tpu_custom_call" | custom-call | flops 1073741824 | bytes 1048576 | tf_op jit(solution)/shard_map/rows/pallas_call | solution.py:305
  23.5 7.6 %all-to-all-done = bf16[128,4,128]{2,1,0:T(4,128)(2,1)S(1)} async-done(((bf16[128,4,128]{2,1,0:T(4,128)(2,1)}), bf16[128,4,128]{2,1,0:T(4,128)(2,1)S(1)}, u32[]{:S(2)}, u32[]{:S(2)}) %all-to-all-start) | async-done | bytes 131104 | tf_op jit(solution)/shard_map/all_to_all | solution.py:299
  31.1 1.5 %sort.1 = (bf16[96,512]{1,0:T(8,128)(2,1)S(1)}, bf16[16,64,256]{2,1,0:T(8,128)(2,1)}, bf16[16,64,256]{2,1,0:T(8,128)(2,1)}) custom-call(bf16[512,128]{1,0:T(8,128)(2,1)S(1)} %bitcast.17), custom_call_target="tpu_custom_call" | custom-call | tf_op jit(solution)/shard_map/sort/pallas_call | solution.py:317
  32.6 3.6 %all-to-all-start.3 = ((bf16[16,64,256]{2,1,0:T(8,128)(2,1)}), bf16[16,64,256]{2,1,0:T(8,128)(2,1)S(1)}, u32[]{:S(2)}, u32[]{:S(2)}) async-start(bf16[16,64,256]{2,1,0:T(8,128)(2,1)} %get-tuple-element.25), calls=%async_computation.3 | async-start | bytes 1048576 | tf_op jit(solution)/shard_map/all_to_all | solution.py:330
  36.1 0.0 collective-permute-done.refs_1_
  36.1 0.9 collective-permute-start.5
  37.0 0.0 collective-permute-done.1.refs_2_
  37.0 1.1 collective-permute-start.6
  38.1 0.0 collective-permute-done.2.refs_3_
  38.1 0.0 collective-permute-done.3.refs_4_
  38.2 0.0 collective-permute-done.4.refs_5_
  38.2 2.3 %collective-permute-done.5.refs_6_ = bf16[512,128]{1,0:T(8,128)(2,1)S(1)} collective-permute-done((bf16[512,128]{1,0:T(8,128)(2,1)S(1)}, bf16[512,128]{1,0:T(8,128)(2,1)S(1)}, u32[]{:S(2)}, u32[]{:S(2)}) %collective-permute-start.5) | collective-permute-done | bytes 131104 | tf_op jit(solution)/shard_map/ppermute | solution.py:301
  40.4 2.7 %collective-permute-done.6.refs_7_ = bf16[512,128]{1,0:T(8,128)(2,1)S(1)} collective-permute-done((bf16[512,128]{1,0:T(8,128)(2,1)S(1)}, bf16[512,128]{1,0:T(8,128)(2,1)S(1)}, u32[]{:S(2)}, u32[]{:S(2)}) %collective-permute-start.6) | collective-permute-done | bytes 131104 | tf_op jit(solution)/shard_map/ppermute | solution.py:301
  43.1 1.7 %cols.1 = (bf16[4096,128]{1,0:T(8,128)(2,1)S(1)}, bf16[128,4096]{1,0:T(8,128)(2,1)S(1)}) custom-call(f32[8,256]{1,0:T(8,128)S(1)} %maximum_maximum_fusion.table, bf16[512,128]{1,0:T(8,128)(2,1)S(1)} %get-tuple-element.22.refs_0_, bf16[512,128]{1,0:T(8,128)(2,1)S(1)} %collective-permute-done.refs_1_, bf16[512,128]{1,0:T(8,128)(2,1)S(1)} %collective-permute-done.1.refs_2_, ...), custom_call_target="tpu_custom_call" | custom-call | flops 2147483648 | bytes 4194304 | tf_op jit(solution)/shard_map/cols/pallas_call | solution.py:334
  44.9 1.0 copy-done.6
  45.8 0.6 all-to-all-done.3.zr
  46.5 6.1 %all-to-all-start.1 = ((bf16[16,64,256]{2,1,0:T(8,128)(2,1)}), bf16[16,64,256]{2,1,0:T(8,128)(2,1)S(1)}, u32[]{:S(2)}, u32[]{:S(2)}) async-start(bf16[16,64,256]{2,1,0:T(8,128)(2,1)} %get-tuple-element.20), calls=%async_computation.1 | async-start | bytes 1048576 | tf_op jit(solution)/shard_map/all_to_all | solution.py:329
  52.6 1.2 copy-done.7
  53.8 15.0 %product.3 = f32[16,32,256]{2,1,0:T(8,128)} custom-call(bf16[16,64,256]{2,1,0:T(8,128)(2,1)S(1)} %all-to-all-done.3.zr, f32[8,4096]{1,0:T(8,128)S(1)} %get-tuple-element.38.weight, bf16[4096,128]{1,0:T(8,128)(2,1)S(1)} %get-tuple-element.23.zc, bf16[128,4096]{1,0:T(8,128)(2,1)S(1)} %copy-done.7), custom_call_target="tpu_custom_call" | custom-call | flops 17179869184 | bytes 4194304 | tf_op jit(solution)/shard_map/product/pallas_call | solution.py:170
  68.8 0.0 all-to-all-done.1.zr
  68.8 6.7 %all-to-all-start.4 = ((f32[16,32,256]{2,1,0:T(8,128)}), f32[16,32,256]{2,1,0:T(8,128)S(1)}, u32[]{:S(2)}, u32[]{:S(2)}) async-start(f32[16,32,256]{2,1,0:T(8,128)} %product.3), calls=%async_computation.4 | async-start | bytes 1048576 | tf_op jit(solution)/shard_map/all_to_all | solution.py:349
  75.5 1.2 copy-done.8
  76.7 15.0 %product.2 = f32[16,32,256]{2,1,0:T(8,128)} custom-call(bf16[16,64,256]{2,1,0:T(8,128)(2,1)S(1)} %all-to-all-done.1.zr, f32[8,4096]{1,0:T(8,128)S(1)} %get-tuple-element.39.weight, bf16[4096,128]{1,0:T(8,128)(2,1)S(1)} %get-tuple-element.23.zc, bf16[128,4096]{1,0:T(8,128)(2,1)S(1)} %copy-done.8), custom_call_target="tpu_custom_call" | custom-call | flops 17179869184 | bytes 4194304 | tf_op jit(solution)/shard_map/product/pallas_call | solution.py:170
  91.7 0.0 all-to-all-done.4.sb
  91.7 6.7 %all-to-all-start.2 = ((f32[16,32,256]{2,1,0:T(8,128)}), f32[16,32,256]{2,1,0:T(8,128)S(1)}, u32[]{:S(2)}, u32[]{:S(2)}) async-start(f32[16,32,256]{2,1,0:T(8,128)} %product.2), calls=%async_computation.2 | async-start | bytes 1048576 | tf_op jit(solution)/shard_map/all_to_all | solution.py:347
  98.4 1.4 %collective-permute-start.7 = (bf16[96,512]{1,0:T(8,128)(2,1)S(1)}, bf16[96,512]{1,0:T(8,128)(2,1)S(1)}, u32[]{:S(2)}, u32[]{:S(2)}) collective-permute-start(bf16[96,512]{1,0:T(8,128)(2,1)S(1)} %get-tuple-element.27.mid), channel_id=1, source_target_pairs={{0,1},{1,2},{2,3},{3,4},{4,5},{5,6},{6,7},{7,8},{8,9},{9,10},{10,1... | collective-permute-start | bytes 294920 | tf_op jit(solution)/shard_map/ppermute | solution.py:331
  99.7 4.2 %collective-permute-start.8 = (bf16[96,512]{1,0:T(8,128)(2,1)S(1)}, bf16[96,512]{1,0:T(8,128)(2,1)S(1)}, u32[]{:S(2)}, u32[]{:S(2)}) collective-permute-start(bf16[96,512]{1,0:T(8,128)(2,1)S(1)} %get-tuple-element.27.mid), channel_id=1, source_target_pairs={{0,127},{1,0},{2,1},{3,2},{4,3},{5,4},{6,5},{7,6},{8,7},{9,8},{10,... | collective-permute-start | bytes 294920 | tf_op jit(solution)/shard_map/ppermute | solution.py:332
  103.9 8.3 %collective-permute-done.7.prev = bf16[96,512]{1,0:T(8,128)(2,1)S(1)} collective-permute-done((bf16[96,512]{1,0:T(8,128)(2,1)S(1)}, bf16[96,512]{1,0:T(8,128)(2,1)S(1)}, u32[]{:S(2)}, u32[]{:S(2)}) %collective-permute-start.7) | collective-permute-done | bytes 98336 | tf_op jit(solution)/shard_map/ppermute | solution.py:331
  112.2 0.0 collective-permute-done.8.nxt
  112.2 1.4 %same.1.diag = f32[32,512]{1,0:T(8,128)S(1)} custom-call(s32[1]{0:T(128)} %bitcast.7.flat, f32[8,512]{1,0:T(8,128)S(1)} %get-tuple-element.26.own, bf16[96,512]{1,0:T(8,128)(2,1)S(1)} %get-tuple-element.27.mid, bf16[96,512]{1,0:T(8,128)(2,1)S(1)} %collective-permute-done.7.prev, bf16[96,512]{1,0:T(8,128)(2,1)S(1)} %collective-permute-done.8.nxt), custom_call_target="tpu_custom_call" | custom-call | flops 2147483648 | bytes 1048576 | tf_op jit(solution)/shard_map/same/pallas_call | solution.py:350
  113.6 0.0 all-to-all-done.2.sa
  113.7 0.4 image.1
  114.1 14.1 %all_to_all.36.stats = f32[128,1,128]{2,1,0:T(1,128)S(1)} all-to-all(f32[128,1,128]{2,1,0:T(1,128)S(1)} %get-tuple-element.28), channel_id=1, replica_groups=mesh['row'=8,'col'=16] {'row','col'}, dimensions={0} | all-to-all | bytes 131072 | tf_op jit(solution)/shard_map/all_to_all | solution.py:370
  128.2 1.1 final.1
  129.2 0.7 copy.17
  130.0 0.7 copy.18
  (8 shorter events, 0.0 us)
Async XLA Ops:
  0.6 1.0 copy-start.9
  1.6 0.7 copy-start
  1.8 0.7 copy-start.5
  1.8 0.7 copy-start.2
  1.8 0.7 copy-start.1
  1.8 0.7 copy-start.3
  1.8 0.7 copy-start.4
  4.0 32.1 %collective-permute-start = (bf16[512,128]{1,0:T(8,128)(2,1)S(1)}, bf16[512,128]{1,0:T(8,128)(2,1)S(1)}, u32[]{:S(2)}, u32[]{:S(2)}) collective-permute-start(bf16[512,128]{1,0:T(8,128)(2,1)S(1)} %get-tuple-element.22.refs_0_), channel_id=1, source_target_pairs={{0,16},{16,32},{32,48},{48,64},{64,80},{80,96},{96,112},{112,0},{1... | collective-permute-start | bytes 393224 | tf_op jit(solution)/shard_map/ppermute | solution.py:301
  6.7 30.3 %collective-permute-start.1 = (bf16[512,128]{1,0:T(8,128)(2,1)S(1)}, bf16[512,128]{1,0:T(8,128)(2,1)S(1)}, u32[]{:S(2)}, u32[]{:S(2)}) collective-permute-start(bf16[512,128]{1,0:T(8,128)(2,1)S(1)} %get-tuple-element.22.refs_0_), channel_id=1, source_target_pairs={{0,32},{16,48},{32,64},{48,80},{64,96},{80,112},{96,0},{112,16},{1... | collective-permute-start | bytes 393224 | tf_op jit(solution)/shard_map/ppermute | solution.py:301
  8.0 30.1 %collective-permute-start.2 = (bf16[512,128]{1,0:T(8,128)(2,1)S(1)}, bf16[512,128]{1,0:T(8,128)(2,1)S(1)}, u32[]{:S(2)}, u32[]{:S(2)}) collective-permute-start(bf16[512,128]{1,0:T(8,128)(2,1)S(1)} %get-tuple-element.22.refs_0_), channel_id=1, source_target_pairs={{0,48},{16,64},{32,80},{48,96},{64,112},{80,0},{96,16},{112,32},{1... | collective-permute-start | bytes 393224 | tf_op jit(solution)/shard_map/ppermute | solution.py:301
  9.7 28.5 %collective-permute-start.3 = (bf16[512,128]{1,0:T(8,128)(2,1)S(1)}, bf16[512,128]{1,0:T(8,128)(2,1)S(1)}, u32[]{:S(2)}, u32[]{:S(2)}) collective-permute-start(bf16[512,128]{1,0:T(8,128)(2,1)S(1)} %get-tuple-element.22.refs_0_), channel_id=1, source_target_pairs={{0,64},{16,80},{32,96},{48,112},{64,0},{80,16},{96,32},{112,48},{1... | collective-permute-start | bytes 393224 | tf_op jit(solution)/shard_map/ppermute | solution.py:301
  10.0 28.1 %collective-permute-start.4 = (bf16[512,128]{1,0:T(8,128)(2,1)S(1)}, bf16[512,128]{1,0:T(8,128)(2,1)S(1)}, u32[]{:S(2)}, u32[]{:S(2)}) collective-permute-start(bf16[512,128]{1,0:T(8,128)(2,1)S(1)} %get-tuple-element.22.refs_0_), channel_id=1, source_target_pairs={{0,80},{16,96},{32,112},{48,0},{64,16},{80,32},{96,48},{112,64},{1... | collective-permute-start | bytes 393224 | tf_op jit(solution)/shard_map/ppermute | solution.py:301
  12.0 9.3 %copy-start.12 = (f32[256]{0:T(256)S(1)}, f32[256]{0:T(256)}, u32[]{:S(2)}) copy-start(f32[256]{0:T(256)} %param.20) | copy-start | bytes 3076
  12.0 19.0 %all-to-all-start = ((bf16[128,4,128]{2,1,0:T(4,128)(2,1)}), bf16[128,4,128]{2,1,0:T(4,128)(2,1)S(1)}, u32[]{:S(2)}, u32[]{:S(2)}) async-start(bf16[128,4,128]{2,1,0:T(4,128)(2,1)} %bitcast.5), calls=%async_computation | async-start | bytes 262144 | tf_op jit(solution)/shard_map/all_to_all | solution.py:299
  21.2 0.7 copy-start.10
  21.3 0.7 copy-start.11
  32.6 13.9 %all-to-all-start.3 = ((bf16[16,64,256]{2,1,0:T(8,128)(2,1)}), bf16[16,64,256]{2,1,0:T(8,128)(2,1)S(1)}, u32[]{:S(2)}, u32[]{:S(2)}) async-start(bf16[16,64,256]{2,1,0:T(8,128)(2,1)} %get-tuple-element.25), calls=%async_computation.3 | async-start | bytes 1048576 | tf_op jit(solution)/shard_map/all_to_all | solution.py:330
  36.1 4.3 %collective-permute-start.5 = (bf16[512,128]{1,0:T(8,128)(2,1)S(1)}, bf16[512,128]{1,0:T(8,128)(2,1)S(1)}, u32[]{:S(2)}, u32[]{:S(2)}) collective-permute-start(bf16[512,128]{1,0:T(8,128)(2,1)S(1)} %get-tuple-element.22.refs_0_), channel_id=1, source_target_pairs={{0,96},{16,112},{32,0},{48,16},{64,32},{80,48},{96,64},{112,80},{1... | collective-permute-start | bytes 393224 | tf_op jit(solution)/shard_map/ppermute | solution.py:301
  37.0 6.1 %collective-permute-start.6 = (bf16[512,128]{1,0:T(8,128)(2,1)S(1)}, bf16[512,128]{1,0:T(8,128)(2,1)S(1)}, u32[]{:S(2)}, u32[]{:S(2)}) collective-permute-start(bf16[512,128]{1,0:T(8,128)(2,1)S(1)} %get-tuple-element.22.refs_0_), channel_id=1, source_target_pairs={{0,112},{16,0},{32,16},{48,32},{64,48},{80,64},{96,80},{112,96},{1... | collective-permute-start | bytes 393224 | tf_op jit(solution)/shard_map/ppermute | solution.py:301
  44.9 1.0 copy-start.6
  46.5 22.3 %all-to-all-start.1 = ((bf16[16,64,256]{2,1,0:T(8,128)(2,1)}), bf16[16,64,256]{2,1,0:T(8,128)(2,1)S(1)}, u32[]{:S(2)}, u32[]{:S(2)}) async-start(bf16[16,64,256]{2,1,0:T(8,128)(2,1)} %get-tuple-element.20), calls=%async_computation.1 | async-start | bytes 1048576 | tf_op jit(solution)/shard_map/all_to_all | solution.py:329
  52.6 1.2 copy-start.7
  68.8 22.9 %all-to-all-start.4 = ((f32[16,32,256]{2,1,0:T(8,128)}), f32[16,32,256]{2,1,0:T(8,128)S(1)}, u32[]{:S(2)}, u32[]{:S(2)}) async-start(f32[16,32,256]{2,1,0:T(8,128)} %product.3), calls=%async_computation.4 | async-start | bytes 1048576 | tf_op jit(solution)/shard_map/all_to_all | solution.py:349
  75.5 1.2 copy-start.8
  91.7 21.9 %all-to-all-start.2 = ((f32[16,32,256]{2,1,0:T(8,128)}), f32[16,32,256]{2,1,0:T(8,128)S(1)}, u32[]{:S(2)}, u32[]{:S(2)}) async-start(f32[16,32,256]{2,1,0:T(8,128)} %product.2), calls=%async_computation.2 | async-start | bytes 1048576 | tf_op jit(solution)/shard_map/all_to_all | solution.py:347
  98.4 13.9 %collective-permute-start.7 = (bf16[96,512]{1,0:T(8,128)(2,1)S(1)}, bf16[96,512]{1,0:T(8,128)(2,1)S(1)}, u32[]{:S(2)}, u32[]{:S(2)}) collective-permute-start(bf16[96,512]{1,0:T(8,128)(2,1)S(1)} %get-tuple-element.27.mid), channel_id=1, source_target_pairs={{0,1},{1,2},{2,3},{3,4},{4,5},{5,6},{6,7},{7,8},{8,9},{9,10},{10,1... | collective-permute-start | bytes 294920 | tf_op jit(solution)/shard_map/ppermute | solution.py:331
  99.7 12.5 %collective-permute-start.8 = (bf16[96,512]{1,0:T(8,128)(2,1)S(1)}, bf16[96,512]{1,0:T(8,128)(2,1)S(1)}, u32[]{:S(2)}, u32[]{:S(2)}) collective-permute-start(bf16[96,512]{1,0:T(8,128)(2,1)S(1)} %get-tuple-element.27.mid), channel_id=1, source_target_pairs={{0,127},{1,0},{2,1},{3,2},{4,3},{5,4},{6,5},{7,6},{8,7},{9,8},{10,... | collective-permute-start | bytes 294920 | tf_op jit(solution)/shard_map/ppermute | solution.py:332

commit v2 on v0

v2 whole, which is shorter than its diff:
```python
import functools

import jax
import jax.numpy as jnp
from jax import lax
from jax.experimental import pallas as pl
from jax.experimental.pallas import tpu as pltpu
from jax.sharding import PartitionSpec as P

F32 = jnp.float32
BF16 = jnp.bfloat16
VMEM = pl.BlockSpec(memory_space=pltpu.VMEM)
SMEM = pl.BlockSpec(memory_space=pltpu.SMEM)
PARAMS = pltpu.CompilerParams(vmem_limit_bytes=16 * 1024 * 1024)
LARGE = pltpu.CompilerParams(vmem_limit_bytes=40 * 1024 * 1024)
V0, T0, P0, N0 = 64, 96, 97, 99
TASK = 70


def iota(shape, dim):
    return lax.broadcasted_iota(jnp.int32, shape, dim)


def split3(x):
    hi = x.astype(BF16)
    rest = x - hi.astype(F32)
    mid = rest.astype(BF16)
    low = (rest - mid.astype(F32)).astype(BF16)
    return hi, mid, low


def look_up(table, task):
    hit = (iota((table.shape[1], task.shape[1]), 0) == task).astype(BF16)
    tab = jnp.concatenate(split3(table), axis=0)
    got = jnp.dot(tab, hit, preferred_element_type=F32)
    return got[0:8] + got[8:16] + got[16:24]


def pack_kernel(
    feat, tid, cnt, rank, probes, net_w, net_b, scale, table, cols, rows_out, vq_out, nv_out, pos_out
):
    rows = feat.shape[1]
    ntask = cnt.shape[1]
    width = probes.shape[0]
    counts = cnt[...].astype(F32)
    before = iota((ntask, ntask), 1) < iota((ntask, ntask), 0)
    start = jnp.sum(jnp.where(before, counts, 0.0), axis=1, keepdims=True)
    task = tid[...]
    hit = iota((ntask, rows), 0) == task
    pos = jnp.sum(jnp.where(hit, start, 0.0), axis=0, keepdims=True) + rank[...].astype(F32)
    pos_col = jnp.concatenate([pos, jnp.zeros((7, rows), F32)], axis=0).T[:, 0:1]
    order = jnp.sum((pos_col < pos).astype(F32), axis=0, keepdims=True)
    tile = jnp.floor(order * (1.0 / 64.0))
    inner = order - tile * 64.0
    block = jnp.floor(inner * 0.25)
    order_r = tile * 64.0 + (inner - block * 4.0) * 16.0 + block
    square = iota((rows, rows), 0)
    place_c = (square == order.astype(jnp.int32)).astype(BF16)
    place_r = (square == order_r.astype(jnp.int32)).astype(BF16)
    column = jnp.concatenate([net_b[...], scale[...], jnp.zeros((6, 64), F32)], axis=0).T
    hidden = jnp.tanh(
        lax.dot_general(
            net_w[...], feat[...], (((0,), (0,)), ((), ())), preferred_element_type=F32
        )
        + column[:, 0:1]
    )
    latent = (hidden * column[:, 1:2]).astype(BF16)
    local = pos - jnp.floor(pos * (1.0 / rows)) * rows
    high = jnp.floor(local * (1.0 / 16.0))
    noise = look_up(table[...], task)[5:6]
    extra = jnp.concatenate(
        [task.astype(F32), high, local - 16.0 * high]
        + [a.astype(F32) for a in split3(noise)]
        + [jnp.zeros((26, rows), F32)],
        axis=0,
    ).astype(BF16)
    whole = jnp.concatenate([latent, probes[...], extra], axis=0)
    turn = (((1,), (1,)), ((), ()))
    cols[...] = lax.dot_general(place_c, whole, turn, preferred_element_type=F32).astype(BF16)
    data = lax.dot_general(place_r, whole, turn, preferred_element_type=F32)
    half = rows // 2
    pair = jnp.concatenate([data[:half, :V0], data[half:, :V0]], axis=1).astype(BF16)
    at = (iota((16, rows), 1) % 16 == iota((16, rows), 0)).astype(BF16)
    group = jnp.where(iota((rows, 128), 0) // 16 == iota((rows, 128), 1), data[:, T0 : T0 + 1], 0.0)
    tasks = jnp.dot(at, group.astype(BF16), preferred_element_type=F32).astype(BF16)
    for k in range(rows_out.shape[0]):
        rows_out[k, :half, :] = pair
        rows_out[k, half:, :] = tasks
    place = data[:, P0 : P0 + 1] * 16.0 + data[:, P0 + 1 : P0 + 2]
    noise_c = data[:, N0 : N0 + 1] + data[:, N0 + 1 : N0 + 2] + data[:, N0 + 2 : N0 + 3]
    v = data[:, V0:T0]
    nv = noise_c * v

    def fold(x, m):
        return jnp.concatenate(
            [x[t * 64 + m * 16 : t * 64 + m * 16 + 16] for t in range(rows // 64)], axis=0
        )

    vq_out[...] = jnp.concatenate([fold(v, m) for m in range(4)], axis=1)
    nv_out[...] = jnp.concatenate([fold(nv, m) for m in range(4)], axis=1)
    lane = iota((rows // 4, 128), 1)
    posq = jnp.zeros((rows // 4, 128), F32)
    for m in range(4):
        posq = jnp.where(lane == 3 * width + m, fold(place, m), posq)
    pos_out[...] = posq


def cols_kernel(table, *refs):
    chunks, (zc, st) = refs[:-2], refs[-2:]
    rows = chunks[0].shape[0]
    count = len(chunks)
    size = 4 * 16 * count
    width = T0 - V0
    for k in range(rows // 64):
        data = jnp.concatenate(
            [ref[g * 16 : g * 16 + 16, :] for g in range(4 * k, 4 * k + 4) for ref in chunks],
            axis=0,
        ).astype(F32)
        span = slice(k * size, (k + 1) * size)
        lane = iota((size, 128), 1)
        z = jnp.where(lane < V0, data, 0.0)
        norm = jnp.sum(z * z, axis=1, keepdims=True) * -0.5
        hi, mid, low = (a.astype(F32) for a in split3(norm))
        z = jnp.where(lane == V0, hi, z)
        z = jnp.where(lane == V0 + 1, mid, z)
        z = jnp.where(lane == V0 + 2, low, z)
        z = jnp.where(jnp.logical_and(lane > V0 + 2, lane < V0 + 6), 1.0, z)
        z = jnp.where(lane == TASK, data[:, T0 : T0 + 1], z)
        zc[span, :] = z.astype(BF16)
        turned = data.T
        weight = look_up(table[...], turned[T0 : T0 + 1].astype(jnp.int32))
        values = turned[V0:T0]
        for q in range(4):
            st[q * width : (q + 1) * width, span] = (weight[q : q + 1] * values).astype(BF16)
        st[4 * width :, span] = values.astype(BF16)


def product_kernel(tile, own_col, table, zr, ext, zc, st, out, own, kern_ref, task_ref, mine):
    t = pl.program_id(0)
    n_col = zr.shape[0]
    wide = n_col * 16
    rows = 4 * wide

    @pl.when(t == 0)
    def _():
        every = ext[...].reshape(wide, 128).astype(F32).T
        for k in range(task_ref.shape[0]):
            task_ref[k] = every[4 * k : 4 * k + 8]

    data = jnp.concatenate(
        [zr[k, m * 16 : m * 16 + 16, :] for m in range(4) for k in range(n_col)], axis=0
    )
    turned = data.astype(F32).T
    z = jnp.where(t < pl.num_programs(0) // 2, turned[:V0], turned[V0:])
    norm = jnp.sum(z * z, axis=0, keepdims=True) * -0.5
    hi, mid, low = (a.astype(F32) for a in split3(norm))
    sub = iota((16, rows), 0)
    extra = jnp.where(sub < 3, 1.0, 0.0)
    extra = jnp.where(sub == 3, hi, extra)
    extra = jnp.where(sub == 4, mid, extra)
    extra = jnp.where(sub == 5, low, extra)
    z = jnp.concatenate([z, extra, jnp.zeros((48, rows), F32)], axis=0).astype(BF16)
    four = task_ref[t]
    task = jnp.concatenate([four[m : m + 1] for m in range(4)], axis=1)
    weight = look_up(table[...], task.astype(jnp.int32))
    width = st.shape[0] // 5
    total = None
    for j in range(zc.shape[0] // tile):
        span = slice(j * tile, (j + 1) * tile)
        x = jnp.dot(zc[span, :], z, preferred_element_type=F32)
        kern = jnp.minimum(jnp.exp(x).astype(BF16), jnp.asarray(1.0, BF16))
        kern_ref[span, :] = kern
        part = jnp.dot(st[: 4 * width, span], kern, preferred_element_type=F32)
        total = part if total is None else total + part
    size = zc.shape[0] // 32
    first = pl.multiple_of(jnp.clip(4 * t - 1, 0, 26) * size, size)
    band = pl.ds(first, 6 * size)
    same = zc[band, TASK : TASK + 1] == task.astype(BF16)
    kept = jnp.where(same, kern_ref[band, :], jnp.asarray(0.0, BF16))
    summed = weight[4:5] * jnp.dot(st[4 * width :, band], kept, preferred_element_type=F32)
    for q in range(4):
        summed = summed + weight[q : q + 1] * total[q * width : (q + 1) * width]
    folded = jnp.concatenate(
        [summed[:, m * wide : (m + 1) * wide] for m in range(4)], axis=0
    ).T.reshape(n_col, 16, 128)
    out[...] = folded.astype(out.dtype)
    mine[...] = folded
    own[...] = mine[own_col[0]]


def product_call(col, table, gathered, zc, st):
    n_col, packed, _ = gathered.shape
    cols = zc.shape[0]
    width = st.shape[0] // 5
    tiles = (packed - 16) // 32
    rows = n_col * 64
    return pl.pallas_call(
        functools.partial(product_kernel, 1024),
        grid=(tiles,),
        in_specs=[
            SMEM,
            pl.BlockSpec(table.shape, lambda i: (0, 0)),
            pl.BlockSpec((n_col, 64, 128), lambda i: (0, i % (tiles // 2), 0)),
            pl.BlockSpec((n_col, 16, 128), lambda i: (0, tiles * 2, 0)),
            pl.BlockSpec((cols, 128), lambda i: (0, 0)),
            pl.BlockSpec((st.shape[0], cols), lambda i: (0, 0)),
        ],
        out_specs=[
            pl.BlockSpec((n_col, 16, 128), lambda i: (0, i, 0)),
            pl.BlockSpec((16, 128), lambda i: (i, 0)),
        ],
        out_shape=[
            jax.ShapeDtypeStruct((n_col, tiles * 16, 128), BF16),
            jax.ShapeDtypeStruct((tiles * 16, 128), F32),
        ],
        scratch_shapes=[
            pltpu.VMEM((cols, rows), BF16),
            pltpu.VMEM((tiles, 8, n_col * 16), F32),
            pltpu.VMEM((n_col, 16, 128), F32),
        ],
        compiler_params=LARGE,
        cost_estimate=pl.CostEstimate(
            flops=2 * tiles * rows * cols * 512, bytes_accessed=4 << 20, transcendentals=0
        ),
        name="product",
    )(col, table, gathered, gathered, zc, st)


def image_kernel(col, parts, own, vq, nv, pos, send):
    n_col = parts.shape[0]
    img = own[...] + nv[...]
    for k in range(n_col):
        img = img + jnp.where(k == col[0], 0.0, parts[k].astype(F32))
    v = vq[...]

    def over(x):
        s = jnp.sum(x, axis=0, keepdims=True)
        return s[:, 0:32] + s[:, 32:64] + s[:, 64:96] + s[:, 96:128]

    vv, vi = over(v * v), over(v * img)
    ratio = jnp.where(vv > 0.0, vi / jnp.where(vv > 0.0, vv, 1.0), 0.0)
    rest = img - jnp.concatenate([ratio] * 4, axis=1) * v
    row = jnp.concatenate([vv, vi, over(rest * rest), jnp.zeros_like(vv)], axis=1)
    send[:, 0, :] = img
    send[:, 1, :] = v
    send[:, 2, :] = pos[...] + row


def final_kernel(got, residual, direction, alpha_out, beta_out):
    n = got.shape[0]
    rows = residual.shape[1]
    img, v, every = got[:, 0, :], got[:, 1, :], got[:, 2, :]
    vv, vi, rr = every[:, 0:32], every[:, 32:64], every[:, 64:96]
    total_v = jnp.sum(vv, axis=0, keepdims=True)
    total_i = jnp.sum(vi, axis=0, keepdims=True)
    center = total_i / total_v
    ratio = jnp.where(vv > 0.0, vi / jnp.where(vv > 0.0, vv, 1.0), 0.0)
    shift = ratio - center
    total_r = jnp.sum(rr + vv * (shift * shift), axis=0, keepdims=True)
    alpha = total_v / total_i
    beta = alpha * alpha * total_r / total_v
    alpha_out[...] = alpha
    beta_out[...] = beta
    res = v - jnp.concatenate([alpha] * 4, axis=1) * img
    pieces = split3(res) + (v.astype(BF16),)
    total = None
    for m in range(4):
        lanes = slice(m * 32, (m + 1) * 32)
        values = jnp.concatenate([p[:, lanes] for p in pieces], axis=1)
        place = every[:, 96 + m : 97 + m].astype(jnp.int32)
        onehot = (iota((n, rows), 1) == place).astype(BF16)
        part = lax.dot_general(
            values, onehot, (((0,), (0,)), ((), ())), preferred_element_type=F32
        )
        total = part if total is None else total + part
    res_t = total[0:32] + total[32:64] + total[64:96]
    residual[...] = res_t
    beta_col = jnp.concatenate([beta, jnp.zeros((7, 32), F32)], axis=0).T[:, 0:1]
    direction[...] = res_t + beta_col * total[96:128]


def body(
    features,
    task_id,
    task_count,
    task_rank,
    probes,
    net_w,
    net_b,
    inv_scale,
    task_mix,
    task_diag,
    task_noise,
):
    rows, feat = features.shape
    n_row, n_col = lax.axis_size("row"), lax.axis_size("col")
    devices = n_row * n_col
    width = probes.shape[1]
    quarter = rows // 4
    col = lax.axis_index("col").astype(jnp.int32).reshape(1)
    ntask = task_count.shape[0]
    table = jnp.concatenate(
        [task_mix.T, task_diag[None], task_noise[None], jnp.zeros((2, ntask), F32)], axis=0
    )
    mine, share, vq, nv, pos = pl.pallas_call(
        pack_kernel,
        in_specs=[VMEM] * 9,
        out_specs=[VMEM] * 5,
        out_shape=[
            jax.ShapeDtypeStruct((rows, 128), BF16),
            jax.ShapeDtypeStruct((n_col, rows // 2 + 16, 128), BF16),
            jax.ShapeDtypeStruct((quarter, 128), F32),
            jax.ShapeDtypeStruct((quarter, 128), F32),
            jax.ShapeDtypeStruct((quarter, 128), F32),
        ],
        compiler_params=PARAMS,
        name="pack",
    )(
        features.T,
        task_id.reshape(1, -1),
        task_count.reshape(1, -1),
        task_rank.reshape(1, -1),
        probes.T,
        net_w,
        net_b.reshape(1, -1),
        inv_scale.reshape(1, -1),
        table,
    )
    chunks = [mine] + [
        lax.ppermute(mine, "row", [(i, (i + k) % n_row) for i in range(n_row)])
        for k in range(1, n_row)
    ]
    gathered = lax.all_to_all(share, "col", split_axis=0, concat_axis=0, tiled=True)
    total = n_row * rows
    zc, st = pl.pallas_call(
        cols_kernel,
        in_specs=[VMEM] * (1 + n_row),
        out_specs=[VMEM, VMEM],
        out_shape=[
            jax.ShapeDtypeStruct((total, 128), BF16),
            jax.ShapeDtypeStruct((5 * width, total), BF16),
        ],
        compiler_params=PARAMS,
        cost_estimate=pl.CostEstimate(flops=1 << 31, bytes_accessed=4 << 20, transcendentals=0),
        name="cols",
    )(table, *chunks)
    parts, own = product_call(col, table, gathered, zc, st)
    summed = lax.all_to_all(parts, "col", split_axis=0, concat_axis=0, tiled=True)
    send = pl.pallas_call(
        image_kernel,
        in_specs=[SMEM] + [VMEM] * 5,
        out_specs=VMEM,
        out_shape=jax.ShapeDtypeStruct((devices, 3, 128), F32),
        compiler_params=PARAMS,
        name="image",
    )(col, summed, own, vq, nv, pos)
    got = lax.all_to_all(send, ("row", "col"), split_axis=0, concat_axis=0, tiled=True)
    residual, direction, alpha, beta = pl.pallas_call(
        final_kernel,
        in_specs=[VMEM],
        out_specs=[VMEM] * 4,
        out_shape=[
            jax.ShapeDtypeStruct((width, rows), F32),
            jax.ShapeDtypeStruct((width, rows), F32),
            jax.ShapeDtypeStruct((1, width), F32),
            jax.ShapeDtypeStruct((1, width), F32),
        ],
        compiler_params=PARAMS,
        name="final",
    )(got)
    return residual.T, direction.T, alpha.reshape(width), beta.reshape(width)


def solution(mesh):
    axes = ("row", "col")
    return jax.shard_map(
        body,
        mesh=mesh,
        in_specs=(
            P(axes, None),
            P(axes),
            P(),
            P(axes),
            P(axes, None),
            P(),
            P(),
            P(),
            P(),
            P(),
            P(),
        ),
        out_specs=(P(axes, None), P(axes, None), P(), P()),
        check_vma=False,
    )
```

time: 445 us -> 115 us (0.26)
  blocking collectives: 175 us -> 36.7 us
  matrix products: 108 us -> 0 us
  waiting for transfers between devices: 100 us -> 6.09 us
  Pallas kernels: 0 us -> 42.4 us
  between operations: 14 us -> 0.7 us
  other arithmetic: 11.2 us -> 0.79 us
  starting transfers between devices: 25.2 us -> 19.3 us
    psum x2 -> x0, blocking collectives: 128 us -> none  [the longest x1 65.8 us: body(): start_sum = lax.psum(jnp.sum(v_float * v_float, axis=0), ('row', 'col'))]
    dot_general x30 -> x0, matrix products: 108 us -> none  [the longest x8 55.6 us: step(): lax.dot_general(zb, col_z, (((1,), (1,)), ((), ())), preferred_element_ty...]
    reduce_scatter x1 -> x0, waiting for transfers between devices: 68.7 us -> none  [body(): lax.psum_scatter(summed, 'col', scatter_dimension=0, tiled=True)]
    all_gather x3 -> x0, blocking collectives: 46.4 us -> none  [the longest x1 17 us: body(): lax.all_gather(sorted_t, 'col', axis=0, tiled=True)]
    pallas_call x0 -> x5, Pallas kernels: none -> 42.4 us  [the longest x1 35.1 us: product_call(): pl.pallas_call(functools.partial(product_kernel, 1024), grid=(tiles,), in...]
    all_to_all x0 -> x2, blocking collectives: none -> 36.7 us  [the longest x1 21 us: body(): lax.all_to_all(send, ('row', 'col'), split_axis=0, concat_axis=0, tiled=T...]
    all_to_all x4 -> x1, waiting for transfers between devices: 31.3 us -> 0.01 us  [body(): lax.all_to_all(share, 'col', split_axis=0, concat_axis=0, tiled=True)]
    all_to_all x4 -> x1, starting transfers between devices: 25.1 us -> 8.43 us  [body(): lax.all_to_all(share, 'col', split_axis=0, concat_axis=0, tiled=True)]
  transfers between devices with their start and end apart: 7 -> 8, of which waited for: 5 -> 3; matrix products, arithmetic and copies ran while one was open for 3% -> 0% of each run, Pallas kernels for 0% -> 2%
where the time goes in v2:
time: 115 us; the launch traced here: 114 us
  Pallas kernels  42.4 us (37%)
  blocking collectives  36.7 us (32%)
  starting transfers between devices  19.3 us (17%)
  local copies, waits for them, and re-layouts  8.12 us (7%)
  waiting for transfers between devices  6.09 us (5%)
    pallas_call x1, Pallas kernels, product_call(): pl.pallas_call(functools.partial(product_kernel, 1024), grid=(tiles,), in...  35.1 us
    all_to_all x1, blocking collectives, body(): lax.all_to_all(send, ('row', 'col'), split_axis=0, concat_axis=0, tiled=T...  21 us
    all_to_all x1, blocking collectives, body(): lax.all_to_all(parts, 'col', split_axis=0, concat_axis=0, tiled=True)  15.7 us
    ppermute x7, starting transfers between devices, body(): lax.ppermute(mine, 'row', [(i, (i + k) % n_row) for i in range(n_row)])  10.9 us
    all_to_all x1, starting transfers between devices, body(): lax.all_to_all(share, 'col', split_axis=0, concat_axis=0, tiled=True)  8.43 us
    unnamed x20, local copies, waits for them, and re-layouts  8.05 us
    ppermute x7, waiting for transfers between devices, body(): lax.ppermute(mine, 'row', [(i, (i + k) % n_row) for i in range(n_row)])  6.09 us
    pallas_call x1, Pallas kernels, body(): pl.pallas_call(pack_kernel, in_specs=[VMEM] * 9, out_specs=[VMEM] * 5, ou...  2.36 us
  transfers between devices with their start and end apart: 8, of which 3 were waited for; matrix products, arithmetic and copies ran while one was open for 0% of the time, Pallas kernels for 2%

profile of v2, /device:TPU:1, one launch (start us, length us, event | category | flops | bytes accessed | tf_op | source)
XLA Modules:
  0.0 114.1 jit_solution(5890678064375961127)
XLA Ops:
  0.6 0.1 pad.3.clone
  0.7 0.8 maximum_maximum_fusion.table
  1.5 0.0 copy-start
  1.5 0.8 copy-done
  2.3 0.0 copy-start.1
  2.3 0.8 copy-done.1
  3.1 0.0 copy-start.2
  3.1 0.7 copy-done.2
  3.8 0.0 copy-start.3
  3.8 0.7 copy-done.3
  4.5 0.0 copy-start.4
  4.5 0.7 copy-done.4
  5.2 0.0 copy-start.5
  5.2 0.7 copy-done.5
  5.9 0.0 copy-start.6
  5.9 0.7 copy-done.6
  6.5 0.0 copy-start.7
  6.5 0.7 copy-done.7
  7.2 2.4 %pack.1 = (bf16[512,128]{1,0:T(8,128)(2,1)S(1)}, bf16[16,272,128]{2,1,0:T(8,128)(2,1)}, f32[128,128]{1,0:T(8,128)S(1)}, f32[128,128]{1,0:T(8,128)S(1)}, f32[128,128]{1,0:T(8,128)S(1)}) custom-call(bf16[64,512]{1,0:T(8,128)(2,1)S(1)} %bitcast.15, s32[1,512]{1,0:T(1,128)S(1)} %bitcast.17, s32[1,256]{1,0:T(1,128)S(1)} %bitcast.19, s32[1,512]{1,0:T(1,128)S(1)} %bitcast.18, ...), custom_call_target="tpu_custom_call" | custom-call | tf_op jit(solution)/shard_map/pack/pallas_call | solution.py:305
  9.5 8.4 %all-to-all-start = ((bf16[16,272,128]{2,1,0:T(8,128)(2,1)}), bf16[16,272,128]{2,1,0:T(8,128)(2,1)S(1)}, u32[]{:S(2)}, u32[]{:S(2)}) async-start(bf16[16,272,128]{2,1,0:T(8,128)(2,1)} %get-tuple-element.17), calls=%async_computation | async-start | bytes 2228224 | tf_op jit(solution)/shard_map/all_to_all | solution.py:333
  18.0 1.0 collective-permute-start.6
  18.9 2.7 %collective-permute-start.5 = (bf16[512,128]{1,0:T(8,128)(2,1)S(1)}, bf16[512,128]{1,0:T(8,128)(2,1)S(1)}, u32[]{:S(2)}, u32[]{:S(2)}) collective-permute-start(bf16[512,128]{1,0:T(8,128)(2,1)S(1)} %get-tuple-element.18.refs_0_), channel_id=1, source_target_pairs={{0,96},{16,112},{32,0},{48,16},{64,32},{80,48},{96,64},{112,80},{1... | collective-permute-start | bytes 393224 | tf_op jit(solution)/shard_map/ppermute | solution.py:330
  21.7 0.7 collective-permute-start.4
  22.4 2.1 %collective-permute-start.3 = (bf16[512,128]{1,0:T(8,128)(2,1)S(1)}, bf16[512,128]{1,0:T(8,128)(2,1)S(1)}, u32[]{:S(2)}, u32[]{:S(2)}) collective-permute-start(bf16[512,128]{1,0:T(8,128)(2,1)S(1)} %get-tuple-element.18.refs_0_), channel_id=1, source_target_pairs={{0,64},{16,80},{32,96},{48,112},{64,0},{80,16},{96,32},{112,48},{1... | collective-permute-start | bytes 393224 | tf_op jit(solution)/shard_map/ppermute | solution.py:330
  24.5 1.0 collective-permute-start.2
  25.6 0.0 collective-permute-done.6.refs_7_
  25.6 0.7 collective-permute-start.1
  26.3 0.0 collective-permute-done.5.refs_6_
  26.3 2.6 %collective-permute-start = (bf16[512,128]{1,0:T(8,128)(2,1)S(1)}, bf16[512,128]{1,0:T(8,128)(2,1)S(1)}, u32[]{:S(2)}, u32[]{:S(2)}) collective-permute-start(bf16[512,128]{1,0:T(8,128)(2,1)S(1)} %get-tuple-element.18.refs_0_), channel_id=1, source_target_pairs={{0,16},{16,32},{32,48},{48,64},{64,80},{80,96},{96,112},{112,0},{1... | collective-permute-start | bytes 393224 | tf_op jit(solution)/shard_map/ppermute | solution.py:330
  28.9 4.2 %collective-permute-done.4.refs_5_ = bf16[512,128]{1,0:T(8,128)(2,1)S(1)} collective-permute-done((bf16[512,128]{1,0:T(8,128)(2,1)S(1)}, bf16[512,128]{1,0:T(8,128)(2,1)S(1)}, u32[]{:S(2)}, u32[]{:S(2)}) %collective-permute-start.4) | collective-permute-done | bytes 131104 | tf_op jit(solution)/shard_map/ppermute | solution.py:330
  33.0 0.0 collective-permute-done.3.refs_4_
  33.0 1.8 %collective-permute-done.2.refs_3_ = bf16[512,128]{1,0:T(8,128)(2,1)S(1)} collective-permute-done((bf16[512,128]{1,0:T(8,128)(2,1)S(1)}, bf16[512,128]{1,0:T(8,128)(2,1)S(1)}, u32[]{:S(2)}, u32[]{:S(2)}) %collective-permute-start.2) | collective-permute-done | bytes 131104 | tf_op jit(solution)/shard_map/ppermute | solution.py:330
  34.9 0.1 collective-permute-done.1.refs_2_
  34.9 0.0 collective-permute-done.refs_1_
  34.9 2.1 %cols.1 = (bf16[4096,128]{1,0:T(8,128)(2,1)S(1)}, bf16[160,4096]{1,0:T(8,128)(2,1)S(1)}) custom-call(f32[8,256]{1,0:T(8,128)S(1)} %maximum_maximum_fusion.table, bf16[512,128]{1,0:T(8,128)(2,1)S(1)} %get-tuple-element.18.refs_0_, bf16[512,128]{1,0:T(8,128)(2,1)S(1)} %collective-permute-done.refs_1_, bf16[512,128]{1,0:T(8,128)(2,1)S(1)} %collective-permute-done.1.refs_2_, ...), custom_call_target="tpu_custom_call" | custom-call | flops 2147483648 | bytes 4194304 | tf_op jit(solution)/shard_map/cols/pallas_call | solution.py:335
  37.0 0.0 copy-start.8
  37.0 1.1 copy-done.8
  38.1 0.0 all-to-all-done.zr.ext
  38.1 0.0 copy-start.9
  38.1 1.3 %copy-done.9 = bf16[160,4096]{1,0:T(8,128)(2,1)S(1)} copy-done((bf16[160,4096]{1,0:T(8,128)(2,1)S(1)}, bf16[160,4096]{1,0:T(8,128)(2,1)}, u32[]{:S(2)}) %copy-start.9) | copy-done | bytes 1310744
  39.4 35.1 %product.1 = (bf16[16,128,128]{2,1,0:T(8,128)(2,1)S(1)}, f32[128,128]{1,0:T(8,128)S(1)}) custom-call(s32[1]{0:T(128)} %bitcast.own_col.col, f32[8,256]{1,0:T(8,128)S(1)} %maximum_maximum_fusion.table, bf16[16,272,128]{2,1,0:T(8,128)(2,1)S(1)} %all-to-all-done.zr.ext, bf16[16,272,128]{2,1,0:T(8,128)(2,1)S(1)} %all-to-all-done.zr.ext, ...), custom_call_target="tpu_custom_call" | custom-call | flops 34359738368 | bytes 4194304 | tf_op jit(solution)/shard_map/product/pallas_call | solution.py:197
  74.6 15.7 %all_to_all.15.parts = bf16[16,128,128]{2,1,0:T(8,128)(2,1)S(1)} all-to-all(bf16[16,128,128]{2,1,0:T(8,128)(2,1)S(1)} %get-tuple-element.21), channel_id=1, replica_groups=mesh['row'=8,'col'=16] {'col'}, dimensions={0} | all-to-all | bytes 1048576 | tf_op jit(solution)/shard_map/all_to_all | solution.py:348
  90.3 0.5 image.1
  90.8 21.0 %all_to_all.16.got = f32[128,3,128]{2,1,0:T(4,128)S(1)} all-to-all(f32[128,3,128]{2,1,0:T(4,128)S(1)} %image.1), channel_id=1, replica_groups=mesh['row'=8,'col'=16] {'row','col'}, dimensions={0} | all-to-all | bytes 393216 | tf_op jit(solution)/shard_map/all_to_all | solution.py:357
  111.8 2.4 %final.1 = (f32[32,512]{1,0:T(8,128)}, f32[32,512]{1,0:T(8,128)}, f32[1,32]{1,0:T(1,128)}, f32[1,32]{1,0:T(1,128)}) custom-call(f32[128,3,128]{2,1,0:T(4,128)S(1)} %all_to_all.16.got), custom_call_target="tpu_custom_call" | custom-call | tf_op jit(solution)/shard_map/final/pallas_call | solution.py:358
  (1 shorter events, 0.0 us)
Async XLA Ops:
  1.5 0.8 copy-start
  2.3 0.8 copy-start.1
  3.1 0.7 copy-start.2
  3.8 0.7 copy-start.3
  4.5 0.7 copy-start.4
  5.2 0.7 copy-start.5
  5.9 0.7 copy-start.6
  6.5 0.7 copy-start.7
  9.5 28.6 %all-to-all-start = ((bf16[16,272,128]{2,1,0:T(8,128)(2,1)}), bf16[16,272,128]{2,1,0:T(8,128)(2,1)S(1)}, u32[]{:S(2)}, u32[]{:S(2)}) async-start(bf16[16,272,128]{2,1,0:T(8,128)(2,1)} %get-tuple-element.17), calls=%async_computation | async-start | bytes 2228224 | tf_op jit(solution)/shard_map/all_to_all | solution.py:333
  18.0 7.6 %collective-permute-start.6 = (bf16[512,128]{1,0:T(8,128)(2,1)S(1)}, bf16[512,128]{1,0:T(8,128)(2,1)S(1)}, u32[]{:S(2)}, u32[]{:S(2)}) collective-permute-start(bf16[512,128]{1,0:T(8,128)(2,1)S(1)} %get-tuple-element.18.refs_0_), channel_id=1, source_target_pairs={{0,112},{16,0},{32,16},{48,32},{64,48},{80,64},{96,80},{112,96},{1... | collective-permute-start | bytes 393224 | tf_op jit(solution)/shard_map/ppermute | solution.py:330
  18.9 7.3 %collective-permute-start.5 = (bf16[512,128]{1,0:T(8,128)(2,1)S(1)}, bf16[512,128]{1,0:T(8,128)(2,1)S(1)}, u32[]{:S(2)}, u32[]{:S(2)}) collective-permute-start(bf16[512,128]{1,0:T(8,128)(2,1)S(1)} %get-tuple-element.18.refs_0_), channel_id=1, source_target_pairs={{0,96},{16,112},{32,0},{48,16},{64,32},{80,48},{96,64},{112,80},{1... | collective-permute-start | bytes 393224 | tf_op jit(solution)/shard_map/ppermute | solution.py:330
  21.7 11.3 %collective-permute-start.4 = (bf16[512,128]{1,0:T(8,128)(2,1)S(1)}, bf16[512,128]{1,0:T(8,128)(2,1)S(1)}, u32[]{:S(2)}, u32[]{:S(2)}) collective-permute-start(bf16[512,128]{1,0:T(8,128)(2,1)S(1)} %get-tuple-element.18.refs_0_), channel_id=1, source_target_pairs={{0,80},{16,96},{32,112},{48,0},{64,16},{80,32},{96,48},{112,64},{1... | collective-permute-start | bytes 393224 | tf_op jit(solution)/shard_map/ppermute | solution.py:330
  22.4 10.7 %collective-permute-start.3 = (bf16[512,128]{1,0:T(8,128)(2,1)S(1)}, bf16[512,128]{1,0:T(8,128)(2,1)S(1)}, u32[]{:S(2)}, u32[]{:S(2)}) collective-permute-start(bf16[512,128]{1,0:T(8,128)(2,1)S(1)} %get-tuple-element.18.refs_0_), channel_id=1, source_target_pairs={{0,64},{16,80},{32,96},{48,112},{64,0},{80,16},{96,32},{112,48},{1... | collective-permute-start | bytes 393224 | tf_op jit(solution)/shard_map/ppermute | solution.py:330
  24.5 10.3 %collective-permute-start.2 = (bf16[512,128]{1,0:T(8,128)(2,1)S(1)}, bf16[512,128]{1,0:T(8,128)(2,1)S(1)}, u32[]{:S(2)}, u32[]{:S(2)}) collective-permute-start(bf16[512,128]{1,0:T(8,128)(2,1)S(1)} %get-tuple-element.18.refs_0_), channel_id=1, source_target_pairs={{0,48},{16,64},{32,80},{48,96},{64,112},{80,0},{96,16},{112,32},{1... | collective-permute-start | bytes 393224 | tf_op jit(solution)/shard_map/ppermute | solution.py:330
  25.6 9.4 %collective-permute-start.1 = (bf16[512,128]{1,0:T(8,128)(2,1)S(1)}, bf16[512,128]{1,0:T(8,128)(2,1)S(1)}, u32[]{:S(2)}, u32[]{:S(2)}) collective-permute-start(bf16[512,128]{1,0:T(8,128)(2,1)S(1)} %get-tuple-element.18.refs_0_), channel_id=1, source_target_pairs={{0,32},{16,48},{32,64},{48,80},{64,96},{80,112},{96,0},{112,16},{1... | collective-permute-start | bytes 393224 | tf_op jit(solution)/shard_map/ppermute | solution.py:330
  26.3 8.7 %collective-permute-start = (bf16[512,128]{1,0:T(8,128)(2,1)S(1)}, bf16[512,128]{1,0:T(8,128)(2,1)S(1)}, u32[]{:S(2)}, u32[]{:S(2)}) collective-permute-start(bf16[512,128]{1,0:T(8,128)(2,1)S(1)} %get-tuple-element.18.refs_0_), channel_id=1, source_target_pairs={{0,16},{16,32},{32,48},{48,64},{64,80},{80,96},{96,112},{112,0},{1... | collective-permute-start | bytes 393224 | tf_op jit(solution)/shard_map/ppermute | solution.py:330
  37.0 1.1 copy-start.8
  38.1 1.3 %copy-start.9 = (bf16[160,4096]{1,0:T(8,128)(2,1)S(1)}, bf16[160,4096]{1,0:T(8,128)(2,1)}, u32[]{:S(2)}) copy-start(bf16[160,4096]{1,0:T(8,128)(2,1)} %copy-done.8) | copy-start | bytes 3932164

commit v3 on v2

--- a/solution.py
+++ b/solution.py
@@ -1,4 +1,5 @@
 import functools
+import math
 
 import jax
 import jax.numpy as jnp
@@ -12,9 +13,11 @@
 VMEM = pl.BlockSpec(memory_space=pltpu.VMEM)
 SMEM = pl.BlockSpec(memory_space=pltpu.SMEM)
 PARAMS = pltpu.CompilerParams(vmem_limit_bytes=16 * 1024 * 1024)
+ALONE = pltpu.CompilerParams(vmem_limit_bytes=60 * 1024 * 1024)
 LARGE = pltpu.CompilerParams(vmem_limit_bytes=40 * 1024 * 1024)
-V0, T0, P0, N0 = 64, 96, 97, 99
-TASK = 70
+V0, T0, P0, N0 = 64, 96, 97, 112
+NORM, TASK = 192, 198
+LOG2E = math.log2(math.e)
 
 
 def iota(shape, dim):
@@ -36,27 +39,21 @@
     return got[0:8] + got[8:16] + got[16:24]
 
 
-def pack_kernel(
-    feat, tid, cnt, rank, probes, net_w, net_b, scale, table, cols, rows_out, vq_out, nv_out, pos_out
-):
-    rows = feat.shape[1]
-    ntask = cnt.shape[1]
-    width = probes.shape[0]
+def order_of(tid, cnt, rank):
+    rows, ntask = tid.shape[1], cnt.shape[1]
     counts = cnt[...].astype(F32)
     before = iota((ntask, ntask), 1) < iota((ntask, ntask), 0)
     start = jnp.sum(jnp.where(before, counts, 0.0), axis=1, keepdims=True)
-    task = tid[...]
-    hit = iota((ntask, rows), 0) == task
+    hit = iota((ntask, rows), 0) == tid[...]
     pos = jnp.sum(jnp.where(hit, start, 0.0), axis=0, keepdims=True) + rank[...].astype(F32)
     pos_col = jnp.concatenate([pos, jnp.zeros((7, rows), F32)], axis=0).T[:, 0:1]
-    order = jnp.sum((pos_col < pos).astype(F32), axis=0, keepdims=True)
-    tile = jnp.floor(order * (1.0 / 64.0))
-    inner = order - tile * 64.0
-    block = jnp.floor(inner * 0.25)
-    order_r = tile * 64.0 + (inner - block * 4.0) * 16.0 + block
-    square = iota((rows, rows), 0)
-    place_c = (square == order.astype(jnp.int32)).astype(BF16)
-    place_r = (square == order_r.astype(jnp.int32)).astype(BF16)
+    return pos, jnp.sum((pos_col < pos).astype(F32), axis=0, keepdims=True)
+
+
+def pack_cols_kernel(feat, tid, cnt, rank, probes, net_w, net_b, scale, cols, whole_out, order_out):
+    rows = feat.shape[1]
+    pos, order = order_of(tid, cnt, rank)
+    place = (iota((rows, rows), 0) == order.astype(jnp.int32)).astype(BF16)
     column = jnp.concatenate([net_b[...], scale[...], jnp.zeros((6, 64), F32)], axis=0).T
     hidden = jnp.tanh(
         lax.dot_general(
@@ -67,17 +64,34 @@
     latent = (hidden * column[:, 1:2]).astype(BF16)
     local = pos - jnp.floor(pos * (1.0 / rows)) * rows
     high = jnp.floor(local * (1.0 / 16.0))
-    noise = look_up(table[...], task)[5:6]
     extra = jnp.concatenate(
-        [task.astype(F32), high, local - 16.0 * high]
-        + [a.astype(F32) for a in split3(noise)]
-        + [jnp.zeros((26, rows), F32)],
-        axis=0,
+        [tid[...].astype(F32), high, local - 16.0 * high, jnp.zeros((29, rows), F32)], axis=0
     ).astype(BF16)
     whole = jnp.concatenate([latent, probes[...], extra], axis=0)
-    turn = (((1,), (1,)), ((), ()))
-    cols[...] = lax.dot_general(place_c, whole, turn, preferred_element_type=F32).astype(BF16)
-    data = lax.dot_general(place_r, whole, turn, preferred_element_type=F32)
+    whole_out[...] = whole
+    order_out[...] = jnp.concatenate([order, jnp.zeros((7, rows), F32)], axis=0)
+    cols[...] = lax.dot_general(
+        place, whole, (((1,), (1,)), ((), ())), preferred_element_type=F32
+    ).astype(BF16)
+
+
+def pack_rows_kernel(whole, order_in, table, rows_out, vq_out, nv_out, pos_out):
+    rows = whole.shape[1]
+    width = T0 - V0
+    order = order_in[0:1]
+    tile = jnp.floor(order * (1.0 / 64.0))
+    inner = order - tile * 64.0
+    block = jnp.floor(inner * 0.25)
+    order_r = tile * 64.0 + (inner - block * 4.0) * 16.0 + block
+    place_r = (iota((rows, rows), 0) == order_r.astype(jnp.int32)).astype(BF16)
+    noise = look_up(table[...], whole[T0 : T0 + 1].astype(jnp.int32))[5:6]
+    noise = jnp.concatenate(split3(noise) + (jnp.zeros((13, rows), BF16),), axis=0)
+    data = lax.dot_general(
+        place_r,
+        jnp.concatenate([whole[: T0 + 16], noise], axis=0),
+        (((1,), (1,)), ((), ())),
+        preferred_element_type=F32,
+    )
     half = rows // 2
     pair = jnp.concatenate([data[:half, :V0], data[half:, :V0]], axis=1).astype(BF16)
     at = (iota((16, rows), 1) % 16 == iota((16, rows), 0)).astype(BF16)
@@ -119,14 +133,15 @@
         span = slice(k * size, (k + 1) * size)
         lane = iota((size, 128), 1)
         z = jnp.where(lane < V0, data, 0.0)
-        norm = jnp.sum(z * z, axis=1, keepdims=True) * -0.5
-        hi, mid, low = (a.astype(F32) for a in split3(norm))
-        z = jnp.where(lane == V0, hi, z)
-        z = jnp.where(lane == V0 + 1, mid, z)
-        z = jnp.where(lane == V0 + 2, low, z)
-        z = jnp.where(jnp.logical_and(lane > V0 + 2, lane < V0 + 6), 1.0, z)
-        z = jnp.where(lane == TASK, data[:, T0 : T0 + 1], z)
-        zc[span, :] = z.astype(BF16)
+        norm = jnp.sum(z * z, axis=1, keepdims=True) * (-0.5 * LOG2E)
+        hi, mid, low = (p.astype(F32) for p in split3(z * LOG2E))
+        zc[span, :128] = (hi + pltpu.roll(mid, V0, 1)).astype(BF16)
+        hi, mid, task = (p.astype(F32) for p in split3(norm))
+        low = jnp.where(lane == NORM - 128, hi, low)
+        low = jnp.where(lane == NORM - 127, mid, low)
+        low = jnp.where(lane == NORM - 126, task, low)
+        low = jnp.where(jnp.logical_and(lane > NORM - 126, lane < NORM - 122), 1.0, low)
+        zc[span, 128:] = jnp.where(lane == TASK - 128, data[:, T0 : T0 + 1], low).astype(BF16)
         turned = data.T
         weight = look_up(table[...], turned[T0 : T0 + 1].astype(jnp.int32))
         values = turned[V0:T0]
@@ -152,14 +167,15 @@
     )
     turned = data.astype(F32).T
     z = jnp.where(t < pl.num_programs(0) // 2, turned[:V0], turned[V0:])
-    norm = jnp.sum(z * z, axis=0, keepdims=True) * -0.5
+    norm = jnp.sum(z * z, axis=0, keepdims=True) * (-0.5 * LOG2E)
     hi, mid, low = (a.astype(F32) for a in split3(norm))
     sub = iota((16, rows), 0)
     extra = jnp.where(sub < 3, 1.0, 0.0)
     extra = jnp.where(sub == 3, hi, extra)
     extra = jnp.where(sub == 4, mid, extra)
     extra = jnp.where(sub == 5, low, extra)
-    z = jnp.concatenate([z, extra, jnp.zeros((48, rows), F32)], axis=0).astype(BF16)
+    z = z.astype(BF16)
+    z = jnp.concatenate([z, z, z, extra.astype(BF16), jnp.zeros((48, rows), BF16)], axis=0)
     four = task_ref[t]
     task = jnp.concatenate([four[m : m + 1] for m in range(4)], axis=1)
     weight = look_up(table[...], task.astype(jnp.int32))
@@ -168,7 +184,7 @@
     for j in range(zc.shape[0] // tile):
         span = slice(j * tile, (j + 1) * tile)
         x = jnp.dot(zc[span, :], z, preferred_element_type=F32)
-        kern = jnp.minimum(jnp.exp(x).astype(BF16), jnp.asarray(1.0, BF16))
+        kern = jnp.minimum(jnp.exp2(x).astype(BF16), jnp.asarray(1.0, BF16))
         kern_ref[span, :] = kern
         part = jnp.dot(st[: 4 * width, span], kern, preferred_element_type=F32)
         total = part if total is None else total + part
@@ -202,7 +218,7 @@
             pl.BlockSpec(table.shape, lambda i: (0, 0)),
             pl.BlockSpec((n_col, 64, 128), lambda i: (0, i % (tiles // 2), 0)),
             pl.BlockSpec((n_col, 16, 128), lambda i: (0, tiles * 2, 0)),
-            pl.BlockSpec((cols, 128), lambda i: (0, 0)),
+            pl.BlockSpec(zc.shape, lambda i: (0, 0)),
             pl.BlockSpec((st.shape[0], cols), lambda i: (0, 0)),
         ],
         out_specs=[
@@ -302,19 +318,17 @@
     table = jnp.concatenate(
         [task_mix.T, task_diag[None], task_noise[None], jnp.zeros((2, ntask), F32)], axis=0
     )
-    mine, share, vq, nv, pos = pl.pallas_call(
-        pack_kernel,
-        in_specs=[VMEM] * 9,
-        out_specs=[VMEM] * 5,
+    mine, whole, order = pl.pallas_call(
+        pack_cols_kernel,
+        in_specs=[VMEM] * 8,
+        out_specs=[VMEM] * 3,
         out_shape=[
             jax.ShapeDtypeStruct((rows, 128), BF16),
-            jax.ShapeDtypeStruct((n_col, rows // 2 + 16, 128), BF16),
-            jax.ShapeDtypeStruct((quarter, 128), F32),
-            jax.ShapeDtypeStruct((quarter, 128), F32),
-            jax.ShapeDtypeStruct((quarter, 128), F32),
-        ],
-        compiler_params=PARAMS,
-        name="pack",
+            jax.ShapeDtypeStruct((128, rows), BF16),
+            jax.ShapeDtypeStruct((8, rows), F32),
+        ],
+        compiler_params=ALONE,
+        name="pack_cols",
     )(
         features.T,
         task_id.reshape(1, -1),
@@ -324,12 +338,25 @@
         net_w,
         net_b.reshape(1, -1),
         inv_scale.reshape(1, -1),
-        table,
     )
     chunks = [mine] + [
-        lax.ppermute(mine, "row", [(i, (i + k) % n_row) for i in range(n_row)])
-        for k in range(1, n_row)
+        lax.ppermute(mine, "row", [(i, (i + 2 * k) % n_row) for i in range(n_row)])
+        for k in range(1, n_row // 2)
     ]
+    chunks = chunks + [lax.ppermute(c, "row", [(i, i ^ 1) for i in range(n_row)]) for c in chunks]
+    share, vq, nv, pos = pl.pallas_call(
+        pack_rows_kernel,
+        in_specs=[VMEM] * 3,
+        out_specs=[VMEM] * 4,
+        out_shape=[
+            jax.ShapeDtypeStruct((n_col, rows // 2 + 16, 128), BF16),
+            jax.ShapeDtypeStruct((quarter, 128), F32),
+            jax.ShapeDtypeStruct((quarter, 128), F32),
+            jax.ShapeDtypeStruct((quarter, 128), F32),
+        ],
+        compiler_params=PARAMS,
+        name="pack_rows",
+    )(whole, order, table)
     gathered = lax.all_to_all(share, "col", split_axis=0, concat_axis=0, tiled=True)
     total = n_row * rows
     zc, st = pl.pallas_call(
@@ -337,7 +364,7 @@
         in_specs=[VMEM] * (1 + n_row),
         out_specs=[VMEM, VMEM],
         out_shape=[
-            jax.ShapeDtypeStruct((total, 128), BF16),
+            jax.ShapeDtypeStruct((total, 256), BF16),
             jax.ShapeDtypeStruct((5 * width, total), BF16),
         ],
         compiler_params=PARAMS,

time: 115 us -> 110 us (0.957)
  blocking collectives: 36.7 us -> 32.7 us
  Pallas kernels: 42.4 us -> 46.2 us
  waiting for transfers between devices: 6.09 us -> 3.41 us
    all_to_all x1, blocking collectives: 21 us -> 15.9 us  [body(): lax.all_to_all(send, ('row', 'col'), split_axis=0, concat_axis=0, tiled=T...]
    ppermute x7, waiting for transfers between devices: 6.09 us -> 3.41 us  [the longest x3 2.42 us: body(): lax.ppermute(mine, 'row', [(i, (i + 2 * k) % n_row) for i in range(n_row)])]
    pallas_call x1 -> x2, Pallas kernels: 2.36 us -> 4.21 us  [the longest x1 2.3 us: body(): pl.pallas_call(pack_cols_kernel, in_specs=[VMEM] * 8, out_specs=[VMEM] *...]
    pallas_call x1, Pallas kernels: 35.1 us -> 36.4 us  [product_call(): pl.pallas_call(functools.partial(product_kernel, 1024), grid=(tiles,), in...]
    unnamed x20 -> x14, local copies, waits for them, and re-layouts: 8.05 us -> 6.93 us
  transfers between devices with their start and end apart: 8 -> 8, of which waited for: 3 -> 3; matrix products, arithmetic and copies ran while one was open for 0% -> 0% of each run, Pallas kernels for 2% -> 3%
where the time goes in v3:
time: 110 us
  Pallas kernels  46.2 us (42%)
  blocking collectives  32.7 us (30%)
  starting transfers between devices  19 us (17%)
  local copies, waits for them, and re-layouts  7 us (6%)
  waiting for transfers between devices  3.41 us (3%)
    pallas_call x1, Pallas kernels, product_call(): pl.pallas_call(functools.partial(product_kernel, 1024), grid=(tiles,), in...  36.4 us
    all_to_all x1, blocking collectives, body(): lax.all_to_all(parts, 'col', split_axis=0, concat_axis=0, tiled=True)  16.8 us
    all_to_all x1, blocking collectives, body(): lax.all_to_all(send, ('row', 'col'), split_axis=0, concat_axis=0, tiled=T...  15.9 us
    all_to_all x1, starting transfers between devices, body(): lax.all_to_all(share, 'col', split_axis=0, concat_axis=0, tiled=True)  8.43 us
    unnamed x14, local copies, waits for them, and re-layouts  6.93 us
    ppermute x4, starting transfers between devices, body(): lax.ppermute(c, 'row', [(i, i ^ 1) for i in range(n_row)])  6.76 us
    ppermute x3, starting transfers between devices, body(): lax.ppermute(mine, 'row', [(i, (i + 2 * k) % n_row) for i in range(n_row)])  3.85 us
    pallas_call x1, Pallas kernels, body(): pl.pallas_call(cols_kernel, in_specs=[VMEM] * (1 + n_row), out_specs=[VME...  2.77 us
  transfers between devices with their start and end apart: 8, of which 3 were waited for; matrix products, arithmetic and copies ran while one was open for 0% of the time, Pallas kernels for 3%

profile of v3, /device:TPU:1, one launch (start us, length us, event | category | flops | bytes accessed | tf_op | source)
XLA Modules:
  0.0 109.9 jit_solution(1000001388777274693)
XLA Ops:
  0.6 0.1 pad.3.clone
  0.7 0.8 maximum_maximum_fusion.table
  1.5 2.3 %pack_cols.1 = (bf16[512,128]{1,0:T(8,128)(2,1)}, bf16[128,512]{1,0:T(8,128)(2,1)}, f32[8,512]{1,0:T(8,128)}) custom-call(bf16[64,512]{1,0:T(8,128)(2,1)} %bitcast.15, s32[1,512]{1,0:T(1,128)} %bitcast.18, s32[1,256]{1,0:T(1,128)} %bitcast.20, s32[1,512]{1,0:T(1,128)} %bitcast.19, bf16[32,512]{1,0:T(8,128)(2,1)} %bitcast.16, bf16[64,64]{1,0:T(8,128)(2,1)} %net_w.1, ...), custom_call_target="tpu_custom_call" | custom-call | tf_op jit(solution)/shard_map/pack_cols/pallas_call | solution.py:321
  3.8 0.0 copy-start
  3.8 0.9 copy-done
  4.7 0.0 copy-start.1
  4.7 0.7 copy-done.1
  5.4 0.0 copy-start.2
  5.4 1.9 %pack_rows.1 = (bf16[16,272,128]{2,1,0:T(8,128)(2,1)}, f32[128,128]{1,0:T(8,128)S(1)}, f32[128,128]{1,0:T(8,128)S(1)}, f32[128,128]{1,0:T(8,128)S(1)}) custom-call(bf16[128,512]{1,0:T(8,128)(2,1)S(1)} %copy-done, f32[8,512]{1,0:T(8,128)S(1)} %copy-done.1, f32[8,256]{1,0:T(8,128)S(1)} %maximum_maximum_fusion.table), custom_call_target="tpu_custom_call" | custom-call | tf_op jit(solution)/shard_map/pack_rows/pallas_call | solution.py:347
  7.3 8.4 %all-to-all-start = ((bf16[16,272,128]{2,1,0:T(8,128)(2,1)}), bf16[16,272,128]{2,1,0:T(8,128)(2,1)S(1)}, u32[]{:S(2)}, u32[]{:S(2)}) async-start(bf16[16,272,128]{2,1,0:T(8,128)(2,1)} %get-tuple-element.21), calls=%async_computation | async-start | bytes 2228224 | tf_op jit(solution)/shard_map/all_to_all | solution.py:360
  15.8 0.0 copy-done.2
  15.8 2.8 %collective-permute-start.2 = (bf16[512,128]{1,0:T(8,128)(2,1)S(1)}, bf16[512,128]{1,0:T(8,128)(2,1)S(1)}, u32[]{:S(2)}, u32[]{:S(2)}) collective-permute-start(bf16[512,128]{1,0:T(8,128)(2,1)S(1)} %copy-done.2), channel_id=1, source_target_pairs={{0,96},{16,112},{32,0},{48,16},{64,32},{80,48},{96,64},{112,80},{1... | collective-permute-start | bytes 393224 | tf_op jit(solution)/shard_map/ppermute | solution.py:343
  18.6 0.3 collective-permute-start.1
  18.9 0.7 collective-permute-start
  19.6 1.8 %collective-permute-start.3 = (bf16[512,128]{1,0:T(8,128)(2,1)S(1)}, bf16[512,128]{1,0:T(8,128)(2,1)S(1)}, u32[]{:S(2)}, u32[]{:S(2)}) collective-permute-start(bf16[512,128]{1,0:T(8,128)(2,1)S(1)} %copy-done.2), channel_id=1, source_target_pairs={{0,16},{16,0},{32,48},{48,32},{64,80},{80,64},{96,112},{112,96},{1... | collective-permute-start | bytes 393224 | tf_op jit(solution)/shard_map/ppermute | solution.py:346
  21.4 2.0 %collective-permute-done.2.refs_3_ = bf16[512,128]{1,0:T(8,128)(2,1)S(1)} collective-permute-done((bf16[512,128]{1,0:T(8,128)(2,1)S(1)}, bf16[512,128]{1,0:T(8,128)(2,1)S(1)}, u32[]{:S(2)}, u32[]{:S(2)}) %collective-permute-start.2) | collective-permute-done | bytes 131104 | tf_op jit(solution)/shard_map/ppermute | solution.py:343
  23.4 1.7 %collective-permute-start.6 = (bf16[512,128]{1,0:T(8,128)(2,1)S(1)}, bf16[512,128]{1,0:T(8,128)(2,1)S(1)}, u32[]{:S(2)}, u32[]{:S(2)}) collective-permute-start(bf16[512,128]{1,0:T(8,128)(2,1)S(1)} %collective-permute-done.2.refs_3_), channel_id=1, source_target_pairs={{0,16},{16,0},{32,48},{48,32},{64,80},{80,64},{96,112},{112,96},{1... | collective-permute-start | bytes 393224 | tf_op jit(solution)/shard_map/ppermute | solution.py:346
  25.1 0.0 collective-permute-done.1.refs_2_
  25.1 2.3 %collective-permute-start.5 = (bf16[512,128]{1,0:T(8,128)(2,1)S(1)}, bf16[512,128]{1,0:T(8,128)(2,1)S(1)}, u32[]{:S(2)}, u32[]{:S(2)}) collective-permute-start(bf16[512,128]{1,0:T(8,128)(2,1)S(1)} %collective-permute-done.1.refs_2_), channel_id=1, source_target_pairs={{0,16},{16,0},{32,48},{48,32},{64,80},{80,64},{96,112},{112,96},{1... | collective-permute-start | bytes 393224 | tf_op jit(solution)/shard_map/ppermute | solution.py:346
  27.4 0.4 collective-permute-done.refs_1_
  27.9 0.9 collective-permute-start.4
  28.8 0.0 collective-permute-done.3.refs_4_
  28.8 0.0 collective-permute-done.6.refs_7_
  28.8 0.0 collective-permute-done.5.refs_6_
  28.8 1.0 collective-permute-done.4.refs_5_
  29.8 2.8 %cols.1 = (bf16[4096,256]{1,0:T(8,128)(2,1)S(1)}, bf16[160,4096]{1,0:T(8,128)(2,1)S(1)}) custom-call(f32[8,256]{1,0:T(8,128)S(1)} %maximum_maximum_fusion.table, bf16[512,128]{1,0:T(8,128)(2,1)S(1)} %copy-done.2, bf16[512,128]{1,0:T(8,128)(2,1)S(1)} %collective-permute-done.refs_1_, bf16[512,128]{1,0:T(8,128)(2,1)S(1)} %collective-permute-done.1.refs_2_, ...), custom_call_target="tpu_custom_call" | custom-call | flops 2147483648 | bytes 4194304 | tf_op jit(solution)/shard_map/cols/pallas_call | solution.py:362
  32.6 0.0 copy-start.3
  32.6 1.3 %copy-done.3 = bf16[4096,256]{1,0:T(8,128)(2,1)} copy-done((bf16[4096,256]{1,0:T(8,128)(2,1)}, bf16[4096,256]{1,0:T(8,128)(2,1)S(1)}, u32[]{:S(2)}) %copy-start.3) | copy-done | bytes 2097176
  33.9 0.0 copy-start.5
  33.9 1.1 copy-done.5
  35.0 0.0 all-to-all-done.zr.ext
  35.0 0.0 copy-start.4
  35.0 1.6 %copy-done.4 = bf16[4096,256]{1,0:T(8,128)(2,1)S(1)} copy-done((bf16[4096,256]{1,0:T(8,128)(2,1)S(1)}, bf16[4096,256]{1,0:T(8,128)(2,1)}, u32[]{:S(2)}) %copy-start.4) | copy-done | bytes 2097176
  36.6 0.0 copy-start.6
  36.6 1.3 %copy-done.6 = bf16[160,4096]{1,0:T(8,128)(2,1)S(1)} copy-done((bf16[160,4096]{1,0:T(8,128)(2,1)S(1)}, bf16[160,4096]{1,0:T(8,128)(2,1)}, u32[]{:S(2)}) %copy-start.6) | copy-done | bytes 1310744
  37.9 36.4 %product.1 = (bf16[16,128,128]{2,1,0:T(8,128)(2,1)S(1)}, f32[128,128]{1,0:T(8,128)S(1)}) custom-call(s32[1]{0:T(128)} %bitcast.own_col.col, f32[8,256]{1,0:T(8,128)S(1)} %maximum_maximum_fusion.table, bf16[16,272,128]{2,1,0:T(8,128)(2,1)S(1)} %all-to-all-done.zr.ext, bf16[16,272,128]{2,1,0:T(8,128)(2,1)S(1)} %all-to-all-done.zr.ext, ...), custom_call_target="tpu_custom_call" | custom-call | flops 34359738368 | bytes 4194304 | tf_op jit(solution)/shard_map/product/pallas_call | solution.py:213
  74.3 16.8 %all_to_all.15.parts = bf16[16,128,128]{2,1,0:T(8,128)(2,1)S(1)} all-to-all(bf16[16,128,128]{2,1,0:T(8,128)(2,1)S(1)} %get-tuple-element.25), channel_id=1, replica_groups=mesh['row'=8,'col'=16] {'col'}, dimensions={0} | all-to-all | bytes 1048576 | tf_op jit(solution)/shard_map/all_to_all | solution.py:375
  91.1 0.5 image.1
  91.6 15.9 %all_to_all.16.got = f32[128,3,128]{2,1,0:T(4,128)S(1)} all-to-all(f32[128,3,128]{2,1,0:T(4,128)S(1)} %image.1), channel_id=1, replica_groups=mesh['row'=8,'col'=16] {'row','col'}, dimensions={0} | all-to-all | bytes 393216 | tf_op jit(solution)/shard_map/all_to_all | solution.py:384
  107.6 2.4 %final.1 = (f32[32,512]{1,0:T(8,128)}, f32[32,512]{1,0:T(8,128)}, f32[1,32]{1,0:T(1,128)}, f32[1,32]{1,0:T(1,128)}) custom-call(f32[128,3,128]{2,1,0:T(4,128)S(1)} %all_to_all.16.got), custom_call_target="tpu_custom_call" | custom-call | tf_op jit(solution)/shard_map/final/pallas_call | solution.py:385
  (1 shorter events, 0.0 us)
Async XLA Ops:
  3.8 0.9 copy-start
  4.7 0.7 copy-start.1
  5.4 10.3 %copy-start.2 = (bf16[512,128]{1,0:T(8,128)(2,1)S(1)}, bf16[512,128]{1,0:T(8,128)(2,1)}, u32[]{:S(2)}) copy-start(bf16[512,128]{1,0:T(8,128)(2,1)} %get-tuple-element.22.refs_0_) | copy-start | bytes 393220
  7.3 27.6 %all-to-all-start = ((bf16[16,272,128]{2,1,0:T(8,128)(2,1)}), bf16[16,272,128]{2,1,0:T(8,128)(2,1)S(1)}, u32[]{:S(2)}, u32[]{:S(2)}) async-start(bf16[16,272,128]{2,1,0:T(8,128)(2,1)} %get-tuple-element.21), calls=%async_computation | async-start | bytes 2228224 | tf_op jit(solution)/shard_map/all_to_all | solution.py:360
  15.8 7.6 %collective-permute-start.2 = (bf16[512,128]{1,0:T(8,128)(2,1)S(1)}, bf16[512,128]{1,0:T(8,128)(2,1)S(1)}, u32[]{:S(2)}, u32[]{:S(2)}) collective-permute-start(bf16[512,128]{1,0:T(8,128)(2,1)S(1)} %copy-done.2), channel_id=1, source_target_pairs={{0,96},{16,112},{32,0},{48,16},{64,32},{80,48},{96,64},{112,80},{1... | collective-permute-start | bytes 393224 | tf_op jit(solution)/shard_map/ppermute | solution.py:343
  18.6 6.5 %collective-permute-start.1 = (bf16[512,128]{1,0:T(8,128)(2,1)S(1)}, bf16[512,128]{1,0:T(8,128)(2,1)S(1)}, u32[]{:S(2)}, u32[]{:S(2)}) collective-permute-start(bf16[512,128]{1,0:T(8,128)(2,1)S(1)} %copy-done.2), channel_id=1, source_target_pairs={{0,64},{16,80},{32,96},{48,112},{64,0},{80,16},{96,32},{112,48},{1... | collective-permute-start | bytes 393224 | tf_op jit(solution)/shard_map/ppermute | solution.py:343
  18.9 8.9 %collective-permute-start = (bf16[512,128]{1,0:T(8,128)(2,1)S(1)}, bf16[512,128]{1,0:T(8,128)(2,1)S(1)}, u32[]{:S(2)}, u32[]{:S(2)}) collective-permute-start(bf16[512,128]{1,0:T(8,128)(2,1)S(1)} %copy-done.2), channel_id=1, source_target_pairs={{0,32},{16,48},{32,64},{48,80},{64,96},{80,112},{96,0},{112,16},{1... | collective-permute-start | bytes 393224 | tf_op jit(solution)/shard_map/ppermute | solution.py:343
  19.6 9.2 %collective-permute-start.3 = (bf16[512,128]{1,0:T(8,128)(2,1)S(1)}, bf16[512,128]{1,0:T(8,128)(2,1)S(1)}, u32[]{:S(2)}, u32[]{:S(2)}) collective-permute-start(bf16[512,128]{1,0:T(8,128)(2,1)S(1)} %copy-done.2), channel_id=1, source_target_pairs={{0,16},{16,0},{32,48},{48,32},{64,80},{80,64},{96,112},{112,96},{1... | collective-permute-start | bytes 393224 | tf_op jit(solution)/shard_map/ppermute | solution.py:346
  23.4 5.4 %collective-permute-start.6 = (bf16[512,128]{1,0:T(8,128)(2,1)S(1)}, bf16[512,128]{1,0:T(8,128)(2,1)S(1)}, u32[]{:S(2)}, u32[]{:S(2)}) collective-permute-start(bf16[512,128]{1,0:T(8,128)(2,1)S(1)} %collective-permute-done.2.refs_3_), channel_id=1, source_target_pairs={{0,16},{16,0},{32,48},{48,32},{64,80},{80,64},{96,112},{112,96},{1... | collective-permute-start | bytes 393224 | tf_op jit(solution)/shard_map/ppermute | solution.py:346
  25.1 3.7 %collective-permute-start.5 = (bf16[512,128]{1,0:T(8,128)(2,1)S(1)}, bf16[512,128]{1,0:T(8,128)(2,1)S(1)}, u32[]{:S(2)}, u32[]{:S(2)}) collective-permute-start(bf16[512,128]{1,0:T(8,128)(2,1)S(1)} %collective-permute-done.1.refs_2_), channel_id=1, source_target_pairs={{0,16},{16,0},{32,48},{48,32},{64,80},{80,64},{96,112},{112,96},{1... | collective-permute-start | bytes 393224 | tf_op jit(solution)/shard_map/ppermute | solution.py:346
  27.9 1.9 %collective-permute-start.4 = (bf16[512,128]{1,0:T(8,128)(2,1)S(1)}, bf16[512,128]{1,0:T(8,128)(2,1)S(1)}, u32[]{:S(2)}, u32[]{:S(2)}) collective-permute-start(bf16[512,128]{1,0:T(8,128)(2,1)S(1)} %collective-permute-done.refs_1_), channel_id=1, source_target_pairs={{0,16},{16,0},{32,48},{48,32},{64,80},{80,64},{96,112},{112,96},{1... | collective-permute-start | bytes 393224 | tf_op jit(solution)/shard_map/ppermute | solution.py:346
  32.6 1.3 %copy-start.3 = (bf16[4096,256]{1,0:T(8,128)(2,1)}, bf16[4096,256]{1,0:T(8,128)(2,1)S(1)}, u32[]{:S(2)}) copy-start(bf16[4096,256]{1,0:T(8,128)(2,1)S(1)} %get-tuple-element.23.zc) | copy-start | bytes 6291460
  33.9 1.1 copy-start.5
  35.0 1.6 %copy-start.4 = (bf16[4096,256]{1,0:T(8,128)(2,1)S(1)}, bf16[4096,256]{1,0:T(8,128)(2,1)}, u32[]{:S(2)}) copy-start(bf16[4096,256]{1,0:T(8,128)(2,1)} %copy-done.3) | copy-start | bytes 6291460
  36.6 1.3 %copy-start.6 = (bf16[160,4096]{1,0:T(8,128)(2,1)S(1)}, bf16[160,4096]{1,0:T(8,128)(2,1)}, u32[]{:S(2)}) copy-start(bf16[160,4096]{1,0:T(8,128)(2,1)} %copy-done.5) | copy-start | bytes 3932164

commit v4 on v2

v4 whole, which is shorter than its diff:
```python
import functools
import math

import jax
import jax.numpy as jnp
from jax import lax
from jax.experimental import pallas as pl
from jax.experimental.pallas import tpu as pltpu
from jax.sharding import PartitionSpec as P

F32 = jnp.float32
BF16 = jnp.bfloat16
VMEM = pl.BlockSpec(memory_space=pltpu.VMEM)
SMEM = pl.BlockSpec(memory_space=pltpu.SMEM)
PARAMS = pltpu.CompilerParams(vmem_limit_bytes=16 * 1024 * 1024)
ALONE = pltpu.CompilerParams(vmem_limit_bytes=60 * 1024 * 1024)
LARGE = pltpu.CompilerParams(vmem_limit_bytes=44 * 1024 * 1024)
V0, T0, N0, ONE, P0, S0 = 64, 96, 97, 100, 103, 112
LOG2E = math.log2(math.e)


def iota(shape, dim):
    return lax.broadcasted_iota(jnp.int32, shape, dim)


def split3(x):
    hi = x.astype(BF16)
    rest = x - hi.astype(F32)
    mid = rest.astype(BF16)
    low = (rest - mid.astype(F32)).astype(BF16)
    return hi, mid, low


def look_up(table, task):
    hit = (iota((table.shape[1], task.shape[1]), 0) == task).astype(BF16)
    tab = jnp.concatenate(split3(table), axis=0)
    got = jnp.dot(tab, hit, preferred_element_type=F32)
    return got[0:8] + got[8:16] + got[16:24]


def order_of(tid, cnt, rank):
    rows, ntask = tid.shape[1], cnt.shape[1]
    counts = cnt[...].astype(F32)
    before = iota((ntask, ntask), 1) < iota((ntask, ntask), 0)
    start = jnp.sum(jnp.where(before, counts, 0.0), axis=1, keepdims=True)
    hit = iota((ntask, rows), 0) == tid[...]
    pos = jnp.sum(jnp.where(hit, start, 0.0), axis=0, keepdims=True) + rank[...].astype(F32)
    pos_col = jnp.concatenate([pos, jnp.zeros((7, rows), F32)], axis=0).T[:, 0:1]
    return pos, jnp.sum((pos_col < pos).astype(F32), axis=0, keepdims=True)


def pack_kernel(
    feat, tid, cnt, rank, probes, net_w, net_b, scale, mix, diag, noise_in,
    cols, rows_out, vq_out, nv_out, pos_out, table_out,
):
    rows = feat.shape[1]
    width = probes.shape[0]
    pos, order = order_of(tid, cnt, rank)
    task = tid[...]
    table = jnp.concatenate(
        [mix[...], diag[...], noise_in[...], jnp.zeros((2, mix.shape[1]), F32)], axis=0
    )
    table_out[...] = table
    column = jnp.concatenate([net_b[...], scale[...], jnp.zeros((6, 64), F32)], axis=0).T
    hidden = jnp.tanh(
        lax.dot_general(
            net_w[...], feat[...], (((0,), (0,)), ((), ())), preferred_element_type=F32
        )
        + column[:, 0:1]
    )
    latent = (hidden * column[:, 1:2]).astype(BF16)
    lat = latent.astype(F32)
    norm = jnp.sum(lat * lat, axis=0, keepdims=True) * (-0.5 * LOG2E)
    local = pos - jnp.floor(pos * (1.0 / rows)) * rows
    high = jnp.floor(local * (1.0 / 16.0))
    noise = look_up(table, task)[5:6]
    extra = jnp.concatenate(
        [task.astype(F32)]
        + [a.astype(F32) for a in split3(norm)]
        + [jnp.ones((3, rows), F32), high, local - 16.0 * high, jnp.zeros((7, rows), F32)]
        + [a.astype(F32) for a in split3(noise)]
        + [jnp.zeros((13, rows), F32)],
        axis=0,
    ).astype(BF16)
    whole = jnp.concatenate([latent, probes[...], extra], axis=0)
    tile = jnp.floor(order * (1.0 / 64.0))
    inner = order - tile * 64.0
    block = jnp.floor(inner * 0.25)
    order_r = tile * 64.0 + (inner - block * 4.0) * 16.0 + block
    square = iota((rows, rows), 0)
    place_c = (square == order.astype(jnp.int32)).astype(BF16)
    place_r = (square == order_r.astype(jnp.int32)).astype(BF16)
    turn = (((1,), (1,)), ((), ()))
    data = lax.dot_general(place_c, whole, turn, preferred_element_type=F32).astype(BF16)
    for k in range(cols.shape[0]):
        cols[k] = data
    data = lax.dot_general(place_r, whole, turn, preferred_element_type=F32)
    half = rows // 2
    rows_out[:half, :] = jnp.concatenate([data[:half, :V0], data[half:, :V0]], axis=1).astype(BF16)
    at = (iota((16, rows), 1) % 16 == iota((16, rows), 0)).astype(BF16)
    group = jnp.where(iota((rows, 128), 0) // 16 == iota((rows, 128), 1), data[:, T0 : T0 + 1], 0.0)
    rows_out[half:, :] = jnp.dot(
        at, group.astype(BF16), preferred_element_type=F32
    ).astype(BF16)
    place = data[:, P0 : P0 + 1] * 16.0 + data[:, P0 + 1 : P0 + 2]
    noise_c = data[:, S0 : S0 + 1] + data[:, S0 + 1 : S0 + 2] + data[:, S0 + 2 : S0 + 3]
    v = data[:, V0:T0]
    nv = noise_c * v

    def fold(x, m):
        return jnp.concatenate(
            [x[t * 64 + m * 16 : t * 64 + m * 16 + 16] for t in range(rows // 64)], axis=0
        )

    vq_out[...] = jnp.concatenate([fold(v, m) for m in range(4)], axis=1)
    nv_out[...] = jnp.concatenate([fold(nv, m) for m in range(4)], axis=1)
    lane = iota((rows // 4, 128), 1)
    posq = jnp.zeros((rows // 4, 128), F32)
    for m in range(4):
        posq = jnp.where(lane == 3 * width + m, fold(place, m), posq)
    pos_out[...] = posq


def prepare_cols(table, cols, zc, st):
    chunks, rows, _ = cols.shape
    size = 4 * 16 * chunks
    width = T0 - V0
    for k in range(rows // 64):
        data = jnp.concatenate(
            [cols[h, g * 16 : g * 16 + 16, :] for g in range(4 * k, 4 * k + 4) for h in range(chunks)],
            axis=0,
        )
        span = slice(k * size, (k + 1) * size)
        wide = data.astype(F32)
        zc[span, 128:] = data
        zc[span, :128] = jnp.where(iota((size, 128), 1) < V0, wide, pltpu.roll(wide, V0, 1)).astype(BF16)
        turned = wide.T
        weight = look_up(table, turned[T0 : T0 + 1].astype(jnp.int32))
        values = turned[V0:T0]
        for q in range(4):
            st[q * width : (q + 1) * width, span] = (weight[q : q + 1] * values).astype(BF16)
        st[4 * width :, span] = values.astype(BF16)


def product_kernel(tile, chunks, table, cols, *refs):
    row_refs = refs[:chunks]
    near, far, kern_ref, task_ref, zc, st = refs[chunks:]
    i = pl.program_id(0)
    steps = pl.num_programs(0)
    tab = table[...]
    half = row_refs[0].shape[0] - 16

    @pl.when(i == 0)
    def _():
        every = jnp.concatenate([r[half:, :] for r in row_refs], axis=0).astype(F32).T
        for k in range(task_ref.shape[0]):
            task_ref[k] = every[8 * k : 8 * k + 8]
        prepare_cols(tab, cols, zc, st)

    first = pl.multiple_of(lax.rem(i, steps // 2) * 128, 128)
    blocks = [r[pl.ds(first, 128), :] for r in row_refs]
    data = jnp.concatenate(
        [b[g * 16 : g * 16 + 16, :] for g in range(8) for b in blocks], axis=0
    )
    rows = data.shape[0]
    turned = data.astype(F32).T
    z = jnp.where(i < steps // 2, turned[:V0], turned[V0:])
    norm = jnp.sum(z * z, axis=0, keepdims=True) * (-0.5 * LOG2E)
    parts = [a.astype(F32) for a in split3(norm)]
    sub = iota((T0 - V0, rows), 0)
    extra = jnp.where(jnp.logical_and(sub >= N0 - T0, sub < ONE - T0), 1.0, 0.0)
    for k in range(3):
        extra = jnp.where(sub == ONE - T0 + k, parts[k], extra)
    z = jnp.concatenate(
        split3(z * LOG2E) + (jnp.zeros((T0 - V0, rows), BF16), extra.astype(BF16)), axis=0
    )
    eight = task_ref[i]
    task = jnp.concatenate([eight[m : m + 1] for m in range(8)], axis=1)
    weight = look_up(tab, task.astype(jnp.int32))
    width = st.shape[0] // 5
    total = None
    for j in range(zc.shape[0] // tile):
        span = slice(j * tile, (j + 1) * tile)
        x = jnp.dot(zc[span, :], z, preferred_element_type=F32)
        kern = jnp.minimum(jnp.exp2(x).astype(BF16), jnp.asarray(1.0, BF16))
        kern_ref[span, :] = kern
        part = jnp.dot(st[: 4 * width, span], kern, preferred_element_type=F32)
        total = part if total is None else total + part
    low = weight[0:1] * total[:width]
    for q in range(1, 4):
        low = low + weight[q : q + 1] * total[q * width : (q + 1) * width]
    size = zc.shape[0] // 32
    count = rows // 2
    for k in range(2):
        lanes = slice(k * count, (k + 1) * count)
        start = pl.multiple_of(jnp.clip(4 * (2 * i + k) - 1, 0, 26) * size, size)
        band = pl.ds(start, 6 * size)
        same = zc[band, 128 + T0 : 129 + T0] == task[:, lanes].astype(BF16)
        kept = jnp.where(same, kern_ref[band, lanes], jnp.asarray(0.0, BF16))
        diag = jnp.dot(st[4 * width :, band], kept, preferred_element_type=F32)
        summed = low[:, lanes] + weight[4:5, lanes] * diag
        quarter = count // 4
        folded = jnp.concatenate(
            [summed[:, m * quarter : (m + 1) * quarter] for m in range(4)], axis=0
        ).T.reshape(chunks, 16, 128)
        near[:, k * 16 : k * 16 + 16, :] = folded[: chunks // 2]
        far[:, k * 16 : k * 16 + 16, :] = folded[chunks // 2 :]


def product_call(table, cols, row_parts):
    chunks = len(row_parts)
    total = cols.shape[0] * cols.shape[1]
    rows = cols.shape[1]
    steps = 4
    tile_rows = chunks * 128
    out = pl.BlockSpec((chunks // 2, 32, 128), lambda i: (0, i, 0))
    return pl.pallas_call(
        functools.partial(product_kernel, 2048, chunks),
        grid=(steps,),
        in_specs=[VMEM] * (2 + chunks),
        out_specs=[out, out],
        out_shape=[jax.ShapeDtypeStruct((chunks // 2, rows // 4, 128), F32)] * 2,
        scratch_shapes=[
            pltpu.VMEM((total, tile_rows), BF16),
            pltpu.VMEM((steps, 8, chunks * 16), F32),
            pltpu.VMEM((total, 256), BF16),
            pltpu.VMEM((5 * (T0 - V0), total), BF16),
        ],
        compiler_params=LARGE,
        cost_estimate=pl.CostEstimate(
            flops=2 * steps * tile_rows * total * 512, bytes_accessed=4 << 20, transcendentals=0
        ),
        name="product",
    )(table, cols, *row_parts)


def add_kernel(near, got, *out):
    for k, ref in enumerate(out):
        ref[...] = near[k] + got[k]


def image_kernel(nv, vq, pos, *refs):
    parts, send = refs[:-1], refs[-1]
    img = nv[...]
    for ref in parts:
        img = img + ref[...]
    v = vq[...]

    def over(x):
        s = jnp.sum(x, axis=0, keepdims=True)
        return s[:, 0:32] + s[:, 32:64] + s[:, 64:96] + s[:, 96:128]

    vv, vi = over(v * v), over(v * img)
    ratio = jnp.where(vv > 0.0, vi / jnp.where(vv > 0.0, vv, 1.0), 0.0)
    rest = img - jnp.concatenate([ratio] * 4, axis=1) * v
    row = jnp.concatenate([vv, vi, over(rest * rest), jnp.zeros_like(vv)], axis=1)
    send[:, 0, :] = img
    send[:, 1, :] = v
    send[:, 2, :] = pos[...] + row


def final_kernel(got, residual, direction, alpha_out, beta_out):
    n = got.shape[0]
    rows = residual.shape[1]
    img, v, every = got[:, 0, :], got[:, 1, :], got[:, 2, :]
    vv, vi, rr = every[:, 0:32], every[:, 32:64], every[:, 64:96]
    total_v = jnp.sum(vv, axis=0, keepdims=True)
    total_i = jnp.sum(vi, axis=0, keepdims=True)
    center = total_i / total_v
    ratio = jnp.where(vv > 0.0, vi / jnp.where(vv > 0.0, vv, 1.0), 0.0)
    shift = ratio - center
    total_r = jnp.sum(rr + vv * (shift * shift), axis=0, keepdims=True)
    alpha = total_v / total_i
    beta = alpha * alpha * total_r / total_v
    alpha_out[...] = alpha
    beta_out[...] = beta
    res = v - jnp.concatenate([alpha] * 4, axis=1) * img
    pieces = split3(res) + (v.astype(BF16),)
    total = None
    for m in range(4):
        lanes = slice(m * 32, (m + 1) * 32)
        values = jnp.concatenate([p[:, lanes] for p in pieces], axis=1)
        place = every[:, 96 + m : 97 + m].astype(jnp.int32)
        onehot = (iota((n, rows), 1) == place).astype(BF16)
        part = lax.dot_general(
            values, onehot, (((0,), (0,)), ((), ())), preferred_element_type=F32
        )
        total = part if total is None else total + part
    res_t = total[0:32] + total[32:64] + total[64:96]
    residual[...] = res_t
    beta_col = jnp.concatenate([beta, jnp.zeros((7, 32), F32)], axis=0).T[:, 0:1]
    direction[...] = res_t + beta_col * total[96:128]


def body(
    features,
    task_id,
    task_count,
    task_rank,
    probes,
    net_w,
    net_b,
    inv_scale,
    task_mix,
    task_diag,
    task_noise,
):
    rows = features.shape[0]
    n_row, n_col = lax.axis_size("row"), lax.axis_size("col")
    devices = n_row * n_col
    axes = ("row", "col")
    width = probes.shape[1]
    quarter = rows // 4
    n_y, n_x, n_z = n_row // 2, n_col // 4, 4
    shape = jax.ShapeDtypeStruct((quarter, 128), F32)
    cols, share, vq, nv, pos, table = pl.pallas_call(
        pack_kernel,
        in_specs=[VMEM] * 11,
        out_specs=[VMEM] * 6,
        out_shape=[
            jax.ShapeDtypeStruct((n_y * n_z, rows, 128), BF16),
            jax.ShapeDtypeStruct((rows // 2 + 16, 128), BF16),
            shape,
            shape,
            shape,
            jax.ShapeDtypeStruct((8, task_count.shape[0]), F32),
        ],
        compiler_params=ALONE,
        name="pack",
    )(
        features.T,
        task_id.reshape(1, -1),
        task_count.reshape(1, -1),
        task_rank.reshape(1, -1),
        probes.T,
        net_w,
        net_b.reshape(1, -1),
        inv_scale.reshape(1, -1),
        task_mix.T,
        task_diag.reshape(1, -1),
        task_noise.reshape(1, -1),
    )
    groups = [
        [(2 * y + c) * n_col + n_z * x + z for y in range(n_y) for z in range(n_z)]
        for c in range(2)
        for x in range(n_x)
    ]
    cols = lax.all_to_all(
        cols, axes, split_axis=0, concat_axis=0, tiled=True, axis_index_groups=groups
    )

    def along_x(value, k):
        return lax.ppermute(value, "col", [(i, (i + n_z * k) % n_col) for i in range(n_col)])

    def other_core(value):
        return lax.ppermute(value, "row", [(i, i ^ 1) for i in range(n_row)])

    own_core = [share] + [along_x(share, k) for k in range(1, n_x)]
    near, far = product_call(table, cols, own_core + [other_core(c) for c in own_core])
    sums = pl.pallas_call(
        add_kernel,
        in_specs=[VMEM] * 2,
        out_specs=[VMEM] * n_x,
        out_shape=[shape] * n_x,
        compiler_params=PARAMS,
        name="add",
    )(near, other_core(far))
    parts = [sums[0]] + [along_x(sums[k], -k) for k in range(1, n_x)]
    send = pl.pallas_call(
        image_kernel,
        in_specs=[VMEM] * (3 + n_x),
        out_specs=VMEM,
        out_shape=jax.ShapeDtypeStruct((devices, 3, 128), F32),
        compiler_params=PARAMS,
        name="image",
    )(nv, vq, pos, *parts)
    got = lax.all_to_all(send, ("row", "col"), split_axis=0, concat_axis=0, tiled=True)
    residual, direction, alpha, beta = pl.pallas_call(
        final_kernel,
        in_specs=[VMEM],
        out_specs=[VMEM] * 4,
        out_shape=[
            jax.ShapeDtypeStruct((width, rows), F32),
            jax.ShapeDtypeStruct((width, rows), F32),
            jax.ShapeDtypeStruct((1, width), F32),
            jax.ShapeDtypeStruct((1, width), F32),
        ],
        compiler_params=PARAMS,
        name="final",
    )(got)
    return residual.T, direction.T, alpha.reshape(width), beta.reshape(width)


def solution(mesh):
    axes = ("row", "col")
    return jax.shard_map(
        body,
        mesh=mesh,
        in_specs=(
            P(axes, None),
            P(axes),
            P(),
            P(axes),
            P(axes, None),
            P(),
            P(),
            P(),
            P(),
            P(),
            P(),
        ),
        out_specs=(P(axes, None), P(axes, None), P(), P()),
        check_vma=False,
    )
```

time: 115 us -> 106 us (0.922)
  blocking collectives: 36.7 us -> 15.9 us
  waiting for transfers between devices: 6.09 us -> 25.1 us
  local copies, waits for them, and re-layouts: 8.12 us -> 0.02 us
  starting transfers between devices: 19.3 us -> 24.6 us
  Pallas kernels: 42.4 us -> 39 us
    all_to_all x1, waiting for transfers between devices: 0.01 us -> 16.6 us  [body(): lax.all_to_all(cols, axes, split_axis=0, concat_axis=0, tiled=True, axis_...]
    all_to_all x1 -> x0, blocking collectives: 15.7 us -> none  [body(): lax.all_to_all(parts, 'col', split_axis=0, concat_axis=0, tiled=True)]
    unnamed x20 -> x10, local copies, waits for them, and re-layouts: 8.05 us -> 0.02 us
    all_to_all x1, blocking collectives: 21 us -> 15.9 us  [body(): lax.all_to_all(send, ('row', 'col'), split_axis=0, concat_axis=0, tiled=T...]
    ppermute x7 -> x11, starting transfers between devices: 10.9 us -> 15.9 us  [the longest x5 8.54 us: other_core(): return lax.ppermute(value, 'row', [(i, i ^ 1) for i in range(n_row)])]
    pallas_call x4, Pallas kernels: 40.1 us -> 36.6 us  [the longest x1 32.8 us: product_call(): pl.pallas_call(functools.partial(product_kernel, 2048, chunks), grid=(ste...]
    ppermute x7 -> x11, waiting for transfers between devices: 6.09 us -> 8.47 us  [the longest x6 6.4 us: along_x(): lax.ppermute(value, 'col', [(i, (i + n_z * k) % n_col) for i in range(n_c...]
  transfers between devices with their start and end apart: 8 -> 12, of which waited for: 3 -> 8; matrix products, arithmetic and copies ran while one was open for 0% -> 0% of each run, Pallas kernels for 2% -> 0%
where the time goes in v4:
time: 106 us; the launch traced here: 105 us
  Pallas kernels  39 us (37%)
  waiting for transfers between devices  25.1 us (24%)
  starting transfers between devices  24.6 us (23%)
  blocking collectives  15.9 us (15%)
    pallas_call x1, Pallas kernels, product_call(): pl.pallas_call(functools.partial(product_kernel, 2048, chunks), grid=(ste...  32.8 us
    all_to_all x1, waiting for transfers between devices, body(): lax.all_to_all(cols, axes, split_axis=0, concat_axis=0, tiled=True, axis_...  16.6 us
    all_to_all x1, blocking collectives, body(): lax.all_to_all(send, ('row', 'col'), split_axis=0, concat_axis=0, tiled=T...  15.9 us
    all_to_all x1, starting transfers between devices, body(): lax.all_to_all(cols, axes, split_axis=0, concat_axis=0, tiled=True, axis_...  8.74 us
    ppermute x5, starting transfers between devices, other_core(): return lax.ppermute(value, 'row', [(i, i ^ 1) for i in range(n_row)])  8.54 us
    ppermute x6, starting transfers between devices, along_x(): lax.ppermute(value, 'col', [(i, (i + n_z * k) % n_col) for i in range(n_c...  7.35 us
    ppermute x6, waiting for transfers between devices, along_x(): lax.ppermute(value, 'col', [(i, (i + n_z * k) % n_col) for i in range(n_c...  6.4 us
    pallas_call x1, Pallas kernels, body(): pl.pallas_call(pack_kernel, in_specs=[VMEM] * 11, out_specs=[VMEM] * 6, o...  3.41 us
  transfers between devices with their start and end apart: 12, of which 8 were waited for; matrix products, arithmetic and copies ran while one was open for 0% of the time, Pallas kernels for 0%

profile of v4, /device:TPU:1, one launch (start us, length us, event | category | flops | bytes accessed | tf_op | source)
XLA Modules:
  0.0 105.3 jit_solution(14583257959855261127)
XLA Ops:
  0.6 3.4 %pack.1 = (bf16[16,512,128]{2,1,0:T(8,128)(2,1)}, bf16[272,128]{1,0:T(8,128)(2,1)}, f32[128,128]{1,0:T(8,128)}, f32[128,128]{1,0:T(8,128)}, f32[128,128]{1,0:T(8,128)}, /*index=5*/f32[8,256]{1,0:T(8,128)}) custom-call(bf16[64,512]{1,0:T(8,128)(2,1)} %bitcast.14, s32[1,512]{1,0:T(1,128)} %bitcast.17, s32[1,256]{1,0:T(1,128)} %bitcast.19, s32[1,512]{1,0:T(1,128)} %bitcast.18, ...), custom_call_target="tpu_custom_call" | custom-call | tf_op jit(solution)/shard_map/pack/pallas_call | solution.py:316
  4.0 0.0 copy-start.3
  4.0 0.0 copy-start.4
  4.1 8.7 %all-to-all-start = ((bf16[16,512,128]{2,1,0:T(8,128)(2,1)}), bf16[16,512,128]{2,1,0:T(8,128)(2,1)S(1)}, u32[]{:S(2)}, u32[]{:S(2)}) async-start(bf16[16,512,128]{2,1,0:T(8,128)(2,1)} %get-tuple-element.24), calls=%async_computation | async-start | bytes 4194304 | tf_op jit(solution)/shard_map/all_to_all | solution.py:348
  12.8 0.0 copy-done.3
  12.8 2.5 %collective-permute-start.2 = (bf16[272,128]{1,0:T(8,128)(2,1)S(1)}, bf16[272,128]{1,0:T(8,128)(2,1)S(1)}, u32[]{:S(2)}, u32[]{:S(2)}) collective-permute-start(bf16[272,128]{1,0:T(8,128)(2,1)S(1)} %copy-done.3), channel_id=1, source_target_pairs={{0,12},{1,13},{2,14},{3,15},{4,0},{5,1},{6,2},{7,3},{8,4},{9,5},{1... | collective-permute-start | bytes 208904 | tf_op jit(solution)/shard_map/ppermute | solution.py:353
  15.4 0.5 collective-permute-start.1
  15.9 0.6 collective-permute-start
  16.5 1.8 %collective-permute-start.3 = (bf16[272,128]{1,0:T(8,128)(2,1)S(1)}, bf16[272,128]{1,0:T(8,128)(2,1)S(1)}, u32[]{:S(2)}, u32[]{:S(2)}) collective-permute-start(bf16[272,128]{1,0:T(8,128)(2,1)S(1)} %copy-done.3), channel_id=1, source_target_pairs={{0,16},{16,0},{32,48},{48,32},{64,80},{80,64},{96,112},{112,96},{1... | collective-permute-start | bytes 208904 | tf_op jit(solution)/shard_map/ppermute | solution.py:356
  18.3 0.0 collective-permute-done.2.refs_3_
  18.3 0.4 collective-permute-start.6
  18.7 1.7 %collective-permute-done.1.refs_2_ = bf16[272,128]{1,0:T(8,128)(2,1)S(1)} collective-permute-done((bf16[272,128]{1,0:T(8,128)(2,1)S(1)}, bf16[272,128]{1,0:T(8,128)(2,1)S(1)}, u32[]{:S(2)}, u32[]{:S(2)}) %collective-permute-start.1) | collective-permute-done | bytes 69664 | tf_op jit(solution)/shard_map/ppermute | solution.py:353
  20.3 2.1 %collective-permute-start.5 = (bf16[272,128]{1,0:T(8,128)(2,1)S(1)}, bf16[272,128]{1,0:T(8,128)(2,1)S(1)}, u32[]{:S(2)}, u32[]{:S(2)}) collective-permute-start(bf16[272,128]{1,0:T(8,128)(2,1)S(1)} %collective-permute-done.1.refs_2_), channel_id=1, source_target_pairs={{0,16},{16,0},{32,48},{48,32},{64,80},{80,64},{96,112},{112,96},{1... | collective-permute-start | bytes 208904 | tf_op jit(solution)/shard_map/ppermute | solution.py:356
  22.4 0.0 collective-permute-done.refs_1_
  22.4 0.7 collective-permute-start.4
  23.2 0.0 collective-permute-done.3.refs_4_
  23.2 0.0 collective-permute-done.6.refs_7_
  23.2 0.2 collective-permute-done.5.refs_6_
  23.3 0.7 collective-permute-done.4.refs_5_
  24.1 16.6 %all-to-all-done.cols = bf16[16,512,128]{2,1,0:T(8,128)(2,1)S(1)} async-done(((bf16[16,512,128]{2,1,0:T(8,128)(2,1)}), bf16[16,512,128]{2,1,0:T(8,128)(2,1)S(1)}, u32[]{:S(2)}, u32[]{:S(2)}) %all-to-all-start) | async-done | bytes 2097184 | tf_op jit(solution)/shard_map/all_to_all | solution.py:348
  40.7 0.0 copy-done.4
  40.7 0.0 copy-start
  40.7 0.0 copy-start.1
  40.7 0.0 copy-start.2
  40.7 32.8 %product.1 = (f32[4,128,128]{2,1,0:T(8,128)S(1)}, f32[4,128,128]{2,1,0:T(8,128)S(1)}) custom-call(f32[8,256]{1,0:T(8,128)S(1)} %copy-done.4, bf16[16,512,128]{2,1,0:T(8,128)(2,1)S(1)} %all-to-all-done.cols, bf16[272,128]{1,0:T(8,128)(2,1)S(1)} %copy-done.3, bf16[272,128]{1,0:T(8,128)(2,1)S(1)} %collective-permute-done.refs_1_, ...), custom_call_target="tpu_custom_call" | custom-call | flops 34359738368 | bytes 4194304 | tf_op jit(solution)/shard_map/product/pallas_call | solution.py:217
  73.5 3.5 %collective-permute-start.7 = (f32[4,128,128]{2,1,0:T(8,128)S(1)}, f32[4,128,128]{2,1,0:T(8,128)S(1)}, u32[]{:S(2)}, u32[]{:S(2)}) collective-permute-start(f32[4,128,128]{2,1,0:T(8,128)S(1)} %get-tuple-element.27), channel_id=1, source_target_pairs={{0,16},{16,0},{32,48},{48,32},{64,80},{80,64},{96,112},{112,96},{1... | collective-permute-start | bytes 786440 | tf_op jit(solution)/shard_map/ppermute | solution.py:356
  77.0 1.2 %collective-permute-done.7.got = f32[4,128,128]{2,1,0:T(8,128)S(1)} collective-permute-done((f32[4,128,128]{2,1,0:T(8,128)S(1)}, f32[4,128,128]{2,1,0:T(8,128)S(1)}, u32[]{:S(2)}, u32[]{:S(2)}) %collective-permute-start.7) | collective-permute-done | bytes 262176 | tf_op jit(solution)/shard_map/ppermute | solution.py:356
  78.2 2.5 %collective-permute-start.8 = (f32[128,128]{1,0:T(8,128)S(1)}, f32[128,128]{1,0:T(8,128)S(1)}, u32[]{:S(2)}, u32[]{:S(2)}) collective-permute-start(f32[128,128]{1,0:T(8,128)S(1)} %get-tuple-element.29), channel_id=1, source_target_pairs={{0,12},{1,13},{2,14},{3,15},{4,0},{5,1},{6,2},{7,3},{8,4},{9,5},{1... | collective-permute-start | bytes 196616 | tf_op jit(solution)/shard_map/ppermute | solution.py:353
  80.7 0.5 collective-permute-start.9
  81.2 0.6 collective-permute-start.10
  81.9 0.2 collective-permute-done.8.refs_1_
  82.1 3.3 %collective-permute-done.9.refs_2_ = f32[128,128]{1,0:T(8,128)S(1)} collective-permute-done((f32[128,128]{1,0:T(8,128)S(1)}, f32[128,128]{1,0:T(8,128)S(1)}, u32[]{:S(2)}, u32[]{:S(2)}) %collective-permute-start.9) | collective-permute-done | bytes 65568 | tf_op jit(solution)/shard_map/ppermute | solution.py:353
  85.4 1.2 %collective-permute-done.10.refs_3_ = f32[128,128]{1,0:T(8,128)S(1)} collective-permute-done((f32[128,128]{1,0:T(8,128)S(1)}, f32[128,128]{1,0:T(8,128)S(1)}, u32[]{:S(2)}, u32[]{:S(2)}) %collective-permute-start.10) | collective-permute-done | bytes 65568 | tf_op jit(solution)/shard_map/ppermute | solution.py:353
  86.6 0.0 copy-done
  86.6 0.0 copy-done.1
  86.6 0.0 copy-done.2
  86.6 0.4 image.1
  87.1 15.9 %all_to_all.10.got = f32[128,3,128]{2,1,0:T(4,128)S(1)} all-to-all(f32[128,3,128]{2,1,0:T(4,128)S(1)} %image.1), channel_id=1, replica_groups=mesh['row'=8,'col'=16] {'row','col'}, dimensions={0} | all-to-all | bytes 393216 | tf_op jit(solution)/shard_map/all_to_all | solution.py:377
  102.9 2.3 %final.1 = (f32[32,512]{1,0:T(8,128)}, f32[32,512]{1,0:T(8,128)}, f32[1,32]{1,0:T(1,128)}, f32[1,32]{1,0:T(1,128)}) custom-call(f32[128,3,128]{2,1,0:T(4,128)S(1)} %all_to_all.10.got), custom_call_target="tpu_custom_call" | custom-call | tf_op jit(solution)/shard_map/final/pallas_call | solution.py:378
  (1 shorter events, 0.0 us)
Async XLA Ops:
  4.0 8.8 %copy-start.3 = (bf16[272,128]{1,0:T(8,128)(2,1)S(1)}, bf16[272,128]{1,0:T(8,128)(2,1)}, u32[]{:S(2)}) copy-start(bf16[272,128]{1,0:T(8,128)(2,1)} %get-tuple-element.25.refs_0_) | copy-start | bytes 208900
  4.0 36.6 %copy-start.4 = (f32[8,256]{1,0:T(8,128)S(1)}, f32[8,256]{1,0:T(8,128)}, u32[]{:S(2)}) copy-start(f32[8,256]{1,0:T(8,128)} %get-tuple-element.23.table) | copy-start | bytes 24580
  4.1 36.6 %all-to-all-start = ((bf16[16,512,128]{2,1,0:T(8,128)(2,1)}), bf16[16,512,128]{2,1,0:T(8,128)(2,1)S(1)}, u32[]{:S(2)}, u32[]{:S(2)}) async-start(bf16[16,512,128]{2,1,0:T(8,128)(2,1)} %get-tuple-element.24), calls=%async_computation | async-start | bytes 4194304 | tf_op jit(solution)/shard_map/all_to_all | solution.py:348
  12.8 5.5 %collective-permute-start.2 = (bf16[272,128]{1,0:T(8,128)(2,1)S(1)}, bf16[272,128]{1,0:T(8,128)(2,1)S(1)}, u32[]{:S(2)}, u32[]{:S(2)}) collective-permute-start(bf16[272,128]{1,0:T(8,128)(2,1)S(1)} %copy-done.3), channel_id=1, source_target_pairs={{0,12},{1,13},{2,14},{3,15},{4,0},{5,1},{6,2},{7,3},{8,4},{9,5},{1... | collective-permute-start | bytes 208904 | tf_op jit(solution)/shard_map/ppermute | solution.py:353
  15.4 5.0 %collective-permute-start.1 = (bf16[272,128]{1,0:T(8,128)(2,1)S(1)}, bf16[272,128]{1,0:T(8,128)(2,1)S(1)}, u32[]{:S(2)}, u32[]{:S(2)}) collective-permute-start(bf16[272,128]{1,0:T(8,128)(2,1)S(1)} %copy-done.3), channel_id=1, source_target_pairs={{0,8},{1,9},{2,10},{3,11},{4,12},{5,13},{6,14},{7,15},{8,0},{9,1},... | collective-permute-start | bytes 208904 | tf_op jit(solution)/shard_map/ppermute | solution.py:353
  15.9 6.6 %collective-permute-start = (bf16[272,128]{1,0:T(8,128)(2,1)S(1)}, bf16[272,128]{1,0:T(8,128)(2,1)S(1)}, u32[]{:S(2)}, u32[]{:S(2)}) collective-permute-start(bf16[272,128]{1,0:T(8,128)(2,1)S(1)} %copy-done.3), channel_id=1, source_target_pairs={{0,4},{1,5},{2,6},{3,7},{4,8},{5,9},{6,10},{7,11},{8,12},{9,13},{1... | collective-permute-start | bytes 208904 | tf_op jit(solution)/shard_map/ppermute | solution.py:353
  16.5 6.7 %collective-permute-start.3 = (bf16[272,128]{1,0:T(8,128)(2,1)S(1)}, bf16[272,128]{1,0:T(8,128)(2,1)S(1)}, u32[]{:S(2)}, u32[]{:S(2)}) collective-permute-start(bf16[272,128]{1,0:T(8,128)(2,1)S(1)} %copy-done.3), channel_id=1, source_target_pairs={{0,16},{16,0},{32,48},{48,32},{64,80},{80,64},{96,112},{112,96},{1... | collective-permute-start | bytes 208904 | tf_op jit(solution)/shard_map/ppermute | solution.py:356
  18.3 4.9 %collective-permute-start.6 = (bf16[272,128]{1,0:T(8,128)(2,1)S(1)}, bf16[272,128]{1,0:T(8,128)(2,1)S(1)}, u32[]{:S(2)}, u32[]{:S(2)}) collective-permute-start(bf16[272,128]{1,0:T(8,128)(2,1)S(1)} %collective-permute-done.2.refs_3_), channel_id=1, source_target_pairs={{0,16},{16,0},{32,48},{48,32},{64,80},{80,64},{96,112},{112,96},{1... | collective-permute-start | bytes 208904 | tf_op jit(solution)/shard_map/ppermute | solution.py:356
  20.3 3.0 %collective-permute-start.5 = (bf16[272,128]{1,0:T(8,128)(2,1)S(1)}, bf16[272,128]{1,0:T(8,128)(2,1)S(1)}, u32[]{:S(2)}, u32[]{:S(2)}) collective-permute-start(bf16[272,128]{1,0:T(8,128)(2,1)S(1)} %collective-permute-done.1.refs_2_), channel_id=1, source_target_pairs={{0,16},{16,0},{32,48},{48,32},{64,80},{80,64},{96,112},{112,96},{1... | collective-permute-start | bytes 208904 | tf_op jit(solution)/shard_map/ppermute | solution.py:356
  22.4 1.6 %collective-permute-start.4 = (bf16[272,128]{1,0:T(8,128)(2,1)S(1)}, bf16[272,128]{1,0:T(8,128)(2,1)S(1)}, u32[]{:S(2)}, u32[]{:S(2)}) collective-permute-start(bf16[272,128]{1,0:T(8,128)(2,1)S(1)} %collective-permute-done.refs_1_), channel_id=1, source_target_pairs={{0,16},{16,0},{32,48},{48,32},{64,80},{80,64},{96,112},{112,96},{1... | collective-permute-start | bytes 208904 | tf_op jit(solution)/shard_map/ppermute | solution.py:356
  40.7 45.9 %copy-start = (f32[128,128]{1,0:T(8,128)S(1)}, f32[128,128]{1,0:T(8,128)}, u32[]{:S(2)}) copy-start(f32[128,128]{1,0:T(8,128)} %get-tuple-element.21.vq) | copy-start | bytes 196612
  40.7 45.9 %copy-start.1 = (f32[128,128]{1,0:T(8,128)S(1)}, f32[128,128]{1,0:T(8,128)}, u32[]{:S(2)}) copy-start(f32[128,128]{1,0:T(8,128)} %get-tuple-element.20.nv) | copy-start | bytes 196612
  40.7 45.9 %copy-start.2 = (f32[128,128]{1,0:T(8,128)S(1)}, f32[128,128]{1,0:T(8,128)}, u32[]{:S(2)}) copy-start(f32[128,128]{1,0:T(8,128)} %get-tuple-element.22.pos) | copy-start | bytes 196612
  73.5 4.7 %collective-permute-start.7 = (f32[4,128,128]{2,1,0:T(8,128)S(1)}, f32[4,128,128]{2,1,0:T(8,128)S(1)}, u32[]{:S(2)}, u32[]{:S(2)}) collective-permute-start(f32[4,128,128]{2,1,0:T(8,128)S(1)} %get-tuple-element.27), channel_id=1, source_target_pairs={{0,16},{16,0},{32,48},{48,32},{64,80},{80,64},{96,112},{112,96},{1... | collective-permute-start | bytes 786440 | tf_op jit(solution)/shard_map/ppermute | solution.py:356
  78.2 3.9 %collective-permute-start.8 = (f32[128,128]{1,0:T(8,128)S(1)}, f32[128,128]{1,0:T(8,128)S(1)}, u32[]{:S(2)}, u32[]{:S(2)}) collective-permute-start(f32[128,128]{1,0:T(8,128)S(1)} %get-tuple-element.29), channel_id=1, source_target_pairs={{0,12},{1,13},{2,14},{3,15},{4,0},{5,1},{6,2},{7,3},{8,4},{9,5},{1... | collective-permute-start | bytes 196616 | tf_op jit(solution)/shard_map/ppermute | solution.py:353
  80.7 4.7 %collective-permute-start.9 = (f32[128,128]{1,0:T(8,128)S(1)}, f32[128,128]{1,0:T(8,128)S(1)}, u32[]{:S(2)}, u32[]{:S(2)}) collective-permute-start(f32[128,128]{1,0:T(8,128)S(1)} %get-tuple-element.30), channel_id=1, source_target_pairs={{0,8},{1,9},{2,10},{3,11},{4,12},{5,13},{6,14},{7,15},{8,0},{9,1},... | collective-permute-start | bytes 196616 | tf_op jit(solution)/shard_map/ppermute | solution.py:353
  81.2 5.4 %collective-permute-start.10 = (f32[128,128]{1,0:T(8,128)S(1)}, f32[128,128]{1,0:T(8,128)S(1)}, u32[]{:S(2)}, u32[]{:S(2)}) collective-permute-start(f32[128,128]{1,0:T(8,128)S(1)} %get-tuple-element.31), channel_id=1, source_target_pairs={{0,4},{1,5},{2,6},{3,7},{4,8},{5,9},{6,10},{7,11},{8,12},{9,13},{1... | collective-permute-start | bytes 196616 | tf_op jit(solution)/shard_map/ppermute | solution.py:353

commit v5 on v4

--- a/solution.py
+++ b/solution.py
@@ -14,7 +14,7 @@
 SMEM = pl.BlockSpec(memory_space=pltpu.SMEM)
 PARAMS = pltpu.CompilerParams(vmem_limit_bytes=16 * 1024 * 1024)
 ALONE = pltpu.CompilerParams(vmem_limit_bytes=60 * 1024 * 1024)
-LARGE = pltpu.CompilerParams(vmem_limit_bytes=44 * 1024 * 1024)
+LARGE = pltpu.CompilerParams(vmem_limit_bytes=36 * 1024 * 1024)
 V0, T0, N0, ONE, P0, S0 = 64, 96, 97, 100, 103, 112
 LOG2E = math.log2(math.e)
 
@@ -92,16 +92,16 @@
     place_r = (square == order_r.astype(jnp.int32)).astype(BF16)
     turn = (((1,), (1,)), ((), ()))
     data = lax.dot_general(place_c, whole, turn, preferred_element_type=F32).astype(BF16)
-    for k in range(cols.shape[0]):
-        cols[k] = data
+    cols[...] = data
     data = lax.dot_general(place_r, whole, turn, preferred_element_type=F32)
     half = rows // 2
-    rows_out[:half, :] = jnp.concatenate([data[:half, :V0], data[half:, :V0]], axis=1).astype(BF16)
+    pair = jnp.concatenate([data[:half, :V0], data[half:, :V0]], axis=1).astype(BF16)
     at = (iota((16, rows), 1) % 16 == iota((16, rows), 0)).astype(BF16)
     group = jnp.where(iota((rows, 128), 0) // 16 == iota((rows, 128), 1), data[:, T0 : T0 + 1], 0.0)
-    rows_out[half:, :] = jnp.dot(
-        at, group.astype(BF16), preferred_element_type=F32
-    ).astype(BF16)
+    tasks = jnp.dot(at, group.astype(BF16), preferred_element_type=F32).astype(BF16)
+    for k in range(rows_out.shape[0]):
+        rows_out[k, :half, :] = pair
+        rows_out[k, half:, :] = tasks
     place = data[:, P0 : P0 + 1] * 16.0 + data[:, P0 + 1 : P0 + 2]
     noise_c = data[:, S0 : S0 + 1] + data[:, S0 + 1 : S0 + 2] + data[:, S0 + 2 : S0 + 3]
     v = data[:, V0:T0]
@@ -122,12 +122,12 @@
 
 
 def prepare_cols(table, cols, zc, st):
-    chunks, rows, _ = cols.shape
-    size = 4 * 16 * chunks
+    rows = cols[0].shape[0]
+    size = 4 * 16 * len(cols)
     width = T0 - V0
     for k in range(rows // 64):
         data = jnp.concatenate(
-            [cols[h, g * 16 : g * 16 + 16, :] for g in range(4 * k, 4 * k + 4) for h in range(chunks)],
+            [c[g * 16 : g * 16 + 16, :] for g in range(4 * k, 4 * k + 4) for c in cols],
             axis=0,
         )
         span = slice(k * size, (k + 1) * size)
@@ -142,29 +142,30 @@
         st[4 * width :, span] = values.astype(BF16)
 
 
-def product_kernel(tile, chunks, table, cols, *refs):
-    row_refs = refs[:chunks]
-    near, far, kern_ref, task_ref, zc, st = refs[chunks:]
-    i = pl.program_id(0)
+def product_kernel(tile, own_col, table, gathered, *refs):
+    cols, (out, own, kern_ref, task_ref, zc, st, mine) = refs[:-7], refs[-7:]
+    t = pl.program_id(0)
     steps = pl.num_programs(0)
+    n_col = gathered.shape[0]
+    half = gathered.shape[1] - 16
+    wide = n_col * 16
+    rows = 4 * wide
     tab = table[...]
-    half = row_refs[0].shape[0] - 16
-
-    @pl.when(i == 0)
+
+    @pl.when(t == 0)
     def _():
-        every = jnp.concatenate([r[half:, :] for r in row_refs], axis=0).astype(F32).T
+        every = gathered[:, half:, :].reshape(wide, 128).astype(F32).T
         for k in range(task_ref.shape[0]):
-            task_ref[k] = every[8 * k : 8 * k + 8]
+            task_ref[k] = every[4 * k : 4 * k + 8]
         prepare_cols(tab, cols, zc, st)
 
-    first = pl.multiple_of(lax.rem(i, steps // 2) * 128, 128)
-    blocks = [r[pl.ds(first, 128), :] for r in row_refs]
+    first = pl.multiple_of(lax.rem(t, steps // 2) * 64, 64)
+    blocks = [gathered[k, pl.ds(first, 64), :] for k in range(n_col)]
     data = jnp.concatenate(
-        [b[g * 16 : g * 16 + 16, :] for g in range(8) for b in blocks], axis=0
-    )
-    rows = data.shape[0]
+        [b[m * 16 : m * 16 + 16, :] for m in range(4) for b in blocks], axis=0
+    )
     turned = data.astype(F32).T
-    z = jnp.where(i < steps // 2, turned[:V0], turned[V0:])
+    z = jnp.where(t < steps // 2, turned[:V0], turned[V0:])
     norm = jnp.sum(z * z, axis=0, keepdims=True) * (-0.5 * LOG2E)
     parts = [a.astype(F32) for a in split3(norm)]
     sub = iota((T0 - V0, rows), 0)
@@ -174,8 +175,8 @@
     z = jnp.concatenate(
         split3(z * LOG2E) + (jnp.zeros((T0 - V0, rows), BF16), extra.astype(BF16)), axis=0
     )
-    eight = task_ref[i]
-    task = jnp.concatenate([eight[m : m + 1] for m in range(8)], axis=1)
+    four = task_ref[t]
+    task = jnp.concatenate([four[m : m + 1] for m in range(4)], axis=1)
     weight = look_up(tab, task.astype(jnp.int32))
     width = st.shape[0] // 5
     total = None
@@ -186,64 +187,57 @@
         kern_ref[span, :] = kern
         part = jnp.dot(st[: 4 * width, span], kern, preferred_element_type=F32)
         total = part if total is None else total + part
-    low = weight[0:1] * total[:width]
-    for q in range(1, 4):
-        low = low + weight[q : q + 1] * total[q * width : (q + 1) * width]
     size = zc.shape[0] // 32
-    count = rows // 2
-    for k in range(2):
-        lanes = slice(k * count, (k + 1) * count)
-        start = pl.multiple_of(jnp.clip(4 * (2 * i + k) - 1, 0, 26) * size, size)
-        band = pl.ds(start, 6 * size)
-        same = zc[band, 128 + T0 : 129 + T0] == task[:, lanes].astype(BF16)
-        kept = jnp.where(same, kern_ref[band, lanes], jnp.asarray(0.0, BF16))
-        diag = jnp.dot(st[4 * width :, band], kept, preferred_element_type=F32)
-        summed = low[:, lanes] + weight[4:5, lanes] * diag
-        quarter = count // 4
-        folded = jnp.concatenate(
-            [summed[:, m * quarter : (m + 1) * quarter] for m in range(4)], axis=0
-        ).T.reshape(chunks, 16, 128)
-        near[:, k * 16 : k * 16 + 16, :] = folded[: chunks // 2]
-        far[:, k * 16 : k * 16 + 16, :] = folded[chunks // 2 :]
-
-
-def product_call(table, cols, row_parts):
-    chunks = len(row_parts)
-    total = cols.shape[0] * cols.shape[1]
-    rows = cols.shape[1]
-    steps = 4
-    tile_rows = chunks * 128
-    out = pl.BlockSpec((chunks // 2, 32, 128), lambda i: (0, i, 0))
+    band = pl.ds(pl.multiple_of(jnp.clip(4 * t - 1, 0, 26) * size, size), 6 * size)
+    same = zc[band, 128 + T0 : 129 + T0] == task.astype(BF16)
+    kept = jnp.where(same, kern_ref[band, :], jnp.asarray(0.0, BF16))
+    summed = weight[4:5] * jnp.dot(st[4 * width :, band], kept, preferred_element_type=F32)
+    for q in range(4):
+        summed = summed + weight[q : q + 1] * total[q * width : (q + 1) * width]
+    folded = jnp.concatenate(
+        [summed[:, m * wide : (m + 1) * wide] for m in range(4)], axis=0
+    ).T.reshape(n_col, 16, 128)
+    out[...] = folded.astype(out.dtype)
+    mine[...] = folded
+    own[...] = mine[own_col[0]]
+
+
+def product_call(col, table, gathered, cols):
+    n_col, packed, _ = gathered.shape
+    total = len(cols) * cols[0].shape[0]
+    tiles = (packed - 16) // 32
+    rows = n_col * 64
     return pl.pallas_call(
-        functools.partial(product_kernel, 2048, chunks),
-        grid=(steps,),
-        in_specs=[VMEM] * (2 + chunks),
-        out_specs=[out, out],
-        out_shape=[jax.ShapeDtypeStruct((chunks // 2, rows // 4, 128), F32)] * 2,
+        functools.partial(product_kernel, 2048),
+        grid=(tiles,),
+        in_specs=[SMEM] + [VMEM] * (2 + len(cols)),
+        out_specs=[
+            pl.BlockSpec((n_col, 16, 128), lambda i: (0, i, 0)),
+            pl.BlockSpec((16, 128), lambda i: (i, 0)),
+        ],
+        out_shape=[
+            jax.ShapeDtypeStruct((n_col, tiles * 16, 128), BF16),
+            jax.ShapeDtypeStruct((tiles * 16, 128), F32),
+        ],
         scratch_shapes=[
-            pltpu.VMEM((total, tile_rows), BF16),
-            pltpu.VMEM((steps, 8, chunks * 16), F32),
+            pltpu.VMEM((total, rows), BF16),
+            pltpu.VMEM((tiles, 8, n_col * 16), F32),
             pltpu.VMEM((total, 256), BF16),
             pltpu.VMEM((5 * (T0 - V0), total), BF16),
+            pltpu.VMEM((n_col, 16, 128), F32),
         ],
         compiler_params=LARGE,
         cost_estimate=pl.CostEstimate(
-            flops=2 * steps * tile_rows * total * 512, bytes_accessed=4 << 20, transcendentals=0
+            flops=2 * tiles * rows * total * 512, bytes_accessed=4 << 20, transcendentals=0
         ),
         name="product",
-    )(table, cols, *row_parts)
-
-
-def add_kernel(near, got, *out):
-    for k, ref in enumerate(out):
-        ref[...] = near[k] + got[k]
-
-
-def image_kernel(nv, vq, pos, *refs):
-    parts, send = refs[:-1], refs[-1]
-    img = nv[...]
-    for ref in parts:
-        img = img + ref[...]
+    )(col, table, gathered, *cols)
+
+
+def image_kernel(col, parts, own, vq, nv, pos, send):
+    img = own[...] + nv[...]
+    for k in range(parts.shape[0]):
+        img = img + jnp.where(k == col[0], 0.0, parts[k].astype(F32))
     v = vq[...]
 
     def over(x):
@@ -311,15 +305,15 @@
     axes = ("row", "col")
     width = probes.shape[1]
     quarter = rows // 4
-    n_y, n_x, n_z = n_row // 2, n_col // 4, 4
+    col = lax.axis_index("col").astype(jnp.int32).reshape(1)
     shape = jax.ShapeDtypeStruct((quarter, 128), F32)
     cols, share, vq, nv, pos, table = pl.pallas_call(
         pack_kernel,
         in_specs=[VMEM] * 11,
         out_specs=[VMEM] * 6,
         out_shape=[
-            jax.ShapeDtypeStruct((n_y * n_z, rows, 128), BF16),
-            jax.ShapeDtypeStruct((rows // 2 + 16, 128), BF16),
+            jax.ShapeDtypeStruct((rows, 128), BF16),
+            jax.ShapeDtypeStruct((n_col, rows // 2 + 16, 128), BF16),
             shape,
             shape,
             shape,
@@ -340,40 +334,22 @@
         task_diag.reshape(1, -1),
         task_noise.reshape(1, -1),
     )
-    groups = [
-        [(2 * y + c) * n_col + n_z * x + z for y in range(n_y) for z in range(n_z)]
-        for c in range(2)
-        for x in range(n_x)
+    gathered = lax.all_to_all(share, "col", split_axis=0, concat_axis=0, tiled=True)
+    chunks = [cols] + [
+        lax.ppermute(cols, "row", [(i, (i + 2 * k) % n_row) for i in range(n_row)])
+        for k in range(1, n_row // 2)
     ]
-    cols = lax.all_to_all(
-        cols, axes, split_axis=0, concat_axis=0, tiled=True, axis_index_groups=groups
-    )
-
-    def along_x(value, k):
-        return lax.ppermute(value, "col", [(i, (i + n_z * k) % n_col) for i in range(n_col)])
-
-    def other_core(value):
-        return lax.ppermute(value, "row", [(i, i ^ 1) for i in range(n_row)])
-
-    own_core = [share] + [along_x(share, k) for k in range(1, n_x)]
-    near, far = product_call(table, cols, own_core + [other_core(c) for c in own_core])
-    sums = pl.pallas_call(
-        add_kernel,
-        in_specs=[VMEM] * 2,
-        out_specs=[VMEM] * n_x,
-        out_shape=[shape] * n_x,
-        compiler_params=PARAMS,
-        name="add",
-    )(near, other_core(far))
-    parts = [sums[0]] + [along_x(sums[k], -k) for k in range(1, n_x)]
+    chunks = chunks + [lax.ppermute(c, "row", [(i, i ^ 1) for i in range(n_row)]) for c in chunks]
+    parts, own = product_call(col, table, gathered, chunks)
+    summed = lax.all_to_all(parts, "col", split_axis=0, concat_axis=0, tiled=True)
     send = pl.pallas_call(
         image_kernel,
-        in_specs=[VMEM] * (3 + n_x),
+        in_specs=[SMEM] + [VMEM] * 5,
         out_specs=VMEM,
         out_shape=jax.ShapeDtypeStruct((devices, 3, 128), F32),
         compiler_params=PARAMS,
         name="image",
-    )(nv, vq, pos, *parts)
+    )(col, summed, own, vq, nv, pos)
     got = lax.all_to_all(send, ("row", "col"), split_axis=0, concat_axis=0, tiled=True)
     residual, direction, alpha, beta = pl.pallas_call(
         final_kernel,

time: 106 us -> 97.2 us (0.917)
  waiting for transfers between devices: 25.1 us -> 5.43 us
  blocking collectives: 15.9 us -> 32.9 us
  starting transfers between devices: 24.6 us -> 19.2 us
    all_to_all x1, waiting for transfers between devices: 16.6 us -> 2.03 us  [body(): lax.all_to_all(share, 'col', split_axis=0, concat_axis=0, tiled=True)]
    all_to_all x0 -> x1, blocking collectives: none -> 13.7 us  [body(): lax.all_to_all(parts, 'col', split_axis=0, concat_axis=0, tiled=True)]
    ppermute x11 -> x7, starting transfers between devices: 15.9 us -> 10.6 us  [the longest x4 6.76 us: body(): lax.ppermute(c, 'row', [(i, i ^ 1) for i in range(n_row)])]
    ppermute x11 -> x7, waiting for transfers between devices: 8.47 us -> 3.41 us  [the longest x3 2.42 us: body(): lax.ppermute(cols, 'row', [(i, (i + 2 * k) % n_row) for i in range(n_row)])]
    all_to_all x1, blocking collectives: 15.9 us -> 19.2 us  [body(): lax.all_to_all(send, ('row', 'col'), split_axis=0, concat_axis=0, tiled=T...]
    pallas_call x3 -> x2, Pallas kernels: 33.2 us -> 33 us  [the longest x1 32.5 us: product_call(): pl.pallas_call(functools.partial(product_kernel, 2048), grid=(tiles,), in...]
  transfers between devices with their start and end apart: 12 -> 8, of which waited for: 8 -> 4; matrix products, arithmetic and copies ran while one was open for 0% -> 0% of each run, Pallas kernels for 0% -> 0%
where the time goes in v5:
time: 97.2 us; the launch traced here: 96.9 us
  Pallas kernels  38.7 us (40%)
  blocking collectives  32.9 us (34%)
  starting transfers between devices  19.2 us (20%)
  waiting for transfers between devices  5.43 us (6%)
    pallas_call x1, Pallas kernels, product_call(): pl.pallas_call(functools.partial(product_kernel, 2048), grid=(tiles,), in...  32.5 us
    all_to_all x1, blocking collectives, body(): lax.all_to_all(send, ('row', 'col'), split_axis=0, concat_axis=0, tiled=T...  19.2 us
    all_to_all x1, blocking collectives, body(): lax.all_to_all(parts, 'col', split_axis=0, concat_axis=0, tiled=True)  13.7 us
    all_to_all x1, starting transfers between devices, body(): lax.all_to_all(share, 'col', split_axis=0, concat_axis=0, tiled=True)  8.57 us
    ppermute x4, starting transfers between devices, body(): lax.ppermute(c, 'row', [(i, i ^ 1) for i in range(n_row)])  6.76 us
    ppermute x3, starting transfers between devices, body(): lax.ppermute(cols, 'row', [(i, (i + 2 * k) % n_row) for i in range(n_row)])  3.84 us
    pallas_call x1, Pallas kernels, body(): pl.pallas_call(pack_kernel, in_specs=[VMEM] * 11, out_specs=[VMEM] * 6, o...  3.38 us
    ppermute x3, waiting for transfers between devices, body(): lax.ppermute(cols, 'row', [(i, (i + 2 * k) % n_row) for i in range(n_row)])  2.42 us
  transfers between devices with their start and end apart: 8, of which 4 were waited for; matrix products, arithmetic and copies ran while one was open for 0% of the time, Pallas kernels for 0%

profile of v5, /device:TPU:1, one launch (start us, length us, event | category | flops | bytes accessed | tf_op | source)
XLA Modules:
  0.0 96.9 jit_solution(10781549010956535394)
XLA Ops:
  0.6 3.4 %pack.1 = (bf16[512,128]{1,0:T(8,128)(2,1)}, bf16[16,272,128]{2,1,0:T(8,128)(2,1)}, f32[128,128]{1,0:T(8,128)}, f32[128,128]{1,0:T(8,128)}, f32[128,128]{1,0:T(8,128)}, /*index=5*/f32[8,256]{1,0:T(8,128)}) custom-call(bf16[64,512]{1,0:T(8,128)(2,1)} %bitcast.15, s32[1,512]{1,0:T(1,128)} %bitcast.18, s32[1,256]{1,0:T(1,128)} %bitcast.20, s32[1,512]{1,0:T(1,128)} %bitcast.19, ...), custom_call_target="tpu_custom_call" | custom-call | tf_op jit(solution)/shard_map/pack/pallas_call | solution.py:310
  4.0 0.0 copy-start.3
  4.0 0.0 copy-start.4
  4.0 8.6 %all-to-all-start = ((bf16[16,272,128]{2,1,0:T(8,128)(2,1)}), bf16[16,272,128]{2,1,0:T(8,128)(2,1)S(1)}, u32[]{:S(2)}, u32[]{:S(2)}) async-start(bf16[16,272,128]{2,1,0:T(8,128)(2,1)} %get-tuple-element.17), calls=%async_computation | async-start | bytes 2228224 | tf_op jit(solution)/shard_map/all_to_all | solution.py:337
  12.6 0.0 copy-done.3
  12.6 2.8 %collective-permute-start.2 = (bf16[512,128]{1,0:T(8,128)(2,1)S(1)}, bf16[512,128]{1,0:T(8,128)(2,1)S(1)}, u32[]{:S(2)}, u32[]{:S(2)}) collective-permute-start(bf16[512,128]{1,0:T(8,128)(2,1)S(1)} %copy-done.3), channel_id=1, source_target_pairs={{0,96},{16,112},{32,0},{48,16},{64,32},{80,48},{96,64},{112,80},{1... | collective-permute-start | bytes 393224 | tf_op jit(solution)/shard_map/ppermute | solution.py:339
  15.4 0.3 collective-permute-start.1
  15.8 0.7 collective-permute-start
  16.5 1.8 %collective-permute-start.3 = (bf16[512,128]{1,0:T(8,128)(2,1)S(1)}, bf16[512,128]{1,0:T(8,128)(2,1)S(1)}, u32[]{:S(2)}, u32[]{:S(2)}) collective-permute-start(bf16[512,128]{1,0:T(8,128)(2,1)S(1)} %copy-done.3), channel_id=1, source_target_pairs={{0,16},{16,0},{32,48},{48,32},{64,80},{80,64},{96,112},{112,96},{1... | collective-permute-start | bytes 393224 | tf_op jit(solution)/shard_map/ppermute | solution.py:342
  18.3 2.0 %collective-permute-done.2.refs_3_ = bf16[512,128]{1,0:T(8,128)(2,1)S(1)} collective-permute-done((bf16[512,128]{1,0:T(8,128)(2,1)S(1)}, bf16[512,128]{1,0:T(8,128)(2,1)S(1)}, u32[]{:S(2)}, u32[]{:S(2)}) %collective-permute-start.2) | collective-permute-done | bytes 131104 | tf_op jit(solution)/shard_map/ppermute | solution.py:339
  20.3 1.7 %collective-permute-start.6 = (bf16[512,128]{1,0:T(8,128)(2,1)S(1)}, bf16[512,128]{1,0:T(8,128)(2,1)S(1)}, u32[]{:S(2)}, u32[]{:S(2)}) collective-permute-start(bf16[512,128]{1,0:T(8,128)(2,1)S(1)} %collective-permute-done.2.refs_3_), channel_id=1, source_target_pairs={{0,16},{16,0},{32,48},{48,32},{64,80},{80,64},{96,112},{112,96},{1... | collective-permute-start | bytes 393224 | tf_op jit(solution)/shard_map/ppermute | solution.py:342
  21.9 0.0 collective-permute-done.1.refs_2_
  21.9 2.3 %collective-permute-start.5 = (bf16[512,128]{1,0:T(8,128)(2,1)S(1)}, bf16[512,128]{1,0:T(8,128)(2,1)S(1)}, u32[]{:S(2)}, u32[]{:S(2)}) collective-permute-start(bf16[512,128]{1,0:T(8,128)(2,1)S(1)} %collective-permute-done.1.refs_2_), channel_id=1, source_target_pairs={{0,16},{16,0},{32,48},{48,32},{64,80},{80,64},{96,112},{112,96},{1... | collective-permute-start | bytes 393224 | tf_op jit(solution)/shard_map/ppermute | solution.py:342
  24.3 0.4 collective-permute-done.refs_1_
  24.7 1.0 collective-permute-start.4
  25.6 0.0 collective-permute-done.3.refs_4_
  25.6 0.0 collective-permute-done.6.refs_7_
  25.6 0.0 collective-permute-done.5.refs_6_
  25.7 1.0 %collective-permute-done.4.refs_5_ = bf16[512,128]{1,0:T(8,128)(2,1)S(1)} collective-permute-done((bf16[512,128]{1,0:T(8,128)(2,1)S(1)}, bf16[512,128]{1,0:T(8,128)(2,1)S(1)}, u32[]{:S(2)}, u32[]{:S(2)}) %collective-permute-start.4) | collective-permute-done | bytes 131104 | tf_op jit(solution)/shard_map/ppermute | solution.py:342
  26.6 2.0 %all-to-all-done.gathered = bf16[16,272,128]{2,1,0:T(8,128)(2,1)S(1)} async-done(((bf16[16,272,128]{2,1,0:T(8,128)(2,1)}), bf16[16,272,128]{2,1,0:T(8,128)(2,1)S(1)}, u32[]{:S(2)}, u32[]{:S(2)}) %all-to-all-start) | async-done | bytes 1114144 | tf_op jit(solution)/shard_map/all_to_all | solution.py:337
  28.7 0.0 copy-done.4
  28.7 0.0 copy-start
  28.7 0.0 copy-start.1
  28.7 0.0 copy-start.2
  28.7 32.5 %product.1 = (bf16[16,128,128]{2,1,0:T(8,128)(2,1)S(1)}, f32[128,128]{1,0:T(8,128)S(1)}) custom-call(s32[1]{0:T(128)} %bitcast.own_col.col, f32[8,256]{1,0:T(8,128)S(1)} %copy-done.4, bf16[16,272,128]{2,1,0:T(8,128)(2,1)S(1)} %all-to-all-done.gathered, bf16[512,128]{1,0:T(8,128)(2,1)S(1)} %copy-done.3, bf16[512,128]{1,0:T(8,128)(2,1)S(1)} %collective-permute-done.refs_1_, ...), custom_call_target="tpu_custom_call" | custom-call | flops 34359738368 | bytes 4194304 | tf_op jit(solution)/shard_map/product/pallas_call | solution.py:210
  61.2 13.7 %all_to_all.15.parts = bf16[16,128,128]{2,1,0:T(8,128)(2,1)S(1)} all-to-all(bf16[16,128,128]{2,1,0:T(8,128)(2,1)S(1)} %get-tuple-element.19), channel_id=1, replica_groups=mesh['row'=8,'col'=16] {'col'}, dimensions={0} | all-to-all | bytes 1048576 | tf_op jit(solution)/shard_map/all_to_all | solution.py:344
  74.9 0.0 copy-done
  74.9 0.0 copy-done.1
  74.9 0.0 copy-done.2
  74.9 0.5 image.1
  75.4 19.2 %all_to_all.16.got = f32[128,3,128]{2,1,0:T(4,128)S(1)} all-to-all(f32[128,3,128]{2,1,0:T(4,128)S(1)} %image.1), channel_id=1, replica_groups=mesh['row'=8,'col'=16] {'row','col'}, dimensions={0} | all-to-all | bytes 393216 | tf_op jit(solution)/shard_map/all_to_all | solution.py:353
  94.6 2.4 %final.1 = (f32[32,512]{1,0:T(8,128)}, f32[32,512]{1,0:T(8,128)}, f32[1,32]{1,0:T(1,128)}, f32[1,32]{1,0:T(1,128)}) custom-call(f32[128,3,128]{2,1,0:T(4,128)S(1)} %all_to_all.16.got), custom_call_target="tpu_custom_call" | custom-call | tf_op jit(solution)/shard_map/final/pallas_call | solution.py:354
Async XLA Ops:
  4.0 8.6 %copy-start.3 = (bf16[512,128]{1,0:T(8,128)(2,1)S(1)}, bf16[512,128]{1,0:T(8,128)(2,1)}, u32[]{:S(2)}) copy-start(bf16[512,128]{1,0:T(8,128)(2,1)} %get-tuple-element.18.refs_0_) | copy-start | bytes 393220
  4.0 24.6 %copy-start.4 = (f32[8,256]{1,0:T(8,128)S(1)}, f32[8,256]{1,0:T(8,128)}, u32[]{:S(2)}) copy-start(f32[8,256]{1,0:T(8,128)} %get-tuple-element.16.table) | copy-start | bytes 24580
  4.0 24.6 %all-to-all-start = ((bf16[16,272,128]{2,1,0:T(8,128)(2,1)}), bf16[16,272,128]{2,1,0:T(8,128)(2,1)S(1)}, u32[]{:S(2)}, u32[]{:S(2)}) async-start(bf16[16,272,128]{2,1,0:T(8,128)(2,1)} %get-tuple-element.17), calls=%async_computation | async-start | bytes 2228224 | tf_op jit(solution)/shard_map/all_to_all | solution.py:337
  12.6 7.7 %collective-permute-start.2 = (bf16[512,128]{1,0:T(8,128)(2,1)S(1)}, bf16[512,128]{1,0:T(8,128)(2,1)S(1)}, u32[]{:S(2)}, u32[]{:S(2)}) collective-permute-start(bf16[512,128]{1,0:T(8,128)(2,1)S(1)} %copy-done.3), channel_id=1, source_target_pairs={{0,96},{16,112},{32,0},{48,16},{64,32},{80,48},{96,64},{112,80},{1... | collective-permute-start | bytes 393224 | tf_op jit(solution)/shard_map/ppermute | solution.py:339
  15.4 6.5 %collective-permute-start.1 = (bf16[512,128]{1,0:T(8,128)(2,1)S(1)}, bf16[512,128]{1,0:T(8,128)(2,1)S(1)}, u32[]{:S(2)}, u32[]{:S(2)}) collective-permute-start(bf16[512,128]{1,0:T(8,128)(2,1)S(1)} %copy-done.3), channel_id=1, source_target_pairs={{0,64},{16,80},{32,96},{48,112},{64,0},{80,16},{96,32},{112,48},{1... | collective-permute-start | bytes 393224 | tf_op jit(solution)/shard_map/ppermute | solution.py:339
  15.8 8.9 %collective-permute-start = (bf16[512,128]{1,0:T(8,128)(2,1)S(1)}, bf16[512,128]{1,0:T(8,128)(2,1)S(1)}, u32[]{:S(2)}, u32[]{:S(2)}) collective-permute-start(bf16[512,128]{1,0:T(8,128)(2,1)S(1)} %copy-done.3), channel_id=1, source_target_pairs={{0,32},{16,48},{32,64},{48,80},{64,96},{80,112},{96,0},{112,16},{1... | collective-permute-start | bytes 393224 | tf_op jit(solution)/shard_map/ppermute | solution.py:339
  16.5 9.2 %collective-permute-start.3 = (bf16[512,128]{1,0:T(8,128)(2,1)S(1)}, bf16[512,128]{1,0:T(8,128)(2,1)S(1)}, u32[]{:S(2)}, u32[]{:S(2)}) collective-permute-start(bf16[512,128]{1,0:T(8,128)(2,1)S(1)} %copy-done.3), channel_id=1, source_target_pairs={{0,16},{16,0},{32,48},{48,32},{64,80},{80,64},{96,112},{112,96},{1... | collective-permute-start | bytes 393224 | tf_op jit(solution)/shard_map/ppermute | solution.py:342
  20.3 5.4 %collective-permute-start.6 = (bf16[512,128]{1,0:T(8,128)(2,1)S(1)}, bf16[512,128]{1,0:T(8,128)(2,1)S(1)}, u32[]{:S(2)}, u32[]{:S(2)}) collective-permute-start(bf16[512,128]{1,0:T(8,128)(2,1)S(1)} %collective-permute-done.2.refs_3_), channel_id=1, source_target_pairs={{0,16},{16,0},{32,48},{48,32},{64,80},{80,64},{96,112},{112,96},{1... | collective-permute-start | bytes 393224 | tf_op jit(solution)/shard_map/ppermute | solution.py:342
  21.9 3.7 %collective-permute-start.5 = (bf16[512,128]{1,0:T(8,128)(2,1)S(1)}, bf16[512,128]{1,0:T(8,128)(2,1)S(1)}, u32[]{:S(2)}, u32[]{:S(2)}) collective-permute-start(bf16[512,128]{1,0:T(8,128)(2,1)S(1)} %collective-permute-done.1.refs_2_), channel_id=1, source_target_pairs={{0,16},{16,0},{32,48},{48,32},{64,80},{80,64},{96,112},{112,96},{1... | collective-permute-start | bytes 393224 | tf_op jit(solution)/shard_map/ppermute | solution.py:342
  24.7 1.9 %collective-permute-start.4 = (bf16[512,128]{1,0:T(8,128)(2,1)S(1)}, bf16[512,128]{1,0:T(8,128)(2,1)S(1)}, u32[]{:S(2)}, u32[]{:S(2)}) collective-permute-start(bf16[512,128]{1,0:T(8,128)(2,1)S(1)} %collective-permute-done.refs_1_), channel_id=1, source_target_pairs={{0,16},{16,0},{32,48},{48,32},{64,80},{80,64},{96,112},{112,96},{1... | collective-permute-start | bytes 393224 | tf_op jit(solution)/shard_map/ppermute | solution.py:342
  28.7 46.2 %copy-start = (f32[128,128]{1,0:T(8,128)S(1)}, f32[128,128]{1,0:T(8,128)}, u32[]{:S(2)}) copy-start(f32[128,128]{1,0:T(8,128)} %get-tuple-element.21.vq) | copy-start | bytes 196612
  28.7 46.2 %copy-start.1 = (f32[128,128]{1,0:T(8,128)S(1)}, f32[128,128]{1,0:T(8,128)}, u32[]{:S(2)}) copy-start(f32[128,128]{1,0:T(8,128)} %get-tuple-element.22.nv) | copy-start | bytes 196612
  28.7 46.2 %copy-start.2 = (f32[128,128]{1,0:T(8,128)S(1)}, f32[128,128]{1,0:T(8,128)}, u32[]{:S(2)}) copy-start(f32[128,128]{1,0:T(8,128)} %get-tuple-element.23.pos) | copy-start | bytes 196612

commit v6 on v5

--- a/solution.py
+++ b/solution.py
@@ -256,34 +256,37 @@
 def final_kernel(got, residual, direction, alpha_out, beta_out):
     n = got.shape[0]
     rows = residual.shape[1]
-    img, v, every = got[:, 0, :], got[:, 1, :], got[:, 2, :]
-    vv, vi, rr = every[:, 0:32], every[:, 32:64], every[:, 64:96]
-    total_v = jnp.sum(vv, axis=0, keepdims=True)
-    total_i = jnp.sum(vi, axis=0, keepdims=True)
-    center = total_i / total_v
-    ratio = jnp.where(vv > 0.0, vi / jnp.where(vv > 0.0, vv, 1.0), 0.0)
-    shift = ratio - center
-    total_r = jnp.sum(rr + vv * (shift * shift), axis=0, keepdims=True)
-    alpha = total_v / total_i
-    beta = alpha * alpha * total_r / total_v
-    alpha_out[...] = alpha
-    beta_out[...] = beta
-    res = v - jnp.concatenate([alpha] * 4, axis=1) * img
+    every = got[:, 2, :]
+    turned = every.T
+
+    def over(axis, pick):
+        vv, vi, rr = (pick(k) for k in range(3))
+        total_v = jnp.sum(vv, axis=axis, keepdims=True)
+        total_i = jnp.sum(vi, axis=axis, keepdims=True)
+        ratio = jnp.where(vv > 0.0, vi / jnp.where(vv > 0.0, vv, 1.0), 0.0)
+        shift = ratio - total_i / total_v
+        total_r = jnp.sum(rr + vv * (shift * shift), axis=axis, keepdims=True)
+        alpha = total_v / total_i
+        return alpha, alpha * alpha * total_r / total_v
+
+    alpha, beta = over(1, lambda k: turned[32 * k : 32 * k + 32])
+    sums = jnp.concatenate([alpha, beta, jnp.zeros((32, 126), F32)], axis=1).T
+    alpha_out[...] = sums[0:1]
+    beta_out[...] = sums[1:2]
+    v = got[:, 1, :].T
+    res = v - jnp.concatenate([alpha] * 4, axis=0) * got[:, 0, :].T
     pieces = split3(res) + (v.astype(BF16),)
     total = None
     for m in range(4):
         lanes = slice(m * 32, (m + 1) * 32)
-        values = jnp.concatenate([p[:, lanes] for p in pieces], axis=1)
+        values = jnp.concatenate([p[lanes] for p in pieces], axis=0)
         place = every[:, 96 + m : 97 + m].astype(jnp.int32)
         onehot = (iota((n, rows), 1) == place).astype(BF16)
-        part = lax.dot_general(
-            values, onehot, (((0,), (0,)), ((), ())), preferred_element_type=F32
-        )
+        part = jnp.dot(values, onehot, preferred_element_type=F32)
         total = part if total is None else total + part
     res_t = total[0:32] + total[32:64] + total[64:96]
     residual[...] = res_t
-    beta_col = jnp.concatenate([beta, jnp.zeros((7, 32), F32)], axis=0).T[:, 0:1]
-    direction[...] = res_t + beta_col * total[96:128]
+    direction[...] = res_t + beta * total[96:128]
 
 
 def body(

time: 97.2 us -> 96.6 us (level)
  no operation moved by 1% of the time
where the time goes in v6:
time: 96.6 us; the launch traced here: 96.3 us
  Pallas kernels  38.1 us (39%)
  blocking collectives  32.9 us (34%)
  starting transfers between devices  19.2 us (20%)
  waiting for transfers between devices  5.43 us (6%)
    pallas_call x1, Pallas kernels, product_call(): pl.pallas_call(functools.partial(product_kernel, 2048), grid=(tiles,), in...  32.5 us
    all_to_all x1, blocking collectives, body(): lax.all_to_all(send, ('row', 'col'), split_axis=0, concat_axis=0, tiled=T...  19.2 us
    all_to_all x1, blocking collectives, body(): lax.all_to_all(parts, 'col', split_axis=0, concat_axis=0, tiled=True)  13.7 us
    all_to_all x1, starting transfers between devices, body(): lax.all_to_all(share, 'col', split_axis=0, concat_axis=0, tiled=True)  8.57 us
    ppermute x4, starting transfers between devices, body(): lax.ppermute(c, 'row', [(i, i ^ 1) for i in range(n_row)])  6.76 us
    ppermute x3, starting transfers between devices, body(): lax.ppermute(cols, 'row', [(i, (i + 2 * k) % n_row) for i in range(n_row)])  3.84 us
    pallas_call x1, Pallas kernels, body(): pl.pallas_call(pack_kernel, in_specs=[VMEM] * 11, out_specs=[VMEM] * 6, o...  3.38 us
    ppermute x3, waiting for transfers between devices, body(): lax.ppermute(cols, 'row', [(i, (i + 2 * k) % n_row) for i in range(n_row)])  2.42 us
  transfers between devices with their start and end apart: 8, of which 4 were waited for; matrix products, arithmetic and copies ran while one was open for 0% of the time, Pallas kernels for 0%

profile of v6, /device:TPU:1, one launch (start us, length us, event | category | flops | bytes accessed | tf_op | source)
XLA Modules:
  0.0 96.3 jit_solution(17663511853252907045)
XLA Ops:
  0.6 3.4 %pack.1 = (bf16[512,128]{1,0:T(8,128)(2,1)}, bf16[16,272,128]{2,1,0:T(8,128)(2,1)}, f32[128,128]{1,0:T(8,128)}, f32[128,128]{1,0:T(8,128)}, f32[128,128]{1,0:T(8,128)}, /*index=5*/f32[8,256]{1,0:T(8,128)}) custom-call(bf16[64,512]{1,0:T(8,128)(2,1)} %bitcast.15, s32[1,512]{1,0:T(1,128)} %bitcast.18, s32[1,256]{1,0:T(1,128)} %bitcast.20, s32[1,512]{1,0:T(1,128)} %bitcast.19, ...), custom_call_target="tpu_custom_call" | custom-call | tf_op jit(solution)/shard_map/pack/pallas_call | solution.py:313
  4.0 0.0 copy-start.3
  4.0 0.0 copy-start.4
  4.0 8.6 %all-to-all-start = ((bf16[16,272,128]{2,1,0:T(8,128)(2,1)}), bf16[16,272,128]{2,1,0:T(8,128)(2,1)S(1)}, u32[]{:S(2)}, u32[]{:S(2)}) async-start(bf16[16,272,128]{2,1,0:T(8,128)(2,1)} %get-tuple-element.17), calls=%async_computation | async-start | bytes 2228224 | tf_op jit(solution)/shard_map/all_to_all | solution.py:340
  12.6 0.0 copy-done.3
  12.6 2.8 %collective-permute-start.2 = (bf16[512,128]{1,0:T(8,128)(2,1)S(1)}, bf16[512,128]{1,0:T(8,128)(2,1)S(1)}, u32[]{:S(2)}, u32[]{:S(2)}) collective-permute-start(bf16[512,128]{1,0:T(8,128)(2,1)S(1)} %copy-done.3), channel_id=1, source_target_pairs={{0,96},{16,112},{32,0},{48,16},{64,32},{80,48},{96,64},{112,80},{1... | collective-permute-start | bytes 393224 | tf_op jit(solution)/shard_map/ppermute | solution.py:342
  15.4 0.3 collective-permute-start.1
  15.8 0.7 collective-permute-start
  16.5 1.8 %collective-permute-start.3 = (bf16[512,128]{1,0:T(8,128)(2,1)S(1)}, bf16[512,128]{1,0:T(8,128)(2,1)S(1)}, u32[]{:S(2)}, u32[]{:S(2)}) collective-permute-start(bf16[512,128]{1,0:T(8,128)(2,1)S(1)} %copy-done.3), channel_id=1, source_target_pairs={{0,16},{16,0},{32,48},{48,32},{64,80},{80,64},{96,112},{112,96},{1... | collective-permute-start | bytes 393224 | tf_op jit(solution)/shard_map/ppermute | solution.py:345
  18.3 2.0 %collective-permute-done.2.refs_3_ = bf16[512,128]{1,0:T(8,128)(2,1)S(1)} collective-permute-done((bf16[512,128]{1,0:T(8,128)(2,1)S(1)}, bf16[512,128]{1,0:T(8,128)(2,1)S(1)}, u32[]{:S(2)}, u32[]{:S(2)}) %collective-permute-start.2) | collective-permute-done | bytes 131104 | tf_op jit(solution)/shard_map/ppermute | solution.py:342
  20.3 1.7 %collective-permute-start.6 = (bf16[512,128]{1,0:T(8,128)(2,1)S(1)}, bf16[512,128]{1,0:T(8,128)(2,1)S(1)}, u32[]{:S(2)}, u32[]{:S(2)}) collective-permute-start(bf16[512,128]{1,0:T(8,128)(2,1)S(1)} %collective-permute-done.2.refs_3_), channel_id=1, source_target_pairs={{0,16},{16,0},{32,48},{48,32},{64,80},{80,64},{96,112},{112,96},{1... | collective-permute-start | bytes 393224 | tf_op jit(solution)/shard_map/ppermute | solution.py:345
  21.9 0.0 collective-permute-done.1.refs_2_
  21.9 2.3 %collective-permute-start.5 = (bf16[512,128]{1,0:T(8,128)(2,1)S(1)}, bf16[512,128]{1,0:T(8,128)(2,1)S(1)}, u32[]{:S(2)}, u32[]{:S(2)}) collective-permute-start(bf16[512,128]{1,0:T(8,128)(2,1)S(1)} %collective-permute-done.1.refs_2_), channel_id=1, source_target_pairs={{0,16},{16,0},{32,48},{48,32},{64,80},{80,64},{96,112},{112,96},{1... | collective-permute-start | bytes 393224 | tf_op jit(solution)/shard_map/ppermute | solution.py:345
  24.3 0.4 collective-permute-done.refs_1_
  24.7 1.0 collective-permute-start.4
  25.6 0.0 collective-permute-done.3.refs_4_
  25.6 0.0 collective-permute-done.6.refs_7_
  25.6 0.0 collective-permute-done.5.refs_6_
  25.7 1.0 %collective-permute-done.4.refs_5_ = bf16[512,128]{1,0:T(8,128)(2,1)S(1)} collective-permute-done((bf16[512,128]{1,0:T(8,128)(2,1)S(1)}, bf16[512,128]{1,0:T(8,128)(2,1)S(1)}, u32[]{:S(2)}, u32[]{:S(2)}) %collective-permute-start.4) | collective-permute-done | bytes 131104 | tf_op jit(solution)/shard_map/ppermute | solution.py:345
  26.6 2.0 %all-to-all-done.gathered = bf16[16,272,128]{2,1,0:T(8,128)(2,1)S(1)} async-done(((bf16[16,272,128]{2,1,0:T(8,128)(2,1)}), bf16[16,272,128]{2,1,0:T(8,128)(2,1)S(1)}, u32[]{:S(2)}, u32[]{:S(2)}) %all-to-all-start) | async-done | bytes 1114144 | tf_op jit(solution)/shard_map/all_to_all | solution.py:340
  28.7 0.0 copy-done.4
  28.7 0.0 copy-start
  28.7 0.0 copy-start.1
  28.7 0.0 copy-start.2
  28.7 32.5 %product.1 = (bf16[16,128,128]{2,1,0:T(8,128)(2,1)S(1)}, f32[128,128]{1,0:T(8,128)S(1)}) custom-call(s32[1]{0:T(128)} %bitcast.own_col.col, f32[8,256]{1,0:T(8,128)S(1)} %copy-done.4, bf16[16,272,128]{2,1,0:T(8,128)(2,1)S(1)} %all-to-all-done.gathered, bf16[512,128]{1,0:T(8,128)(2,1)S(1)} %copy-done.3, bf16[512,128]{1,0:T(8,128)(2,1)S(1)} %collective-permute-done.refs_1_, ...), custom_call_target="tpu_custom_call" | custom-call | flops 34359738368 | bytes 4194304 | tf_op jit(solution)/shard_map/product/pallas_call | solution.py:210
  61.2 13.7 %all_to_all.15.parts = bf16[16,128,128]{2,1,0:T(8,128)(2,1)S(1)} all-to-all(bf16[16,128,128]{2,1,0:T(8,128)(2,1)S(1)} %get-tuple-element.19), channel_id=1, replica_groups=mesh['row'=8,'col'=16] {'col'}, dimensions={0} | all-to-all | bytes 1048576 | tf_op jit(solution)/shard_map/all_to_all | solution.py:347
  74.9 0.0 copy-done
  74.9 0.0 copy-done.1
  74.9 0.0 copy-done.2
  74.9 0.5 image.1
  75.4 19.2 %all_to_all.16.got = f32[128,3,128]{2,1,0:T(4,128)S(1)} all-to-all(f32[128,3,128]{2,1,0:T(4,128)S(1)} %image.1), channel_id=1, replica_groups=mesh['row'=8,'col'=16] {'row','col'}, dimensions={0} | all-to-all | bytes 393216 | tf_op jit(solution)/shard_map/all_to_all | solution.py:356
  94.6 1.7 %final.1 = (f32[32,512]{1,0:T(8,128)}, f32[32,512]{1,0:T(8,128)}, f32[1,32]{1,0:T(1,128)}, f32[1,32]{1,0:T(1,128)}) custom-call(f32[128,3,128]{2,1,0:T(4,128)S(1)} %all_to_all.16.got), custom_call_target="tpu_custom_call" | custom-call | tf_op jit(solution)/shard_map/final/pallas_call | solution.py:357
Async XLA Ops:
  4.0 8.6 %copy-start.3 = (bf16[512,128]{1,0:T(8,128)(2,1)S(1)}, bf16[512,128]{1,0:T(8,128)(2,1)}, u32[]{:S(2)}) copy-start(bf16[512,128]{1,0:T(8,128)(2,1)} %get-tuple-element.18.refs_0_) | copy-start | bytes 393220
  4.0 24.6 %copy-start.4 = (f32[8,256]{1,0:T(8,128)S(1)}, f32[8,256]{1,0:T(8,128)}, u32[]{:S(2)}) copy-start(f32[8,256]{1,0:T(8,128)} %get-tuple-element.16.table) | copy-start | bytes 24580
  4.0 24.6 %all-to-all-start = ((bf16[16,272,128]{2,1,0:T(8,128)(2,1)}), bf16[16,272,128]{2,1,0:T(8,128)(2,1)S(1)}, u32[]{:S(2)}, u32[]{:S(2)}) async-start(bf16[16,272,128]{2,1,0:T(8,128)(2,1)} %get-tuple-element.17), calls=%async_computation | async-start | bytes 2228224 | tf_op jit(solution)/shard_map/all_to_all | solution.py:340
  12.6 7.7 %collective-permute-start.2 = (bf16[512,128]{1,0:T(8,128)(2,1)S(1)}, bf16[512,128]{1,0:T(8,128)(2,1)S(1)}, u32[]{:S(2)}, u32[]{:S(2)}) collective-permute-start(bf16[512,128]{1,0:T(8,128)(2,1)S(1)} %copy-done.3), channel_id=1, source_target_pairs={{0,96},{16,112},{32,0},{48,16},{64,32},{80,48},{96,64},{112,80},{1... | collective-permute-start | bytes 393224 | tf_op jit(solution)/shard_map/ppermute | solution.py:342
  15.4 6.5 %collective-permute-start.1 = (bf16[512,128]{1,0:T(8,128)(2,1)S(1)}, bf16[512,128]{1,0:T(8,128)(2,1)S(1)}, u32[]{:S(2)}, u32[]{:S(2)}) collective-permute-start(bf16[512,128]{1,0:T(8,128)(2,1)S(1)} %copy-done.3), channel_id=1, source_target_pairs={{0,64},{16,80},{32,96},{48,112},{64,0},{80,16},{96,32},{112,48},{1... | collective-permute-start | bytes 393224 | tf_op jit(solution)/shard_map/ppermute | solution.py:342
  15.8 8.9 %collective-permute-start = (bf16[512,128]{1,0:T(8,128)(2,1)S(1)}, bf16[512,128]{1,0:T(8,128)(2,1)S(1)}, u32[]{:S(2)}, u32[]{:S(2)}) collective-permute-start(bf16[512,128]{1,0:T(8,128)(2,1)S(1)} %copy-done.3), channel_id=1, source_target_pairs={{0,32},{16,48},{32,64},{48,80},{64,96},{80,112},{96,0},{112,16},{1... | collective-permute-start | bytes 393224 | tf_op jit(solution)/shard_map/ppermute | solution.py:342
  16.5 9.2 %collective-permute-start.3 = (bf16[512,128]{1,0:T(8,128)(2,1)S(1)}, bf16[512,128]{1,0:T(8,128)(2,1)S(1)}, u32[]{:S(2)}, u32[]{:S(2)}) collective-permute-start(bf16[512,128]{1,0:T(8,128)(2,1)S(1)} %copy-done.3), channel_id=1, source_target_pairs={{0,16},{16,0},{32,48},{48,32},{64,80},{80,64},{96,112},{112,96},{1... | collective-permute-start | bytes 393224 | tf_op jit(solution)/shard_map/ppermute | solution.py:345
  20.3 5.4 %collective-permute-start.6 = (bf16[512,128]{1,0:T(8,128)(2,1)S(1)}, bf16[512,128]{1,0:T(8,128)(2,1)S(1)}, u32[]{:S(2)}, u32[]{:S(2)}) collective-permute-start(bf16[512,128]{1,0:T(8,128)(2,1)S(1)} %collective-permute-done.2.refs_3_), channel_id=1, source_target_pairs={{0,16},{16,0},{32,48},{48,32},{64,80},{80,64},{96,112},{112,96},{1... | collective-permute-start | bytes 393224 | tf_op jit(solution)/shard_map/ppermute | solution.py:345
  21.9 3.7 %collective-permute-start.5 = (bf16[512,128]{1,0:T(8,128)(2,1)S(1)}, bf16[512,128]{1,0:T(8,128)(2,1)S(1)}, u32[]{:S(2)}, u32[]{:S(2)}) collective-permute-start(bf16[512,128]{1,0:T(8,128)(2,1)S(1)} %collective-permute-done.1.refs_2_), channel_id=1, source_target_pairs={{0,16},{16,0},{32,48},{48,32},{64,80},{80,64},{96,112},{112,96},{1... | collective-permute-start | bytes 393224 | tf_op jit(solution)/shard_map/ppermute | solution.py:345
  24.7 1.9 %collective-permute-start.4 = (bf16[512,128]{1,0:T(8,128)(2,1)S(1)}, bf16[512,128]{1,0:T(8,128)(2,1)S(1)}, u32[]{:S(2)}, u32[]{:S(2)}) collective-permute-start(bf16[512,128]{1,0:T(8,128)(2,1)S(1)} %collective-permute-done.refs_1_), channel_id=1, source_target_pairs={{0,16},{16,0},{32,48},{48,32},{64,80},{80,64},{96,112},{112,96},{1... | collective-permute-start | bytes 393224 | tf_op jit(solution)/shard_map/ppermute | solution.py:345
  28.7 46.2 %copy-start = (f32[128,128]{1,0:T(8,128)S(1)}, f32[128,128]{1,0:T(8,128)}, u32[]{:S(2)}) copy-start(f32[128,128]{1,0:T(8,128)} %get-tuple-element.21.vq) | copy-start | bytes 196612
  28.7 46.2 %copy-start.1 = (f32[128,128]{1,0:T(8,128)S(1)}, f32[128,128]{1,0:T(8,128)}, u32[]{:S(2)}) copy-start(f32[128,128]{1,0:T(8,128)} %get-tuple-element.22.nv) | copy-start | bytes 196612
  28.7 46.2 %copy-start.2 = (f32[128,128]{1,0:T(8,128)S(1)}, f32[128,128]{1,0:T(8,128)}, u32[]{:S(2)}) copy-start(f32[128,128]{1,0:T(8,128)} %get-tuple-element.23.pos) | copy-start | bytes 196612

commit v7 on v6

--- a/solution.py
+++ b/solution.py
@@ -122,12 +122,15 @@
 
 
 def prepare_cols(table, cols, zc, st):
-    rows = cols[0].shape[0]
-    size = 4 * 16 * len(cols)
+    chunks = []
+    for c in cols:
+        chunks += [c] if len(c.shape) == 2 else [c.at[h] for h in range(c.shape[0])]
+    rows = chunks[0].shape[0]
+    size = 4 * 16 * len(chunks)
     width = T0 - V0
     for k in range(rows // 64):
         data = jnp.concatenate(
-            [c[g * 16 : g * 16 + 16, :] for g in range(4 * k, 4 * k + 4) for c in cols],
+            [c[g * 16 : g * 16 + 16, :] for g in range(4 * k, 4 * k + 4) for c in chunks],
             axis=0,
         )
         span = slice(k * size, (k + 1) * size)
@@ -142,30 +145,33 @@
         st[4 * width :, span] = values.astype(BF16)
 
 
-def product_kernel(tile, own_col, table, gathered, *refs):
-    cols, (out, own, kern_ref, task_ref, zc, st, mine) = refs[:-7], refs[-7:]
-    t = pl.program_id(0)
+def product_kernel(tile, pieces, last, own_chunk, table, gathered, *refs):
+    cols, refs = refs[:pieces], refs[pieces:]
+    if last:
+        before, out, own, kern_ref, task_ref, zc, st, mine = refs
+    else:
+        out, kern_ref, task_ref, zc, st = refs
+    i = pl.program_id(0)
     steps = pl.num_programs(0)
-    n_col = gathered.shape[0]
+    chunks = gathered.shape[0]
     half = gathered.shape[1] - 16
-    wide = n_col * 16
-    rows = 4 * wide
     tab = table[...]
 
-    @pl.when(t == 0)
+    @pl.when(i == 0)
     def _():
-        every = gathered[:, half:, :].reshape(wide, 128).astype(F32).T
+        every = gathered[:, half:, :].reshape(chunks * 16, 128).astype(F32).T
         for k in range(task_ref.shape[0]):
-            task_ref[k] = every[4 * k : 4 * k + 8]
+            task_ref[k] = every[8 * k : 8 * k + 8]
         prepare_cols(tab, cols, zc, st)
 
-    first = pl.multiple_of(lax.rem(t, steps // 2) * 64, 64)
-    blocks = [gathered[k, pl.ds(first, 64), :] for k in range(n_col)]
+    first = pl.multiple_of(lax.rem(i, steps // 2) * 128, 128)
+    blocks = [gathered[k, pl.ds(first, 128), :] for k in range(chunks)]
     data = jnp.concatenate(
-        [b[m * 16 : m * 16 + 16, :] for m in range(4) for b in blocks], axis=0
-    )
+        [b[g * 16 : g * 16 + 16, :] for g in range(8) for b in blocks], axis=0
+    )
+    rows = data.shape[0]
     turned = data.astype(F32).T
-    z = jnp.where(t < steps // 2, turned[:V0], turned[V0:])
+    z = jnp.where(i < steps // 2, turned[:V0], turned[V0:])
     norm = jnp.sum(z * z, axis=0, keepdims=True) * (-0.5 * LOG2E)
     parts = [a.astype(F32) for a in split3(norm)]
     sub = iota((T0 - V0, rows), 0)
@@ -175,8 +181,8 @@
     z = jnp.concatenate(
         split3(z * LOG2E) + (jnp.zeros((T0 - V0, rows), BF16), extra.astype(BF16)), axis=0
     )
-    four = task_ref[t]
-    task = jnp.concatenate([four[m : m + 1] for m in range(4)], axis=1)
+    eight = task_ref[i]
+    task = jnp.concatenate([eight[m : m + 1] for m in range(8)], axis=1)
     weight = look_up(tab, task.astype(jnp.int32))
     width = st.shape[0] // 5
     total = None
@@ -187,51 +193,70 @@
         kern_ref[span, :] = kern
         part = jnp.dot(st[: 4 * width, span], kern, preferred_element_type=F32)
         total = part if total is None else total + part
+    low = weight[0:1] * total[:width]
+    for q in range(1, 4):
+        low = low + weight[q : q + 1] * total[q * width : (q + 1) * width]
     size = zc.shape[0] // 32
-    band = pl.ds(pl.multiple_of(jnp.clip(4 * t - 1, 0, 26) * size, size), 6 * size)
-    same = zc[band, 128 + T0 : 129 + T0] == task.astype(BF16)
-    kept = jnp.where(same, kern_ref[band, :], jnp.asarray(0.0, BF16))
-    summed = weight[4:5] * jnp.dot(st[4 * width :, band], kept, preferred_element_type=F32)
-    for q in range(4):
-        summed = summed + weight[q : q + 1] * total[q * width : (q + 1) * width]
-    folded = jnp.concatenate(
-        [summed[:, m * wide : (m + 1) * wide] for m in range(4)], axis=0
-    ).T.reshape(n_col, 16, 128)
-    out[...] = folded.astype(out.dtype)
-    mine[...] = folded
-    own[...] = mine[own_col[0]]
-
-
-def product_call(col, table, gathered, cols):
-    n_col, packed, _ = gathered.shape
-    total = len(cols) * cols[0].shape[0]
-    tiles = (packed - 16) // 32
-    rows = n_col * 64
+    count = rows // 2
+    quarter = count // 4
+    for k in range(2):
+        lanes = slice(k * count, (k + 1) * count)
+        start = pl.multiple_of(jnp.clip(4 * (2 * i + k) - 1, 0, 26) * size, size)
+        band = pl.ds(start, 6 * size)
+        same = zc[band, 128 + T0 : 129 + T0] == task[:, lanes].astype(BF16)
+        kept = jnp.where(same, kern_ref[band, lanes], jnp.asarray(0.0, BF16))
+        diag = jnp.dot(st[4 * width :, band], kept, preferred_element_type=F32)
+        summed = low[:, lanes] + weight[4:5, lanes] * diag
+        folded = jnp.concatenate(
+            [summed[:, m * quarter : (m + 1) * quarter] for m in range(4)], axis=0
+        ).T.reshape(chunks, 16, 128)
+        span = slice(k * 16, k * 16 + 16)
+        if last:
+            folded = folded + before[:, span, :]
+            mine[...] = folded
+            own[span, :] = mine[own_chunk[0]]
+        out[:, span, :] = folded.astype(out.dtype)
+
+
+def product_call(own_chunk, table, gathered, cols, before=()):
+    chunks, packed, _ = gathered.shape
+    total = sum(c.size // 128 for c in cols)
+    quarter = (packed - 16) // 2
+    steps = quarter // 32
+    rows = chunks * 128
+    block = pl.BlockSpec((chunks, 32, 128), lambda i: (0, i, 0))
+    out_specs, scratch = [block], []
+    out_shape = [jax.ShapeDtypeStruct((chunks, quarter, 128), BF16 if before else F32)]
+    if before:
+        out_specs.append(pl.BlockSpec((32, 128), lambda i: (i, 0)))
+        out_shape.append(jax.ShapeDtypeStruct((quarter, 128), F32))
+        scratch.append(pltpu.VMEM((chunks, 16, 128), F32))
     return pl.pallas_call(
-        functools.partial(product_kernel, 2048),
-        grid=(tiles,),
-        in_specs=[SMEM] + [VMEM] * (2 + len(cols)),
-        out_specs=[
-            pl.BlockSpec((n_col, 16, 128), lambda i: (0, i, 0)),
-            pl.BlockSpec((16, 128), lambda i: (i, 0)),
-        ],
-        out_shape=[
-            jax.ShapeDtypeStruct((n_col, tiles * 16, 128), BF16),
-            jax.ShapeDtypeStruct((tiles * 16, 128), F32),
-        ],
+        functools.partial(product_kernel, 2048, len(cols), bool(before)),
+        grid=(steps,),
+        in_specs=[SMEM] + [VMEM] * (2 + len(cols)) + [block] * len(before),
+        out_specs=out_specs,
+        out_shape=out_shape,
         scratch_shapes=[
             pltpu.VMEM((total, rows), BF16),
-            pltpu.VMEM((tiles, 8, n_col * 16), F32),
+            pltpu.VMEM((steps, 8, chunks * 16), F32),
             pltpu.VMEM((total, 256), BF16),
             pltpu.VMEM((5 * (T0 - V0), total), BF16),
-            pltpu.VMEM((n_col, 16, 128), F32),
-        ],
+        ]
+        + scratch,
         compiler_params=LARGE,
         cost_estimate=pl.CostEstimate(
-            flops=2 * tiles * rows * total * 512, bytes_accessed=4 << 20, transcendentals=0
+            flops=2 * steps * rows * total * 512, bytes_accessed=4 << 20, transcendentals=0
         ),
         name="product",
-    )(col, table, gathered, *cols)
+    )(own_chunk, table, gathered, *cols, *before)
+
+
+def stack_kernel(count, *refs):
+    if count == 0:
+        refs[-1][...] = refs[0][...]
+    for k in range(count):
+        refs[-1][k] = refs[k][...]
 
 
 def image_kernel(col, parts, own, vq, nv, pos, send):
@@ -248,15 +273,15 @@
     ratio = jnp.where(vv > 0.0, vi / jnp.where(vv > 0.0, vv, 1.0), 0.0)
     rest = img - jnp.concatenate([ratio] * 4, axis=1) * v
     row = jnp.concatenate([vv, vi, over(rest * rest), jnp.zeros_like(vv)], axis=1)
-    send[:, 0, :] = img
-    send[:, 1, :] = v
-    send[:, 2, :] = pos[...] + row
+    send[:, 0, :128] = img
+    send[:, 0, 128:256] = v
+    send[:, 0, 256:] = pos[...] + row
 
 
 def final_kernel(got, residual, direction, alpha_out, beta_out):
     n = got.shape[0]
     rows = residual.shape[1]
-    every = got[:, 2, :]
+    every = got[:, 0, 256:]
     turned = every.T
 
     def over(axis, pick):
@@ -273,8 +298,8 @@
     sums = jnp.concatenate([alpha, beta, jnp.zeros((32, 126), F32)], axis=1).T
     alpha_out[...] = sums[0:1]
     beta_out[...] = sums[1:2]
-    v = got[:, 1, :].T
-    res = v - jnp.concatenate([alpha] * 4, axis=0) * got[:, 0, :].T
+    v = got[:, 0, 128:256].T
+    res = v - jnp.concatenate([alpha] * 4, axis=0) * got[:, 0, :128].T
     pieces = split3(res) + (v.astype(BF16),)
     total = None
     for m in range(4):
@@ -308,7 +333,18 @@
     axes = ("row", "col")
     width = probes.shape[1]
     quarter = rows // 4
-    col = lax.axis_index("col").astype(jnp.int32).reshape(1)
+    col = lax.axis_index("col")
+    own_chunk = (col // 4 * 2 + col % 2).astype(jnp.int32).reshape(1)
+    groups = [[4 * x + z for x in range(n_col // 4) for z in pair] for pair in ((0, 1), (2, 3))]
+
+    def over_rows(value):
+        return lax.all_to_all(
+            value, "col", split_axis=0, concat_axis=0, tiled=True, axis_index_groups=groups
+        )
+
+    def other_core(value):
+        return lax.ppermute(value, "row", [(i, i ^ 1) for i in range(n_row)])
+
     shape = jax.ShapeDtypeStruct((quarter, 128), F32)
     cols, share, vq, nv, pos, table = pl.pallas_call(
         pack_kernel,
@@ -316,7 +352,7 @@
         out_specs=[VMEM] * 6,
         out_shape=[
             jax.ShapeDtypeStruct((rows, 128), BF16),
-            jax.ShapeDtypeStruct((n_col, rows // 2 + 16, 128), BF16),
+            jax.ShapeDtypeStruct((n_col // 2, rows // 2 + 16, 128), BF16),
             shape,
             shape,
             shape,
@@ -337,22 +373,42 @@
         task_diag.reshape(1, -1),
         task_noise.reshape(1, -1),
     )
-    gathered = lax.all_to_all(share, "col", split_axis=0, concat_axis=0, tiled=True)
-    chunks = [cols] + [
+    gathered = over_rows(share)
+    own_y = [cols] + [
         lax.ppermute(cols, "row", [(i, (i + 2 * k) % n_row) for i in range(n_row)])
         for k in range(1, n_row // 2)
     ]
-    chunks = chunks + [lax.ppermute(c, "row", [(i, i ^ 1) for i in range(n_row)]) for c in chunks]
-    parts, own = product_call(col, table, gathered, chunks)
-    summed = lax.all_to_all(parts, "col", split_axis=0, concat_axis=0, tiled=True)
+    other_y = [other_core(c) for c in own_y]
+    stacked = jax.ShapeDtypeStruct((len(own_y),) + cols.shape, BF16)
+    anywhere = pl.BlockSpec(memory_space=pl.ANY)
+    pair_y = pl.pallas_call(
+        functools.partial(stack_kernel, len(own_y)),
+        in_specs=[VMEM] * len(own_y) + [anywhere] * len(other_y),
+        out_specs=VMEM,
+        out_shape=stacked,
+        compiler_params=PARAMS,
+        name="stack",
+    )(*own_y, *other_y)
+    pair_y = lax.ppermute(pair_y, "col", [(i, i ^ 3) for i in range(n_col)])
+    (sums,) = product_call(own_chunk, table, gathered, own_y + other_y)
+    pair_y = pl.pallas_call(
+        functools.partial(stack_kernel, 0),
+        in_specs=[VMEM, anywhere],
+        out_specs=VMEM,
+        out_shape=stacked,
+        compiler_params=PARAMS,
+        name="gate",
+    )(pair_y, sums)
+    parts, own = product_call(own_chunk, table, gathered, [pair_y, other_core(pair_y)], (sums,))
+    summed = over_rows(parts)
     send = pl.pallas_call(
         image_kernel,
         in_specs=[SMEM] + [VMEM] * 5,
         out_specs=VMEM,
-        out_shape=jax.ShapeDtypeStruct((devices, 3, 128), F32),
+        out_shape=jax.ShapeDtypeStruct((devices, 1, 384), F32),
         compiler_params=PARAMS,
         name="image",
-    )(col, summed, own, vq, nv, pos)
+    )(own_chunk, summed, own, vq, nv, pos)
     got = lax.all_to_all(send, ("row", "col"), split_axis=0, concat_axis=0, tiled=True)
     residual, direction, alpha, beta = pl.pallas_call(
         final_kernel,

time: 96.6 us -> 92.7 us (0.960)
  blocking collectives: 32.9 us -> 25.3 us
  starting transfers between devices: 19.2 us -> 23.3 us
  waiting for transfers between devices: 5.43 us -> 3.06 us
  Pallas kernels: 38.1 us -> 39.9 us
    ppermute x4 -> x6, starting transfers between devices: 6.76 us -> 13.1 us  [the longest x5 9.54 us: other_core(): return lax.ppermute(value, 'row', [(i, i ^ 1) for i in range(n_row)])]
    all_to_all x1, blocking collectives: 13.7 us -> 9.84 us  [over_rows(): lax.all_to_all(value, 'col', split_axis=0, concat_axis=0, tiled=True, axi...]
    all_to_all x1, blocking collectives: 19.2 us -> 15.4 us  [body(): lax.all_to_all(send, ('row', 'col'), split_axis=0, concat_axis=0, tiled=T...]
    all_to_all x1, starting transfers between devices: 8.57 us -> 6.33 us  [over_rows(): lax.all_to_all(value, 'col', split_axis=0, concat_axis=0, tiled=True, axi...]
    pallas_call x1 -> x4, Pallas kernels: 32.5 us -> 34.6 us  [the longest x2 34.5 us: product_call(): pl.pallas_call(functools.partial(product_kernel, 2048, len(cols), bool(be...]
    all_to_all x1, waiting for transfers between devices: 2.03 us -> 0.01 us  [over_rows(): lax.all_to_all(value, 'col', split_axis=0, concat_axis=0, tiled=True, axi...]
    ppermute x3, waiting for transfers between devices: 2.42 us -> 0.54 us  [body(): lax.ppermute(cols, 'row', [(i, (i + 2 * k) % n_row) for i in range(n_row)])]
    ppermute x4 -> x6, waiting for transfers between devices: 0.98 us -> 2.51 us  [the longest x5 2.51 us: other_core(): return lax.ppermute(value, 'row', [(i, i ^ 1) for i in range(n_row)])]
  transfers between devices with their start and end apart: 8 -> 10, of which waited for: 4 -> 4; matrix products, arithmetic and copies ran while one was open for 0% -> 0% of each run, Pallas kernels for 0% -> 19%
where the time goes in v7:
time: 92.7 us; the launch traced here: 92.3 us
  Pallas kernels  39.9 us (43%)
  blocking collectives  25.3 us (27%)
  starting transfers between devices  23.3 us (25%)
  waiting for transfers between devices  3.06 us (3%)
    pallas_call x2, Pallas kernels, product_call(): pl.pallas_call(functools.partial(product_kernel, 2048, len(cols), bool(be...  34.5 us
    all_to_all x1, blocking collectives, body(): lax.all_to_all(send, ('row', 'col'), split_axis=0, concat_axis=0, tiled=T...  15.4 us
    all_to_all x1, blocking collectives, over_rows(): lax.all_to_all(value, 'col', split_axis=0, concat_axis=0, tiled=True, axi...  9.84 us
    ppermute x5, starting transfers between devices, other_core(): return lax.ppermute(value, 'row', [(i, i ^ 1) for i in range(n_row)])  9.54 us
    all_to_all x1, starting transfers between devices, over_rows(): lax.all_to_all(value, 'col', split_axis=0, concat_axis=0, tiled=True, axi...  6.33 us
    ppermute x3, starting transfers between devices, body(): lax.ppermute(cols, 'row', [(i, (i + 2 * k) % n_row) for i in range(n_row)])  3.84 us
    ppermute x1, starting transfers between devices, body(): pair_y = lax.ppermute(pair_y, 'col', [(i, i ^ 3) for i in range(n_col)])  3.6 us
    pallas_call x1, Pallas kernels, body(): pl.pallas_call(pack_kernel, in_specs=[VMEM] * 11, out_specs=[VMEM] * 6, o...  3.2 us
  transfers between devices with their start and end apart: 10, of which 4 were waited for; matrix products, arithmetic and copies ran while one was open for 0% of the time, Pallas kernels for 19%

profile of v7, /device:TPU:1, one launch (start us, length us, event | category | flops | bytes accessed | tf_op | source)
XLA Modules:
  0.0 92.3 jit_solution(16434215199400936121)
XLA Ops:
  0.6 3.2 %pack.1 = (bf16[512,128]{1,0:T(8,128)(2,1)}, bf16[8,272,128]{2,1,0:T(8,128)(2,1)}, f32[128,128]{1,0:T(8,128)}, f32[128,128]{1,0:T(8,128)}, f32[128,128]{1,0:T(8,128)}, /*index=5*/f32[8,256]{1,0:T(8,128)}) custom-call(bf16[64,512]{1,0:T(8,128)(2,1)} %bitcast.15, s32[1,512]{1,0:T(1,128)} %bitcast.18, s32[1,256]{1,0:T(1,128)} %bitcast.20, s32[1,512]{1,0:T(1,128)} %bitcast.19, ...), custom_call_target="tpu_custom_call" | custom-call | tf_op jit(solution)/shard_map/pack/pallas_call | solution.py:349
  3.8 0.0 copy-start
  3.8 6.3 %all-to-all-start = ((bf16[8,272,128]{2,1,0:T(8,128)(2,1)}), bf16[8,272,128]{2,1,0:T(8,128)(2,1)S(1)}, u32[]{:S(2)}, u32[]{:S(2)}) async-start(bf16[8,272,128]{2,1,0:T(8,128)(2,1)} %get-tuple-element.17), calls=%async_computation | async-start | bytes 1114112 | tf_op jit(solution)/shard_map/all_to_all | solution.py:341
  10.2 0.0 copy-done
  10.2 2.8 %collective-permute-start.2 = (bf16[512,128]{1,0:T(8,128)(2,1)S(1)}, bf16[512,128]{1,0:T(8,128)(2,1)S(1)}, u32[]{:S(2)}, u32[]{:S(2)}) collective-permute-start(bf16[512,128]{1,0:T(8,128)(2,1)S(1)} %copy-done), channel_id=1, source_target_pairs={{0,96},{16,112},{32,0},{48,16},{64,32},{80,48},{96,64},{112,80},{1... | collective-permute-start | bytes 393224 | tf_op jit(solution)/shard_map/ppermute | solution.py:378
  13.0 0.3 collective-permute-start.1
  13.3 0.7 collective-permute-start
  14.0 1.8 %collective-permute-start.3 = (bf16[512,128]{1,0:T(8,128)(2,1)S(1)}, bf16[512,128]{1,0:T(8,128)(2,1)S(1)}, u32[]{:S(2)}, u32[]{:S(2)}) collective-permute-start(bf16[512,128]{1,0:T(8,128)(2,1)S(1)} %copy-done), channel_id=1, source_target_pairs={{0,16},{16,0},{32,48},{48,32},{64,80},{80,64},{96,112},{112,96},{1... | collective-permute-start | bytes 393224 | tf_op jit(solution)/shard_map/ppermute | solution.py:346
  15.8 0.1 collective-permute-done.2.refs_3_
  16.0 3.6 %collective-permute-start.6 = (bf16[512,128]{1,0:T(8,128)(2,1)S(1)}, bf16[512,128]{1,0:T(8,128)(2,1)S(1)}, u32[]{:S(2)}, u32[]{:S(2)}) collective-permute-start(bf16[512,128]{1,0:T(8,128)(2,1)S(1)} %collective-permute-done.2.refs_3_), channel_id=1, source_target_pairs={{0,16},{16,0},{32,48},{48,32},{64,80},{80,64},{96,112},{112,96},{1... | collective-permute-start | bytes 393224 | tf_op jit(solution)/shard_map/ppermute | solution.py:346
  19.5 0.0 collective-permute-done.1.refs_2_
  19.5 2.3 %collective-permute-start.5 = (bf16[512,128]{1,0:T(8,128)(2,1)S(1)}, bf16[512,128]{1,0:T(8,128)(2,1)S(1)}, u32[]{:S(2)}, u32[]{:S(2)}) collective-permute-start(bf16[512,128]{1,0:T(8,128)(2,1)S(1)} %collective-permute-done.1.refs_2_), channel_id=1, source_target_pairs={{0,16},{16,0},{32,48},{48,32},{64,80},{80,64},{96,112},{112,96},{1... | collective-permute-start | bytes 393224 | tf_op jit(solution)/shard_map/ppermute | solution.py:346
  21.8 0.4 collective-permute-done.refs_1_
  22.3 1.0 %collective-permute-start.4 = (bf16[512,128]{1,0:T(8,128)(2,1)S(1)}, bf16[512,128]{1,0:T(8,128)(2,1)S(1)}, u32[]{:S(2)}, u32[]{:S(2)}) collective-permute-start(bf16[512,128]{1,0:T(8,128)(2,1)S(1)} %collective-permute-done.refs_1_), channel_id=1, source_target_pairs={{0,16},{16,0},{32,48},{48,32},{64,80},{80,64},{96,112},{112,96},{1... | collective-permute-start | bytes 393224 | tf_op jit(solution)/shard_map/ppermute | solution.py:346
  23.2 0.0 copy-start.4
  23.2 0.0 collective-permute-done.3.refs_4_
  23.2 0.0 collective-permute-done.6.refs_7_
  23.2 0.0 collective-permute-done.5.refs_6_
  23.2 1.0 %collective-permute-done.4.refs_5_ = bf16[512,128]{1,0:T(8,128)(2,1)S(1)} collective-permute-done((bf16[512,128]{1,0:T(8,128)(2,1)S(1)}, bf16[512,128]{1,0:T(8,128)(2,1)S(1)}, u32[]{:S(2)}, u32[]{:S(2)}) %collective-permute-start.4) | collective-permute-done | bytes 131104 | tf_op jit(solution)/shard_map/ppermute | solution.py:346
  24.2 3.6 %collective-permute-start.7 = (bf16[4,512,128]{2,1,0:T(8,128)(2,1)S(1)}, bf16[4,512,128]{2,1,0:T(8,128)(2,1)S(1)}, u32[]{:S(2)}, u32[]{:S(2)}) collective-permute-start(bf16[4,512,128]{2,1,0:T(8,128)(2,1)S(1)} %stack.1), channel_id=1, source_target_pairs={{0,3},{1,2},{2,1},{3,0},{4,7},{5,6},{6,5},{7,4},{8,11},{9,10},{10,... | collective-permute-start | bytes 1572872 | tf_op jit(solution)/shard_map/ppermute | solution.py:392
  27.8 0.0 all-to-all-done.gathered
  27.8 0.0 copy-done.4
  27.8 17.2 %product.2.refs_1_.refs_2_ = f32[8,128,128]{2,1,0:T(8,128)S(1)} custom-call(s32[1]{0:T(128)} %bitcast.own_chunk.col, f32[8,256]{1,0:T(8,128)S(1)} %copy-done.4, bf16[8,272,128]{2,1,0:T(8,128)(2,1)S(1)} %all-to-all-done.gathered, bf16[512,128]{1,0:T(8,128)(2,1)S(1)} %copy-done, bf16[512,128]{1,0:T(8,128)(2,1)S(1)} %collective-permute-done.refs_1_, ...), custom_call_target="tpu_custom_call" | custom-call | flops 17179869184 | bytes 4194304 | tf_op jit(solution)/shard_map/product/pallas_call | solution.py:234
  45.1 0.0 collective-permute-done.7.refs_0_
  45.1 0.9 collective-permute-start.8
  46.0 1.5 %collective-permute-done.8.refs_1_ = bf16[4,512,128]{2,1,0:T(8,128)(2,1)S(1)} collective-permute-done((bf16[4,512,128]{2,1,0:T(8,128)(2,1)S(1)}, bf16[4,512,128]{2,1,0:T(8,128)(2,1)S(1)}, u32[]{:S(2)}, u32[]{:S(2)}) %collective-permute-start.8) | collective-permute-done | bytes 524320 | tf_op jit(solution)/shard_map/ppermute | solution.py:346
  47.6 17.3 %product.3 = (bf16[8,128,128]{2,1,0:T(8,128)(2,1)S(1)}, f32[128,128]{1,0:T(8,128)S(1)}) custom-call(s32[1]{0:T(128)} %bitcast.own_chunk.col, f32[8,256]{1,0:T(8,128)S(1)} %copy-done.4, bf16[8,272,128]{2,1,0:T(8,128)(2,1)S(1)} %all-to-all-done.gathered, bf16[4,512,128]{2,1,0:T(8,128)(2,1)S(1)} %gate.1.refs_0_, ...), custom_call_target="tpu_custom_call" | custom-call | flops 17179869184 | bytes 4194304 | tf_op jit(solution)/shard_map/product/pallas_call | solution.py:234
  64.8 0.0 copy-start.1
  64.9 0.0 copy-start.2
  64.9 0.0 copy-start.3
  64.9 9.8 %all_to_all.15.parts = bf16[8,128,128]{2,1,0:T(8,128)(2,1)S(1)} all-to-all(bf16[8,128,128]{2,1,0:T(8,128)(2,1)S(1)} %get-tuple-element.19), channel_id=1, replica_groups={{0,1,4,5,8,9,12,13},{2,3,6,7,10,11,14,15},{16,17,20,21,24,25,28,29},{18..., dimensions={0} | all-to-all | bytes 524288 | tf_op jit(solution)/shard_map/all_to_all | solution.py:341
  74.7 0.0 copy-done.1
  74.7 0.0 copy-done.2
  74.7 0.0 copy-done.3
  74.7 0.4 image.1
  75.2 15.4 %all_to_all.16.got = f32[128,1,384]{2,1,0:T(1,128)S(1)} all-to-all(f32[128,1,384]{2,1,0:T(1,128)S(1)} %image.1), channel_id=1, replica_groups=mesh['row'=8,'col'=16] {'row','col'}, dimensions={0} | all-to-all | bytes 393216 | tf_op jit(solution)/shard_map/all_to_all | solution.py:412
  90.6 1.7 %final.1 = (f32[32,512]{1,0:T(8,128)}, f32[32,512]{1,0:T(8,128)}, f32[1,32]{1,0:T(1,128)}, f32[1,32]{1,0:T(1,128)}) custom-call(f32[128,1,384]{2,1,0:T(1,128)S(1)} %all_to_all.16.got), custom_call_target="tpu_custom_call" | custom-call | tf_op jit(solution)/shard_map/final/pallas_call | solution.py:413
  (2 shorter events, 0.1 us)
Async XLA Ops:
  3.8 6.3 %copy-start = (bf16[512,128]{1,0:T(8,128)(2,1)S(1)}, bf16[512,128]{1,0:T(8,128)(2,1)}, u32[]{:S(2)}) copy-start(bf16[512,128]{1,0:T(8,128)(2,1)} %get-tuple-element.18.refs_0_) | copy-start | bytes 393220
  3.8 24.0 %all-to-all-start = ((bf16[8,272,128]{2,1,0:T(8,128)(2,1)}), bf16[8,272,128]{2,1,0:T(8,128)(2,1)S(1)}, u32[]{:S(2)}, u32[]{:S(2)}) async-start(bf16[8,272,128]{2,1,0:T(8,128)(2,1)} %get-tuple-element.17), calls=%async_computation | async-start | bytes 1114112 | tf_op jit(solution)/shard_map/all_to_all | solution.py:341
  10.2 5.8 %collective-permute-start.2 = (bf16[512,128]{1,0:T(8,128)(2,1)S(1)}, bf16[512,128]{1,0:T(8,128)(2,1)S(1)}, u32[]{:S(2)}, u32[]{:S(2)}) collective-permute-start(bf16[512,128]{1,0:T(8,128)(2,1)S(1)} %copy-done), channel_id=1, source_target_pairs={{0,96},{16,112},{32,0},{48,16},{64,32},{80,48},{96,64},{112,80},{1... | collective-permute-start | bytes 393224 | tf_op jit(solution)/shard_map/ppermute | solution.py:378
  13.0 6.5 %collective-permute-start.1 = (bf16[512,128]{1,0:T(8,128)(2,1)S(1)}, bf16[512,128]{1,0:T(8,128)(2,1)S(1)}, u32[]{:S(2)}, u32[]{:S(2)}) collective-permute-start(bf16[512,128]{1,0:T(8,128)(2,1)S(1)} %copy-done), channel_id=1, source_target_pairs={{0,64},{16,80},{32,96},{48,112},{64,0},{80,16},{96,32},{112,48},{1... | collective-permute-start | bytes 393224 | tf_op jit(solution)/shard_map/ppermute | solution.py:378
  13.3 8.9 %collective-permute-start = (bf16[512,128]{1,0:T(8,128)(2,1)S(1)}, bf16[512,128]{1,0:T(8,128)(2,1)S(1)}, u32[]{:S(2)}, u32[]{:S(2)}) collective-permute-start(bf16[512,128]{1,0:T(8,128)(2,1)S(1)} %copy-done), channel_id=1, source_target_pairs={{0,32},{16,48},{32,64},{48,80},{64,96},{80,112},{96,0},{112,16},{1... | collective-permute-start | bytes 393224 | tf_op jit(solution)/shard_map/ppermute | solution.py:378
  14.0 9.2 %collective-permute-start.3 = (bf16[512,128]{1,0:T(8,128)(2,1)S(1)}, bf16[512,128]{1,0:T(8,128)(2,1)S(1)}, u32[]{:S(2)}, u32[]{:S(2)}) collective-permute-start(bf16[512,128]{1,0:T(8,128)(2,1)S(1)} %copy-done), channel_id=1, source_target_pairs={{0,16},{16,0},{32,48},{48,32},{64,80},{80,64},{96,112},{112,96},{1... | collective-permute-start | bytes 393224 | tf_op jit(solution)/shard_map/ppermute | solution.py:346
  16.0 7.3 %collective-permute-start.6 = (bf16[512,128]{1,0:T(8,128)(2,1)S(1)}, bf16[512,128]{1,0:T(8,128)(2,1)S(1)}, u32[]{:S(2)}, u32[]{:S(2)}) collective-permute-start(bf16[512,128]{1,0:T(8,128)(2,1)S(1)} %collective-permute-done.2.refs_3_), channel_id=1, source_target_pairs={{0,16},{16,0},{32,48},{48,32},{64,80},{80,64},{96,112},{112,96},{1... | collective-permute-start | bytes 393224 | tf_op jit(solution)/shard_map/ppermute | solution.py:346
  19.5 3.7 %collective-permute-start.5 = (bf16[512,128]{1,0:T(8,128)(2,1)S(1)}, bf16[512,128]{1,0:T(8,128)(2,1)S(1)}, u32[]{:S(2)}, u32[]{:S(2)}) collective-permute-start(bf16[512,128]{1,0:T(8,128)(2,1)S(1)} %collective-permute-done.1.refs_2_), channel_id=1, source_target_pairs={{0,16},{16,0},{32,48},{48,32},{64,80},{80,64},{96,112},{112,96},{1... | collective-permute-start | bytes 393224 | tf_op jit(solution)/shard_map/ppermute | solution.py:346
  22.3 1.9 %collective-permute-start.4 = (bf16[512,128]{1,0:T(8,128)(2,1)S(1)}, bf16[512,128]{1,0:T(8,128)(2,1)S(1)}, u32[]{:S(2)}, u32[]{:S(2)}) collective-permute-start(bf16[512,128]{1,0:T(8,128)(2,1)S(1)} %collective-permute-done.refs_1_), channel_id=1, source_target_pairs={{0,16},{16,0},{32,48},{48,32},{64,80},{80,64},{96,112},{112,96},{1... | collective-permute-start | bytes 393224 | tf_op jit(solution)/shard_map/ppermute | solution.py:346
  23.2 4.6 %copy-start.4 = (f32[8,256]{1,0:T(8,128)S(1)}, f32[8,256]{1,0:T(8,128)}, u32[]{:S(2)}) copy-start(f32[8,256]{1,0:T(8,128)} %get-tuple-element.16.table) | copy-start | bytes 24580
  24.2 20.8 %collective-permute-start.7 = (bf16[4,512,128]{2,1,0:T(8,128)(2,1)S(1)}, bf16[4,512,128]{2,1,0:T(8,128)(2,1)S(1)}, u32[]{:S(2)}, u32[]{:S(2)}) collective-permute-start(bf16[4,512,128]{2,1,0:T(8,128)(2,1)S(1)} %stack.1), channel_id=1, source_target_pairs={{0,3},{1,2},{2,1},{3,0},{4,7},{5,6},{6,5},{7,4},{8,11},{9,10},{10,... | collective-permute-start | bytes 1572872 | tf_op jit(solution)/shard_map/ppermute | solution.py:392
  45.1 2.4 %collective-permute-start.8 = (bf16[4,512,128]{2,1,0:T(8,128)(2,1)S(1)}, bf16[4,512,128]{2,1,0:T(8,128)(2,1)S(1)}, u32[]{:S(2)}, u32[]{:S(2)}) collective-permute-start(bf16[4,512,128]{2,1,0:T(8,128)(2,1)S(1)} %gate.1.refs_0_), channel_id=1, source_target_pairs={{0,16},{16,0},{32,48},{48,32},{64,80},{80,64},{96,112},{112,96},{1... | collective-permute-start | bytes 1572872 | tf_op jit(solution)/shard_map/ppermute | solution.py:346
  64.8 9.9 %copy-start.1 = (f32[128,128]{1,0:T(8,128)S(1)}, f32[128,128]{1,0:T(8,128)}, u32[]{:S(2)}) copy-start(f32[128,128]{1,0:T(8,128)} %get-tuple-element.21.vq) | copy-start | bytes 196612
  64.9 9.9 %copy-start.2 = (f32[128,128]{1,0:T(8,128)S(1)}, f32[128,128]{1,0:T(8,128)}, u32[]{:S(2)}) copy-start(f32[128,128]{1,0:T(8,128)} %get-tuple-element.22.nv) | copy-start | bytes 196612
  64.9 9.9 %copy-start.3 = (f32[128,128]{1,0:T(8,128)S(1)}, f32[128,128]{1,0:T(8,128)}, u32[]{:S(2)}) copy-start(f32[128,128]{1,0:T(8,128)} %get-tuple-element.23.pos) | copy-start | bytes 196612

commit v8 on v7

--- a/solution.py
+++ b/solution.py
@@ -15,7 +15,7 @@
 PARAMS = pltpu.CompilerParams(vmem_limit_bytes=16 * 1024 * 1024)
 ALONE = pltpu.CompilerParams(vmem_limit_bytes=60 * 1024 * 1024)
 LARGE = pltpu.CompilerParams(vmem_limit_bytes=36 * 1024 * 1024)
-V0, T0, N0, ONE, P0, S0 = 64, 96, 97, 100, 103, 112
+V0, T0, N0, ONE, P0, S0, W0 = 64, 96, 97, 100, 103, 105, 112
 LOG2E = math.log2(math.e)
 
 
@@ -73,13 +73,15 @@
     norm = jnp.sum(lat * lat, axis=0, keepdims=True) * (-0.5 * LOG2E)
     local = pos - jnp.floor(pos * (1.0 / rows)) * rows
     high = jnp.floor(local * (1.0 / 16.0))
-    noise = look_up(table, task)[5:6]
+    found = look_up(table, task)
     extra = jnp.concatenate(
         [task.astype(F32)]
         + [a.astype(F32) for a in split3(norm)]
-        + [jnp.ones((3, rows), F32), high, local - 16.0 * high, jnp.zeros((7, rows), F32)]
-        + [a.astype(F32) for a in split3(noise)]
-        + [jnp.zeros((13, rows), F32)],
+        + [jnp.ones((3, rows), F32), high, local - 16.0 * high]
+        + [a.astype(F32) for a in split3(found[5:6])]
+        + [jnp.zeros((4, rows), F32)]
+        + [a.astype(F32) for a in split3(found[0:4])]
+        + [jnp.zeros((4, rows), F32)],
         axis=0,
     ).astype(BF16)
     whole = jnp.concatenate([latent, probes[...], extra], axis=0)
@@ -121,7 +123,7 @@
     pos_out[...] = posq
 
 
-def prepare_cols(table, cols, zc, st):
+def prepare_cols(cols, zc, st):
     chunks = []
     for c in cols:
         chunks += [c] if len(c.shape) == 2 else [c.at[h] for h in range(c.shape[0])]
@@ -138,7 +140,7 @@
         zc[span, 128:] = data
         zc[span, :128] = jnp.where(iota((size, 128), 1) < V0, wide, pltpu.roll(wide, V0, 1)).astype(BF16)
         turned = wide.T
-        weight = look_up(table, turned[T0 : T0 + 1].astype(jnp.int32))
+        weight = turned[W0 : W0 + 4] + turned[W0 + 4 : W0 + 8] + turned[W0 + 8 : W0 + 12]
         values = turned[V0:T0]
         for q in range(4):
             st[q * width : (q + 1) * width, span] = (weight[q : q + 1] * values).astype(BF16)
@@ -162,7 +164,7 @@
         every = gathered[:, half:, :].reshape(chunks * 16, 128).astype(F32).T
         for k in range(task_ref.shape[0]):
             task_ref[k] = every[8 * k : 8 * k + 8]
-        prepare_cols(tab, cols, zc, st)
+        prepare_cols(cols, zc, st)
 
     first = pl.multiple_of(lax.rem(i, steps // 2) * 128, 128)
     blocks = [gathered[k, pl.ds(first, 128), :] for k in range(chunks)]
@@ -383,12 +385,12 @@
     anywhere = pl.BlockSpec(memory_space=pl.ANY)
     pair_y = pl.pallas_call(
         functools.partial(stack_kernel, len(own_y)),
-        in_specs=[VMEM] * len(own_y) + [anywhere] * len(other_y),
+        in_specs=[VMEM] * len(own_y),
         out_specs=VMEM,
         out_shape=stacked,
         compiler_params=PARAMS,
         name="stack",
-    )(*own_y, *other_y)
+    )(*own_y)
     pair_y = lax.ppermute(pair_y, "col", [(i, i ^ 3) for i in range(n_col)])
     (sums,) = product_call(own_chunk, table, gathered, own_y + other_y)
     pair_y = pl.pallas_call(

time: 92.7 us -> 91.5 us (0.987)
  transfers between devices with their start and end apart: 10 -> 10, of which waited for: 4 -> 3; matrix products, arithmetic and copies ran while one was open for 0% -> 0% of each run, Pallas kernels for 19% -> 19%
where the time goes in v8:
time: 91.5 us; the launch traced here: 91.2 us
  Pallas kernels  39.3 us (43%)
  blocking collectives  26 us (28%)
  starting transfers between devices  22.9 us (25%)
  waiting for transfers between devices  2.21 us (2%)
    pallas_call x2, Pallas kernels, product_call(): pl.pallas_call(functools.partial(product_kernel, 2048, len(cols), bool(be...  33.9 us
    all_to_all x1, blocking collectives, body(): lax.all_to_all(send, ('row', 'col'), split_axis=0, concat_axis=0, tiled=T...  16.1 us
    all_to_all x1, blocking collectives, over_rows(): lax.all_to_all(value, 'col', split_axis=0, concat_axis=0, tiled=True, axi...  9.86 us
    ppermute x5, starting transfers between devices, other_core(): return lax.ppermute(value, 'row', [(i, i ^ 1) for i in range(n_row)])  9.15 us
    all_to_all x1, starting transfers between devices, over_rows(): lax.all_to_all(value, 'col', split_axis=0, concat_axis=0, tiled=True, axi...  6.34 us
    ppermute x3, starting transfers between devices, body(): lax.ppermute(cols, 'row', [(i, (i + 2 * k) % n_row) for i in range(n_row)])  3.84 us
    ppermute x1, starting transfers between devices, body(): pair_y = lax.ppermute(pair_y, 'col', [(i, i ^ 3) for i in range(n_col)])  3.59 us
    pallas_call x1, Pallas kernels, body(): pl.pallas_call(pack_kernel, in_specs=[VMEM] * 11, out_specs=[VMEM] * 6, o...  3.2 us
  transfers between devices with their start and end apart: 10, of which 3 were waited for; matrix products, arithmetic and copies ran while one was open for 0% of the time, Pallas kernels for 19%

profile of v8, /device:TPU:1, one launch (start us, length us, event | category | flops | bytes accessed | tf_op | source)
XLA Modules:
  0.0 91.2 jit_solution(11020515687091197775)
XLA Ops:
  0.6 3.2 %pack.1 = (bf16[512,128]{1,0:T(8,128)(2,1)}, bf16[8,272,128]{2,1,0:T(8,128)(2,1)}, f32[128,128]{1,0:T(8,128)}, f32[128,128]{1,0:T(8,128)}, f32[128,128]{1,0:T(8,128)}, /*index=5*/f32[8,256]{1,0:T(8,128)}) custom-call(bf16[64,512]{1,0:T(8,128)(2,1)} %bitcast.15, s32[1,512]{1,0:T(1,128)} %bitcast.18, s32[1,256]{1,0:T(1,128)} %bitcast.20, s32[1,512]{1,0:T(1,128)} %bitcast.19, ...), custom_call_target="tpu_custom_call" | custom-call | tf_op jit(solution)/shard_map/pack/pallas_call | solution.py:351
  3.8 0.0 copy-start
  3.8 6.3 %all-to-all-start = ((bf16[8,272,128]{2,1,0:T(8,128)(2,1)}), bf16[8,272,128]{2,1,0:T(8,128)(2,1)S(1)}, u32[]{:S(2)}, u32[]{:S(2)}) async-start(bf16[8,272,128]{2,1,0:T(8,128)(2,1)} %get-tuple-element.17), calls=%async_computation | async-start | bytes 1114112 | tf_op jit(solution)/shard_map/all_to_all | solution.py:343
  10.2 0.0 copy-done
  10.2 2.8 %collective-permute-start.2 = (bf16[512,128]{1,0:T(8,128)(2,1)S(1)}, bf16[512,128]{1,0:T(8,128)(2,1)S(1)}, u32[]{:S(2)}, u32[]{:S(2)}) collective-permute-start(bf16[512,128]{1,0:T(8,128)(2,1)S(1)} %copy-done), channel_id=1, source_target_pairs={{0,96},{16,112},{32,0},{48,16},{64,32},{80,48},{96,64},{112,80},{1... | collective-permute-start | bytes 393224 | tf_op jit(solution)/shard_map/ppermute | solution.py:380
  13.0 0.3 collective-permute-start.1
  13.3 0.7 collective-permute-start
  14.0 1.8 %collective-permute-start.4 = (bf16[512,128]{1,0:T(8,128)(2,1)S(1)}, bf16[512,128]{1,0:T(8,128)(2,1)S(1)}, u32[]{:S(2)}, u32[]{:S(2)}) collective-permute-start(bf16[512,128]{1,0:T(8,128)(2,1)S(1)} %copy-done), channel_id=1, source_target_pairs={{0,16},{16,0},{32,48},{48,32},{64,80},{80,64},{96,112},{112,96},{1... | collective-permute-start | bytes 393224 | tf_op jit(solution)/shard_map/ppermute | solution.py:348
  15.8 0.2 collective-permute-done.2.refs_3_
  16.0 3.5 %collective-permute-start.7 = (bf16[512,128]{1,0:T(8,128)(2,1)S(1)}, bf16[512,128]{1,0:T(8,128)(2,1)S(1)}, u32[]{:S(2)}, u32[]{:S(2)}) collective-permute-start(bf16[512,128]{1,0:T(8,128)(2,1)S(1)} %collective-permute-done.2.refs_3_), channel_id=1, source_target_pairs={{0,16},{16,0},{32,48},{48,32},{64,80},{80,64},{96,112},{112,96},{1... | collective-permute-start | bytes 393224 | tf_op jit(solution)/shard_map/ppermute | solution.py:348
  19.5 0.0 collective-permute-done.1.refs_2_
  19.5 2.3 %collective-permute-start.6 = (bf16[512,128]{1,0:T(8,128)(2,1)S(1)}, bf16[512,128]{1,0:T(8,128)(2,1)S(1)}, u32[]{:S(2)}, u32[]{:S(2)}) collective-permute-start(bf16[512,128]{1,0:T(8,128)(2,1)S(1)} %collective-permute-done.1.refs_2_), channel_id=1, source_target_pairs={{0,16},{16,0},{32,48},{48,32},{64,80},{80,64},{96,112},{112,96},{1... | collective-permute-start | bytes 393224 | tf_op jit(solution)/shard_map/ppermute | solution.py:348
  21.8 0.4 collective-permute-done.refs_1_
  22.3 1.0 %collective-permute-start.5 = (bf16[512,128]{1,0:T(8,128)(2,1)S(1)}, bf16[512,128]{1,0:T(8,128)(2,1)S(1)}, u32[]{:S(2)}, u32[]{:S(2)}) collective-permute-start(bf16[512,128]{1,0:T(8,128)(2,1)S(1)} %collective-permute-done.refs_1_), channel_id=1, source_target_pairs={{0,16},{16,0},{32,48},{48,32},{64,80},{80,64},{96,112},{112,96},{1... | collective-permute-start | bytes 393224 | tf_op jit(solution)/shard_map/ppermute | solution.py:348
  23.2 0.0 copy-start.4
  23.3 3.6 %collective-permute-start.3 = (bf16[4,512,128]{2,1,0:T(8,128)(2,1)S(1)}, bf16[4,512,128]{2,1,0:T(8,128)(2,1)S(1)}, u32[]{:S(2)}, u32[]{:S(2)}) collective-permute-start(bf16[4,512,128]{2,1,0:T(8,128)(2,1)S(1)} %stack.1), channel_id=1, source_target_pairs={{0,3},{1,2},{2,1},{3,0},{4,7},{5,6},{6,5},{7,4},{8,11},{9,10},{10,... | collective-permute-start | bytes 1572872 | tf_op jit(solution)/shard_map/ppermute | solution.py:394
  26.8 0.0 collective-permute-done.4.refs_4_
  26.8 0.0 collective-permute-done.7.refs_7_
  26.9 0.0 collective-permute-done.6.refs_6_
  26.9 0.0 collective-permute-done.5.refs_5_
  26.9 0.0 all-to-all-done.gathered
  26.9 0.0 copy-done.4
  26.9 16.9 %product.2.refs_1_.refs_2_ = f32[8,128,128]{2,1,0:T(8,128)S(1)} custom-call(s32[1]{0:T(128)} %bitcast.own_chunk.col, f32[8,256]{1,0:T(8,128)S(1)} %copy-done.4, bf16[8,272,128]{2,1,0:T(8,128)(2,1)S(1)} %all-to-all-done.gathered, bf16[512,128]{1,0:T(8,128)(2,1)S(1)} %copy-done, bf16[512,128]{1,0:T(8,128)(2,1)S(1)} %collective-permute-done.refs_1_, ...), custom_call_target="tpu_custom_call" | custom-call | flops 17179869184 | bytes 4194304 | tf_op jit(solution)/shard_map/product/pallas_call | solution.py:236
  43.8 0.0 collective-permute-done.3.refs_0_
  43.9 0.6 collective-permute-start.8
  44.4 1.6 %collective-permute-done.8.refs_1_ = bf16[4,512,128]{2,1,0:T(8,128)(2,1)S(1)} collective-permute-done((bf16[4,512,128]{2,1,0:T(8,128)(2,1)S(1)}, bf16[4,512,128]{2,1,0:T(8,128)(2,1)S(1)}, u32[]{:S(2)}, u32[]{:S(2)}) %collective-permute-start.8) | collective-permute-done | bytes 524320 | tf_op jit(solution)/shard_map/ppermute | solution.py:348
  46.0 17.0 %product.3 = (bf16[8,128,128]{2,1,0:T(8,128)(2,1)S(1)}, f32[128,128]{1,0:T(8,128)S(1)}) custom-call(s32[1]{0:T(128)} %bitcast.own_chunk.col, f32[8,256]{1,0:T(8,128)S(1)} %copy-done.4, bf16[8,272,128]{2,1,0:T(8,128)(2,1)S(1)} %all-to-all-done.gathered, bf16[4,512,128]{2,1,0:T(8,128)(2,1)S(1)} %gate.1.refs_0_, ...), custom_call_target="tpu_custom_call" | custom-call | flops 17179869184 | bytes 4194304 | tf_op jit(solution)/shard_map/product/pallas_call | solution.py:236
  63.0 0.0 copy-start.1
  63.0 0.0 copy-start.2
  63.1 0.0 copy-start.3
  63.1 9.9 %all_to_all.15.parts = bf16[8,128,128]{2,1,0:T(8,128)(2,1)S(1)} all-to-all(bf16[8,128,128]{2,1,0:T(8,128)(2,1)S(1)} %get-tuple-element.19), channel_id=1, replica_groups={{0,1,4,5,8,9,12,13},{2,3,6,7,10,11,14,15},{16,17,20,21,24,25,28,29},{18..., dimensions={0} | all-to-all | bytes 524288 | tf_op jit(solution)/shard_map/all_to_all | solution.py:343
  72.9 0.0 copy-done.1
  72.9 0.0 copy-done.2
  72.9 0.0 copy-done.3
  72.9 0.4 image.1
  73.4 16.1 %all_to_all.16.got = f32[128,1,384]{2,1,0:T(1,128)S(1)} all-to-all(f32[128,1,384]{2,1,0:T(1,128)S(1)} %image.1), channel_id=1, replica_groups=mesh['row'=8,'col'=16] {'row','col'}, dimensions={0} | all-to-all | bytes 393216 | tf_op jit(solution)/shard_map/all_to_all | solution.py:414
  89.5 1.7 %final.1 = (f32[32,512]{1,0:T(8,128)}, f32[32,512]{1,0:T(8,128)}, f32[1,32]{1,0:T(1,128)}, f32[1,32]{1,0:T(1,128)}) custom-call(f32[128,1,384]{2,1,0:T(1,128)S(1)} %all_to_all.16.got), custom_call_target="tpu_custom_call" | custom-call | tf_op jit(solution)/shard_map/final/pallas_call | solution.py:415
  (2 shorter events, 0.1 us)
Async XLA Ops:
  3.8 6.3 %copy-start = (bf16[512,128]{1,0:T(8,128)(2,1)S(1)}, bf16[512,128]{1,0:T(8,128)(2,1)}, u32[]{:S(2)}) copy-start(bf16[512,128]{1,0:T(8,128)(2,1)} %get-tuple-element.18.refs_0_) | copy-start | bytes 393220
  3.8 23.0 %all-to-all-start = ((bf16[8,272,128]{2,1,0:T(8,128)(2,1)}), bf16[8,272,128]{2,1,0:T(8,128)(2,1)S(1)}, u32[]{:S(2)}, u32[]{:S(2)}) async-start(bf16[8,272,128]{2,1,0:T(8,128)(2,1)} %get-tuple-element.17), calls=%async_computation | async-start | bytes 1114112 | tf_op jit(solution)/shard_map/all_to_all | solution.py:343
  10.2 5.8 %collective-permute-start.2 = (bf16[512,128]{1,0:T(8,128)(2,1)S(1)}, bf16[512,128]{1,0:T(8,128)(2,1)S(1)}, u32[]{:S(2)}, u32[]{:S(2)}) collective-permute-start(bf16[512,128]{1,0:T(8,128)(2,1)S(1)} %copy-done), channel_id=1, source_target_pairs={{0,96},{16,112},{32,0},{48,16},{64,32},{80,48},{96,64},{112,80},{1... | collective-permute-start | bytes 393224 | tf_op jit(solution)/shard_map/ppermute | solution.py:380
  13.0 6.5 %collective-permute-start.1 = (bf16[512,128]{1,0:T(8,128)(2,1)S(1)}, bf16[512,128]{1,0:T(8,128)(2,1)S(1)}, u32[]{:S(2)}, u32[]{:S(2)}) collective-permute-start(bf16[512,128]{1,0:T(8,128)(2,1)S(1)} %copy-done), channel_id=1, source_target_pairs={{0,64},{16,80},{32,96},{48,112},{64,0},{80,16},{96,32},{112,48},{1... | collective-permute-start | bytes 393224 | tf_op jit(solution)/shard_map/ppermute | solution.py:380
  13.3 8.9 %collective-permute-start = (bf16[512,128]{1,0:T(8,128)(2,1)S(1)}, bf16[512,128]{1,0:T(8,128)(2,1)S(1)}, u32[]{:S(2)}, u32[]{:S(2)}) collective-permute-start(bf16[512,128]{1,0:T(8,128)(2,1)S(1)} %copy-done), channel_id=1, source_target_pairs={{0,32},{16,48},{32,64},{48,80},{64,96},{80,112},{96,0},{112,16},{1... | collective-permute-start | bytes 393224 | tf_op jit(solution)/shard_map/ppermute | solution.py:380
  14.0 12.8 %collective-permute-start.4 = (bf16[512,128]{1,0:T(8,128)(2,1)S(1)}, bf16[512,128]{1,0:T(8,128)(2,1)S(1)}, u32[]{:S(2)}, u32[]{:S(2)}) collective-permute-start(bf16[512,128]{1,0:T(8,128)(2,1)S(1)} %copy-done), channel_id=1, source_target_pairs={{0,16},{16,0},{32,48},{48,32},{64,80},{80,64},{96,112},{112,96},{1... | collective-permute-start | bytes 393224 | tf_op jit(solution)/shard_map/ppermute | solution.py:348
  16.0 10.9 %collective-permute-start.7 = (bf16[512,128]{1,0:T(8,128)(2,1)S(1)}, bf16[512,128]{1,0:T(8,128)(2,1)S(1)}, u32[]{:S(2)}, u32[]{:S(2)}) collective-permute-start(bf16[512,128]{1,0:T(8,128)(2,1)S(1)} %collective-permute-done.2.refs_3_), channel_id=1, source_target_pairs={{0,16},{16,0},{32,48},{48,32},{64,80},{80,64},{96,112},{112,96},{1... | collective-permute-start | bytes 393224 | tf_op jit(solution)/shard_map/ppermute | solution.py:348
  19.5 7.3 %collective-permute-start.6 = (bf16[512,128]{1,0:T(8,128)(2,1)S(1)}, bf16[512,128]{1,0:T(8,128)(2,1)S(1)}, u32[]{:S(2)}, u32[]{:S(2)}) collective-permute-start(bf16[512,128]{1,0:T(8,128)(2,1)S(1)} %collective-permute-done.1.refs_2_), channel_id=1, source_target_pairs={{0,16},{16,0},{32,48},{48,32},{64,80},{80,64},{96,112},{112,96},{1... | collective-permute-start | bytes 393224 | tf_op jit(solution)/shard_map/ppermute | solution.py:348
  22.3 4.6 %collective-permute-start.5 = (bf16[512,128]{1,0:T(8,128)(2,1)S(1)}, bf16[512,128]{1,0:T(8,128)(2,1)S(1)}, u32[]{:S(2)}, u32[]{:S(2)}) collective-permute-start(bf16[512,128]{1,0:T(8,128)(2,1)S(1)} %collective-permute-done.refs_1_), channel_id=1, source_target_pairs={{0,16},{16,0},{32,48},{48,32},{64,80},{80,64},{96,112},{112,96},{1... | collective-permute-start | bytes 393224 | tf_op jit(solution)/shard_map/ppermute | solution.py:348
  23.2 3.7 %copy-start.4 = (f32[8,256]{1,0:T(8,128)S(1)}, f32[8,256]{1,0:T(8,128)}, u32[]{:S(2)}) copy-start(f32[8,256]{1,0:T(8,128)} %get-tuple-element.16.table) | copy-start | bytes 24580
  23.3 20.6 %collective-permute-start.3 = (bf16[4,512,128]{2,1,0:T(8,128)(2,1)S(1)}, bf16[4,512,128]{2,1,0:T(8,128)(2,1)S(1)}, u32[]{:S(2)}, u32[]{:S(2)}) collective-permute-start(bf16[4,512,128]{2,1,0:T(8,128)(2,1)S(1)} %stack.1), channel_id=1, source_target_pairs={{0,3},{1,2},{2,1},{3,0},{4,7},{5,6},{6,5},{7,4},{8,11},{9,10},{10,... | collective-permute-start | bytes 1572872 | tf_op jit(solution)/shard_map/ppermute | solution.py:394
  43.9 2.2 %collective-permute-start.8 = (bf16[4,512,128]{2,1,0:T(8,128)(2,1)S(1)}, bf16[4,512,128]{2,1,0:T(8,128)(2,1)S(1)}, u32[]{:S(2)}, u32[]{:S(2)}) collective-permute-start(bf16[4,512,128]{2,1,0:T(8,128)(2,1)S(1)} %gate.1.refs_0_), channel_id=1, source_target_pairs={{0,16},{16,0},{32,48},{48,32},{64,80},{80,64},{96,112},{112,96},{1... | collective-permute-start | bytes 1572872 | tf_op jit(solution)/shard_map/ppermute | solution.py:348
  63.0 9.9 %copy-start.1 = (f32[128,128]{1,0:T(8,128)S(1)}, f32[128,128]{1,0:T(8,128)}, u32[]{:S(2)}) copy-start(f32[128,128]{1,0:T(8,128)} %get-tuple-element.21.vq) | copy-start | bytes 196612
  63.0 9.9 %copy-start.2 = (f32[128,128]{1,0:T(8,128)S(1)}, f32[128,128]{1,0:T(8,128)}, u32[]{:S(2)}) copy-start(f32[128,128]{1,0:T(8,128)} %get-tuple-element.22.nv) | copy-start | bytes 196612
  63.1 9.9 %copy-start.3 = (f32[128,128]{1,0:T(8,128)S(1)}, f32[128,128]{1,0:T(8,128)}, u32[]{:S(2)}) copy-start(f32[128,128]{1,0:T(8,128)} %get-tuple-element.23.pos) | copy-start | bytes 196612

commit v9 on v8

--- a/solution.py
+++ b/solution.py
@@ -378,7 +378,7 @@
     gathered = over_rows(share)
     own_y = [cols] + [
         lax.ppermute(cols, "row", [(i, (i + 2 * k) % n_row) for i in range(n_row)])
-        for k in range(1, n_row // 2)
+        for k in (1, 3, 2)
     ]
     other_y = [other_core(c) for c in own_y]
     stacked = jax.ShapeDtypeStruct((len(own_y),) + cols.shape, BF16)

time: 91.5 us -> 91.5 us (level)
  blocking collectives: 26 us -> 27.3 us
  starting transfers between devices: 22.9 us -> 21.7 us
    ppermute x5, starting transfers between devices: 9.15 us -> 7 us  [other_core(): return lax.ppermute(value, 'row', [(i, i ^ 1) for i in range(n_row)])]
    all_to_all x1, blocking collectives: 16.1 us -> 17.4 us  [body(): lax.all_to_all(send, ('row', 'col'), split_axis=0, concat_axis=0, tiled=T...]
  transfers between devices with their start and end apart: 10 -> 10, of which waited for: 3 -> 2; matrix products, arithmetic and copies ran while one was open for 0% -> 0% of each run, Pallas kernels for 19% -> 19%
where the time goes in v9:
time: 91.5 us; the launch traced here: 91.2 us
  Pallas kernels  39.3 us (43%)
  blocking collectives  27.3 us (30%)
  starting transfers between devices  21.7 us (24%)
  waiting for transfers between devices  2.18 us (2%)
    pallas_call x2, Pallas kernels, product_call(): pl.pallas_call(functools.partial(product_kernel, 2048, len(cols), bool(be...  33.9 us
    all_to_all x1, blocking collectives, body(): lax.all_to_all(send, ('row', 'col'), split_axis=0, concat_axis=0, tiled=T...  17.4 us
    all_to_all x1, blocking collectives, over_rows(): lax.all_to_all(value, 'col', split_axis=0, concat_axis=0, tiled=True, axi...  9.87 us
    ppermute x5, starting transfers between devices, other_core(): return lax.ppermute(value, 'row', [(i, i ^ 1) for i in range(n_row)])  7 us
    all_to_all x1, starting transfers between devices, over_rows(): lax.all_to_all(value, 'col', split_axis=0, concat_axis=0, tiled=True, axi...  6.34 us
    ppermute x3, starting transfers between devices, body(): lax.ppermute(cols, 'row', [(i, (i + 2 * k) % n_row) for i in range(n_row)])  4.46 us
    ppermute x1, starting transfers between devices, body(): pair_y = lax.ppermute(pair_y, 'col', [(i, i ^ 3) for i in range(n_col)])  3.86 us
    pallas_call x1, Pallas kernels, body(): pl.pallas_call(pack_kernel, in_specs=[VMEM] * 11, out_specs=[VMEM] * 6, o...  3.2 us
  transfers between devices with their start and end apart: 10, of which 2 were waited for; matrix products, arithmetic and copies ran while one was open for 0% of the time, Pallas kernels for 19%

profile of v9, /device:TPU:1, one launch (start us, length us, event | category | flops | bytes accessed | tf_op | source)
XLA Modules:
  0.0 91.2 jit_solution(6846189506045466810)
XLA Ops:
  0.6 3.2 %pack.1 = (bf16[512,128]{1,0:T(8,128)(2,1)}, bf16[8,272,128]{2,1,0:T(8,128)(2,1)}, f32[128,128]{1,0:T(8,128)}, f32[128,128]{1,0:T(8,128)}, f32[128,128]{1,0:T(8,128)}, /*index=5*/f32[8,256]{1,0:T(8,128)}) custom-call(bf16[64,512]{1,0:T(8,128)(2,1)} %bitcast.15, s32[1,512]{1,0:T(1,128)} %bitcast.18, s32[1,256]{1,0:T(1,128)} %bitcast.20, s32[1,512]{1,0:T(1,128)} %bitcast.19, ...), custom_call_target="tpu_custom_call" | custom-call | tf_op jit(solution)/shard_map/pack/pallas_call | solution.py:351
  3.8 0.0 copy-start
  3.8 6.3 %all-to-all-start = ((bf16[8,272,128]{2,1,0:T(8,128)(2,1)}), bf16[8,272,128]{2,1,0:T(8,128)(2,1)S(1)}, u32[]{:S(2)}, u32[]{:S(2)}) async-start(bf16[8,272,128]{2,1,0:T(8,128)(2,1)} %get-tuple-element.17), calls=%async_computation | async-start | bytes 1114112 | tf_op jit(solution)/shard_map/all_to_all | solution.py:343
  10.2 0.0 copy-done
  10.2 3.0 %collective-permute-start.2 = (bf16[512,128]{1,0:T(8,128)(2,1)S(1)}, bf16[512,128]{1,0:T(8,128)(2,1)S(1)}, u32[]{:S(2)}, u32[]{:S(2)}) collective-permute-start(bf16[512,128]{1,0:T(8,128)(2,1)S(1)} %copy-done), channel_id=1, source_target_pairs={{0,64},{16,80},{32,96},{48,112},{64,0},{80,16},{96,32},{112,48},{1... | collective-permute-start | bytes 393224 | tf_op jit(solution)/shard_map/ppermute | solution.py:380
  13.2 0.8 collective-permute-start.1
  14.0 0.7 collective-permute-start
  14.6 1.8 %collective-permute-start.4 = (bf16[512,128]{1,0:T(8,128)(2,1)S(1)}, bf16[512,128]{1,0:T(8,128)(2,1)S(1)}, u32[]{:S(2)}, u32[]{:S(2)}) collective-permute-start(bf16[512,128]{1,0:T(8,128)(2,1)S(1)} %copy-done), channel_id=1, source_target_pairs={{0,16},{16,0},{32,48},{48,32},{64,80},{80,64},{96,112},{112,96},{1... | collective-permute-start | bytes 393224 | tf_op jit(solution)/shard_map/ppermute | solution.py:348
  16.4 0.0 collective-permute-done.2.refs_3_
  16.4 2.0 %collective-permute-start.7 = (bf16[512,128]{1,0:T(8,128)(2,1)S(1)}, bf16[512,128]{1,0:T(8,128)(2,1)S(1)}, u32[]{:S(2)}, u32[]{:S(2)}) collective-permute-start(bf16[512,128]{1,0:T(8,128)(2,1)S(1)} %collective-permute-done.2.refs_3_), channel_id=1, source_target_pairs={{0,16},{16,0},{32,48},{48,32},{64,80},{80,64},{96,112},{112,96},{1... | collective-permute-start | bytes 393224 | tf_op jit(solution)/shard_map/ppermute | solution.py:348
  18.4 0.5 collective-permute-done.1.refs_2_
  19.0 1.9 %collective-permute-start.6 = (bf16[512,128]{1,0:T(8,128)(2,1)S(1)}, bf16[512,128]{1,0:T(8,128)(2,1)S(1)}, u32[]{:S(2)}, u32[]{:S(2)}) collective-permute-start(bf16[512,128]{1,0:T(8,128)(2,1)S(1)} %collective-permute-done.1.refs_2_), channel_id=1, source_target_pairs={{0,16},{16,0},{32,48},{48,32},{64,80},{80,64},{96,112},{112,96},{1... | collective-permute-start | bytes 393224 | tf_op jit(solution)/shard_map/ppermute | solution.py:348
  20.8 0.0 collective-permute-done.refs_1_
  20.8 0.8 collective-permute-start.5
  21.6 0.0 copy-start.4
  21.7 3.9 %collective-permute-start.3 = (bf16[4,512,128]{2,1,0:T(8,128)(2,1)S(1)}, bf16[4,512,128]{2,1,0:T(8,128)(2,1)S(1)}, u32[]{:S(2)}, u32[]{:S(2)}) collective-permute-start(bf16[4,512,128]{2,1,0:T(8,128)(2,1)S(1)} %stack.1), channel_id=1, source_target_pairs={{0,3},{1,2},{2,1},{3,0},{4,7},{5,6},{6,5},{7,4},{8,11},{9,10},{10,... | collective-permute-start | bytes 1572872 | tf_op jit(solution)/shard_map/ppermute | solution.py:394
  25.5 0.0 collective-permute-done.4.refs_4_
  25.6 0.0 collective-permute-done.7.refs_7_
  25.6 0.0 collective-permute-done.6.refs_6_
  25.6 0.0 collective-permute-done.5.refs_5_
  25.6 0.0 all-to-all-done.gathered
  25.6 0.0 copy-done.4
  25.6 16.9 %product.2.refs_1_.refs_2_ = f32[8,128,128]{2,1,0:T(8,128)S(1)} custom-call(s32[1]{0:T(128)} %bitcast.own_chunk.col, f32[8,256]{1,0:T(8,128)S(1)} %copy-done.4, bf16[8,272,128]{2,1,0:T(8,128)(2,1)S(1)} %all-to-all-done.gathered, bf16[512,128]{1,0:T(8,128)(2,1)S(1)} %copy-done, bf16[512,128]{1,0:T(8,128)(2,1)S(1)} %collective-permute-done.refs_1_, ...), custom_call_target="tpu_custom_call" | custom-call | flops 17179869184 | bytes 4194304 | tf_op jit(solution)/shard_map/product/pallas_call | solution.py:236
  42.5 0.0 collective-permute-done.3.refs_0_
  42.6 0.5 collective-permute-start.8
  43.1 1.6 %collective-permute-done.8.refs_1_ = bf16[4,512,128]{2,1,0:T(8,128)(2,1)S(1)} collective-permute-done((bf16[4,512,128]{2,1,0:T(8,128)(2,1)S(1)}, bf16[4,512,128]{2,1,0:T(8,128)(2,1)S(1)}, u32[]{:S(2)}, u32[]{:S(2)}) %collective-permute-start.8) | collective-permute-done | bytes 524320 | tf_op jit(solution)/shard_map/ppermute | solution.py:348
  44.8 17.0 %product.3 = (bf16[8,128,128]{2,1,0:T(8,128)(2,1)S(1)}, f32[128,128]{1,0:T(8,128)S(1)}) custom-call(s32[1]{0:T(128)} %bitcast.own_chunk.col, f32[8,256]{1,0:T(8,128)S(1)} %copy-done.4, bf16[8,272,128]{2,1,0:T(8,128)(2,1)S(1)} %all-to-all-done.gathered, bf16[4,512,128]{2,1,0:T(8,128)(2,1)S(1)} %gate.1.refs_0_, ...), custom_call_target="tpu_custom_call" | custom-call | flops 17179869184 | bytes 4194304 | tf_op jit(solution)/shard_map/product/pallas_call | solution.py:236
  61.8 0.0 copy-start.1
  61.8 0.0 copy-start.2
  61.8 0.0 copy-start.3
  61.8 9.9 %all_to_all.15.parts = bf16[8,128,128]{2,1,0:T(8,128)(2,1)S(1)} all-to-all(bf16[8,128,128]{2,1,0:T(8,128)(2,1)S(1)} %get-tuple-element.19), channel_id=1, replica_groups={{0,1,4,5,8,9,12,13},{2,3,6,7,10,11,14,15},{16,17,20,21,24,25,28,29},{18..., dimensions={0} | all-to-all | bytes 524288 | tf_op jit(solution)/shard_map/all_to_all | solution.py:343
  71.7 0.0 copy-done.1
  71.7 0.0 copy-done.2
  71.7 0.0 copy-done.3
  71.7 0.4 image.1
  72.1 17.4 %all_to_all.16.got = f32[128,1,384]{2,1,0:T(1,128)S(1)} all-to-all(f32[128,1,384]{2,1,0:T(1,128)S(1)} %image.1), channel_id=1, replica_groups=mesh['row'=8,'col'=16] {'row','col'}, dimensions={0} | all-to-all | bytes 393216 | tf_op jit(solution)/shard_map/all_to_all | solution.py:414
  89.5 1.7 %final.1 = (f32[32,512]{1,0:T(8,128)}, f32[32,512]{1,0:T(8,128)}, f32[1,32]{1,0:T(1,128)}, f32[1,32]{1,0:T(1,128)}) custom-call(f32[128,1,384]{2,1,0:T(1,128)S(1)} %all_to_all.16.got), custom_call_target="tpu_custom_call" | custom-call | tf_op jit(solution)/shard_map/final/pallas_call | solution.py:415
  (2 shorter events, 0.1 us)
Async XLA Ops:
  3.8 6.3 %copy-start = (bf16[512,128]{1,0:T(8,128)(2,1)S(1)}, bf16[512,128]{1,0:T(8,128)(2,1)}, u32[]{:S(2)}) copy-start(bf16[512,128]{1,0:T(8,128)(2,1)} %get-tuple-element.18.refs_0_) | copy-start | bytes 393220
  3.8 21.7 %all-to-all-start = ((bf16[8,272,128]{2,1,0:T(8,128)(2,1)}), bf16[8,272,128]{2,1,0:T(8,128)(2,1)S(1)}, u32[]{:S(2)}, u32[]{:S(2)}) async-start(bf16[8,272,128]{2,1,0:T(8,128)(2,1)} %get-tuple-element.17), calls=%async_computation | async-start | bytes 1114112 | tf_op jit(solution)/shard_map/all_to_all | solution.py:343
  10.2 6.3 %collective-permute-start.2 = (bf16[512,128]{1,0:T(8,128)(2,1)S(1)}, bf16[512,128]{1,0:T(8,128)(2,1)S(1)}, u32[]{:S(2)}, u32[]{:S(2)}) collective-permute-start(bf16[512,128]{1,0:T(8,128)(2,1)S(1)} %copy-done), channel_id=1, source_target_pairs={{0,64},{16,80},{32,96},{48,112},{64,0},{80,16},{96,32},{112,48},{1... | collective-permute-start | bytes 393224 | tf_op jit(solution)/shard_map/ppermute | solution.py:380
  13.2 5.8 %collective-permute-start.1 = (bf16[512,128]{1,0:T(8,128)(2,1)S(1)}, bf16[512,128]{1,0:T(8,128)(2,1)S(1)}, u32[]{:S(2)}, u32[]{:S(2)}) collective-permute-start(bf16[512,128]{1,0:T(8,128)(2,1)S(1)} %copy-done), channel_id=1, source_target_pairs={{0,96},{16,112},{32,0},{48,16},{64,32},{80,48},{96,64},{112,80},{1... | collective-permute-start | bytes 393224 | tf_op jit(solution)/shard_map/ppermute | solution.py:380
  14.0 6.9 %collective-permute-start = (bf16[512,128]{1,0:T(8,128)(2,1)S(1)}, bf16[512,128]{1,0:T(8,128)(2,1)S(1)}, u32[]{:S(2)}, u32[]{:S(2)}) collective-permute-start(bf16[512,128]{1,0:T(8,128)(2,1)S(1)} %copy-done), channel_id=1, source_target_pairs={{0,32},{16,48},{32,64},{48,80},{64,96},{80,112},{96,0},{112,16},{1... | collective-permute-start | bytes 393224 | tf_op jit(solution)/shard_map/ppermute | solution.py:380
  14.6 10.9 %collective-permute-start.4 = (bf16[512,128]{1,0:T(8,128)(2,1)S(1)}, bf16[512,128]{1,0:T(8,128)(2,1)S(1)}, u32[]{:S(2)}, u32[]{:S(2)}) collective-permute-start(bf16[512,128]{1,0:T(8,128)(2,1)S(1)} %copy-done), channel_id=1, source_target_pairs={{0,16},{16,0},{32,48},{48,32},{64,80},{80,64},{96,112},{112,96},{1... | collective-permute-start | bytes 393224 | tf_op jit(solution)/shard_map/ppermute | solution.py:348
  16.4 9.1 %collective-permute-start.7 = (bf16[512,128]{1,0:T(8,128)(2,1)S(1)}, bf16[512,128]{1,0:T(8,128)(2,1)S(1)}, u32[]{:S(2)}, u32[]{:S(2)}) collective-permute-start(bf16[512,128]{1,0:T(8,128)(2,1)S(1)} %collective-permute-done.2.refs_3_), channel_id=1, source_target_pairs={{0,16},{16,0},{32,48},{48,32},{64,80},{80,64},{96,112},{112,96},{1... | collective-permute-start | bytes 393224 | tf_op jit(solution)/shard_map/ppermute | solution.py:348
  19.0 6.6 %collective-permute-start.6 = (bf16[512,128]{1,0:T(8,128)(2,1)S(1)}, bf16[512,128]{1,0:T(8,128)(2,1)S(1)}, u32[]{:S(2)}, u32[]{:S(2)}) collective-permute-start(bf16[512,128]{1,0:T(8,128)(2,1)S(1)} %collective-permute-done.1.refs_2_), channel_id=1, source_target_pairs={{0,16},{16,0},{32,48},{48,32},{64,80},{80,64},{96,112},{112,96},{1... | collective-permute-start | bytes 393224 | tf_op jit(solution)/shard_map/ppermute | solution.py:348
  20.8 4.7 %collective-permute-start.5 = (bf16[512,128]{1,0:T(8,128)(2,1)S(1)}, bf16[512,128]{1,0:T(8,128)(2,1)S(1)}, u32[]{:S(2)}, u32[]{:S(2)}) collective-permute-start(bf16[512,128]{1,0:T(8,128)(2,1)S(1)} %collective-permute-done.refs_1_), channel_id=1, source_target_pairs={{0,16},{16,0},{32,48},{48,32},{64,80},{80,64},{96,112},{112,96},{1... | collective-permute-start | bytes 393224 | tf_op jit(solution)/shard_map/ppermute | solution.py:348
  21.6 3.9 %copy-start.4 = (f32[8,256]{1,0:T(8,128)S(1)}, f32[8,256]{1,0:T(8,128)}, u32[]{:S(2)}) copy-start(f32[8,256]{1,0:T(8,128)} %get-tuple-element.16.table) | copy-start | bytes 24580
  21.7 20.9 %collective-permute-start.3 = (bf16[4,512,128]{2,1,0:T(8,128)(2,1)S(1)}, bf16[4,512,128]{2,1,0:T(8,128)(2,1)S(1)}, u32[]{:S(2)}, u32[]{:S(2)}) collective-permute-start(bf16[4,512,128]{2,1,0:T(8,128)(2,1)S(1)} %stack.1), channel_id=1, source_target_pairs={{0,3},{1,2},{2,1},{3,0},{4,7},{5,6},{6,5},{7,4},{8,11},{9,10},{10,... | collective-permute-start | bytes 1572872 | tf_op jit(solution)/shard_map/ppermute | solution.py:394
  42.6 2.2 %collective-permute-start.8 = (bf16[4,512,128]{2,1,0:T(8,128)(2,1)S(1)}, bf16[4,512,128]{2,1,0:T(8,128)(2,1)S(1)}, u32[]{:S(2)}, u32[]{:S(2)}) collective-permute-start(bf16[4,512,128]{2,1,0:T(8,128)(2,1)S(1)} %gate.1.refs_0_), channel_id=1, source_target_pairs={{0,16},{16,0},{32,48},{48,32},{64,80},{80,64},{96,112},{112,96},{1... | collective-permute-start | bytes 1572872 | tf_op jit(solution)/shard_map/ppermute | solution.py:348
  61.8 9.9 %copy-start.1 = (f32[128,128]{1,0:T(8,128)S(1)}, f32[128,128]{1,0:T(8,128)}, u32[]{:S(2)}) copy-start(f32[128,128]{1,0:T(8,128)} %get-tuple-element.21.vq) | copy-start | bytes 196612
  61.8 9.9 %copy-start.2 = (f32[128,128]{1,0:T(8,128)S(1)}, f32[128,128]{1,0:T(8,128)}, u32[]{:S(2)}) copy-start(f32[128,128]{1,0:T(8,128)} %get-tuple-element.22.nv) | copy-start | bytes 196612
  61.8 9.9 %copy-start.3 = (f32[128,128]{1,0:T(8,128)S(1)}, f32[128,128]{1,0:T(8,128)}, u32[]{:S(2)}) copy-start(f32[128,128]{1,0:T(8,128)} %get-tuple-element.23.pos) | copy-start | bytes 196612

commit v10 on v8

--- a/solution.py
+++ b/solution.py
@@ -51,7 +51,7 @@
 
 def pack_kernel(
     feat, tid, cnt, rank, probes, net_w, net_b, scale, mix, diag, noise_in,
-    cols, rows_out, vq_out, nv_out, pos_out, table_out,
+    cols, rows_out, vq_out, nv_out, pos_out, table_out, held,
 ):
     rows = feat.shape[1]
     width = probes.shape[0]
@@ -85,17 +85,15 @@
         axis=0,
     ).astype(BF16)
     whole = jnp.concatenate([latent, probes[...], extra], axis=0)
-    tile = jnp.floor(order * (1.0 / 64.0))
-    inner = order - tile * 64.0
-    block = jnp.floor(inner * 0.25)
-    order_r = tile * 64.0 + (inner - block * 4.0) * 16.0 + block
     square = iota((rows, rows), 0)
     place_c = (square == order.astype(jnp.int32)).astype(BF16)
-    place_r = (square == order_r.astype(jnp.int32)).astype(BF16)
     turn = (((1,), (1,)), ((), ()))
-    data = lax.dot_general(place_c, whole, turn, preferred_element_type=F32).astype(BF16)
+    held[...] = lax.dot_general(place_c, whole, turn, preferred_element_type=F32)
+    data = held[...].astype(BF16)
     cols[...] = data
-    data = lax.dot_general(place_r, whole, turn, preferred_element_type=F32)
+    data = jnp.concatenate(
+        [held[pl.ds(t + m, 16, stride=4), :] for t in range(0, rows, 64) for m in range(4)], axis=0
+    )
     half = rows // 2
     pair = jnp.concatenate([data[:half, :V0], data[half:, :V0]], axis=1).astype(BF16)
     at = (iota((16, rows), 1) % 16 == iota((16, rows), 0)).astype(BF16)
@@ -360,6 +358,7 @@
             shape,
             jax.ShapeDtypeStruct((8, task_count.shape[0]), F32),
         ],
+        scratch_shapes=[pltpu.VMEM((rows, 128), F32)],
         compiler_params=ALONE,
         name="pack",
     )(

time: 91.5 us -> 91.4 us (level)
  waiting for transfers between devices: 2.21 us -> 4.06 us
  starting transfers between devices: 22.9 us -> 21.1 us
    ppermute x5, starting transfers between devices: 9.15 us -> 7.31 us  [other_core(): return lax.ppermute(value, 'row', [(i, i ^ 1) for i in range(n_row)])]
    ppermute x3, waiting for transfers between devices: 0.59 us -> 2.42 us  [body(): lax.ppermute(cols, 'row', [(i, (i + 2 * k) % n_row) for i in range(n_row)])]
where the time goes in v10:
time: 91.4 us; the launch traced here: 91 us
  Pallas kernels  39.2 us (43%)
  blocking collectives  25.9 us (28%)
  starting transfers between devices  21.1 us (23%)
  waiting for transfers between devices  4.06 us (4%)
    pallas_call x2, Pallas kernels, product_call(): pl.pallas_call(functools.partial(product_kernel, 2048, len(cols), bool(be...  33.9 us
    all_to_all x1, blocking collectives, body(): lax.all_to_all(send, ('row', 'col'), split_axis=0, concat_axis=0, tiled=T...  16.1 us
    all_to_all x1, blocking collectives, over_rows(): lax.all_to_all(value, 'col', split_axis=0, concat_axis=0, tiled=True, axi...  9.86 us
    ppermute x5, starting transfers between devices, other_core(): return lax.ppermute(value, 'row', [(i, i ^ 1) for i in range(n_row)])  7.31 us
    all_to_all x1, starting transfers between devices, over_rows(): lax.all_to_all(value, 'col', split_axis=0, concat_axis=0, tiled=True, axi...  6.34 us
    ppermute x3, starting transfers between devices, body(): lax.ppermute(cols, 'row', [(i, (i + 2 * k) % n_row) for i in range(n_row)])  3.84 us
    ppermute x1, starting transfers between devices, body(): pair_y = lax.ppermute(pair_y, 'col', [(i, i ^ 3) for i in range(n_col)])  3.59 us
    pallas_call x1, Pallas kernels, body(): pl.pallas_call(pack_kernel, in_specs=[VMEM] * 11, out_specs=[VMEM] * 6, o...  3.07 us
  transfers between devices with their start and end apart: 10, of which 3 were waited for; matrix products, arithmetic and copies ran while one was open for 0% of the time, Pallas kernels for 19%

profile of v10, /device:TPU:1, one launch (start us, length us, event | category | flops | bytes accessed | tf_op | source)
XLA Modules:
  0.0 91.0 jit_solution(237368453837405657)
XLA Ops:
  0.6 3.1 %pack.1 = (bf16[512,128]{1,0:T(8,128)(2,1)}, bf16[8,272,128]{2,1,0:T(8,128)(2,1)}, f32[128,128]{1,0:T(8,128)}, f32[128,128]{1,0:T(8,128)}, f32[128,128]{1,0:T(8,128)}, /*index=5*/f32[8,256]{1,0:T(8,128)}) custom-call(bf16[64,512]{1,0:T(8,128)(2,1)} %bitcast.15, s32[1,512]{1,0:T(1,128)} %bitcast.18, s32[1,256]{1,0:T(1,128)} %bitcast.20, s32[1,512]{1,0:T(1,128)} %bitcast.19, ...), custom_call_target="tpu_custom_call" | custom-call | tf_op jit(solution)/shard_map/pack/pallas_call | solution.py:349
  3.7 0.0 copy-start
  3.7 6.3 %all-to-all-start = ((bf16[8,272,128]{2,1,0:T(8,128)(2,1)}), bf16[8,272,128]{2,1,0:T(8,128)(2,1)S(1)}, u32[]{:S(2)}, u32[]{:S(2)}) async-start(bf16[8,272,128]{2,1,0:T(8,128)(2,1)} %get-tuple-element.17), calls=%async_computation | async-start | bytes 1114112 | tf_op jit(solution)/shard_map/all_to_all | solution.py:341
  10.0 0.0 copy-done
  10.0 2.8 %collective-permute-start.2 = (bf16[512,128]{1,0:T(8,128)(2,1)S(1)}, bf16[512,128]{1,0:T(8,128)(2,1)S(1)}, u32[]{:S(2)}, u32[]{:S(2)}) collective-permute-start(bf16[512,128]{1,0:T(8,128)(2,1)S(1)} %copy-done), channel_id=1, source_target_pairs={{0,96},{16,112},{32,0},{48,16},{64,32},{80,48},{96,64},{112,80},{1... | collective-permute-start | bytes 393224 | tf_op jit(solution)/shard_map/ppermute | solution.py:379
  12.9 0.3 collective-permute-start.1
  13.2 0.7 collective-permute-start
  13.9 1.8 %collective-permute-start.4 = (bf16[512,128]{1,0:T(8,128)(2,1)S(1)}, bf16[512,128]{1,0:T(8,128)(2,1)S(1)}, u32[]{:S(2)}, u32[]{:S(2)}) collective-permute-start(bf16[512,128]{1,0:T(8,128)(2,1)S(1)} %copy-done), channel_id=1, source_target_pairs={{0,16},{16,0},{32,48},{48,32},{64,80},{80,64},{96,112},{112,96},{1... | collective-permute-start | bytes 393224 | tf_op jit(solution)/shard_map/ppermute | solution.py:346
  15.7 2.0 %collective-permute-done.2.refs_3_ = bf16[512,128]{1,0:T(8,128)(2,1)S(1)} collective-permute-done((bf16[512,128]{1,0:T(8,128)(2,1)S(1)}, bf16[512,128]{1,0:T(8,128)(2,1)S(1)}, u32[]{:S(2)}, u32[]{:S(2)}) %collective-permute-start.2) | collective-permute-done | bytes 131104 | tf_op jit(solution)/shard_map/ppermute | solution.py:379
  17.7 1.7 %collective-permute-start.7 = (bf16[512,128]{1,0:T(8,128)(2,1)S(1)}, bf16[512,128]{1,0:T(8,128)(2,1)S(1)}, u32[]{:S(2)}, u32[]{:S(2)}) collective-permute-start(bf16[512,128]{1,0:T(8,128)(2,1)S(1)} %collective-permute-done.2.refs_3_), channel_id=1, source_target_pairs={{0,16},{16,0},{32,48},{48,32},{64,80},{80,64},{96,112},{112,96},{1... | collective-permute-start | bytes 393224 | tf_op jit(solution)/shard_map/ppermute | solution.py:346
  19.4 0.0 collective-permute-done.1.refs_2_
  19.4 2.3 %collective-permute-start.6 = (bf16[512,128]{1,0:T(8,128)(2,1)S(1)}, bf16[512,128]{1,0:T(8,128)(2,1)S(1)}, u32[]{:S(2)}, u32[]{:S(2)}) collective-permute-start(bf16[512,128]{1,0:T(8,128)(2,1)S(1)} %collective-permute-done.1.refs_2_), channel_id=1, source_target_pairs={{0,16},{16,0},{32,48},{48,32},{64,80},{80,64},{96,112},{112,96},{1... | collective-permute-start | bytes 393224 | tf_op jit(solution)/shard_map/ppermute | solution.py:346
  21.7 0.4 collective-permute-done.refs_1_
  22.1 1.0 %collective-permute-start.5 = (bf16[512,128]{1,0:T(8,128)(2,1)S(1)}, bf16[512,128]{1,0:T(8,128)(2,1)S(1)}, u32[]{:S(2)}, u32[]{:S(2)}) collective-permute-start(bf16[512,128]{1,0:T(8,128)(2,1)S(1)} %collective-permute-done.refs_1_), channel_id=1, source_target_pairs={{0,16},{16,0},{32,48},{48,32},{64,80},{80,64},{96,112},{112,96},{1... | collective-permute-start | bytes 393224 | tf_op jit(solution)/shard_map/ppermute | solution.py:346
  23.1 0.0 copy-start.4
  23.1 3.6 %collective-permute-start.3 = (bf16[4,512,128]{2,1,0:T(8,128)(2,1)S(1)}, bf16[4,512,128]{2,1,0:T(8,128)(2,1)S(1)}, u32[]{:S(2)}, u32[]{:S(2)}) collective-permute-start(bf16[4,512,128]{2,1,0:T(8,128)(2,1)S(1)} %stack.1), channel_id=1, source_target_pairs={{0,3},{1,2},{2,1},{3,0},{4,7},{5,6},{6,5},{7,4},{8,11},{9,10},{10,... | collective-permute-start | bytes 1572872 | tf_op jit(solution)/shard_map/ppermute | solution.py:393
  26.7 0.0 collective-permute-done.4.refs_4_
  26.7 0.0 collective-permute-done.7.refs_7_
  26.7 0.0 collective-permute-done.6.refs_6_
  26.7 0.0 collective-permute-done.5.refs_5_
  26.7 0.0 all-to-all-done.gathered
  26.7 0.0 copy-done.4
  26.8 16.9 %product.2.refs_1_.refs_2_ = f32[8,128,128]{2,1,0:T(8,128)S(1)} custom-call(s32[1]{0:T(128)} %bitcast.own_chunk.col, f32[8,256]{1,0:T(8,128)S(1)} %copy-done.4, bf16[8,272,128]{2,1,0:T(8,128)(2,1)S(1)} %all-to-all-done.gathered, bf16[512,128]{1,0:T(8,128)(2,1)S(1)} %copy-done, bf16[512,128]{1,0:T(8,128)(2,1)S(1)} %collective-permute-done.refs_1_, ...), custom_call_target="tpu_custom_call" | custom-call | flops 17179869184 | bytes 4194304 | tf_op jit(solution)/shard_map/product/pallas_call | solution.py:234
  43.7 0.0 collective-permute-done.3.refs_0_
  43.8 0.5 collective-permute-start.8
  44.3 1.6 %collective-permute-done.8.refs_1_ = bf16[4,512,128]{2,1,0:T(8,128)(2,1)S(1)} collective-permute-done((bf16[4,512,128]{2,1,0:T(8,128)(2,1)S(1)}, bf16[4,512,128]{2,1,0:T(8,128)(2,1)S(1)}, u32[]{:S(2)}, u32[]{:S(2)}) %collective-permute-start.8) | collective-permute-done | bytes 524320 | tf_op jit(solution)/shard_map/ppermute | solution.py:346
  45.9 17.0 %product.3 = (bf16[8,128,128]{2,1,0:T(8,128)(2,1)S(1)}, f32[128,128]{1,0:T(8,128)S(1)}) custom-call(s32[1]{0:T(128)} %bitcast.own_chunk.col, f32[8,256]{1,0:T(8,128)S(1)} %copy-done.4, bf16[8,272,128]{2,1,0:T(8,128)(2,1)S(1)} %all-to-all-done.gathered, bf16[4,512,128]{2,1,0:T(8,128)(2,1)S(1)} %gate.1.refs_0_, ...), custom_call_target="tpu_custom_call" | custom-call | flops 17179869184 | bytes 4194304 | tf_op jit(solution)/shard_map/product/pallas_call | solution.py:234
  62.9 0.0 copy-start.1
  62.9 0.0 copy-start.2
  62.9 0.0 copy-start.3
  62.9 9.9 %all_to_all.15.parts = bf16[8,128,128]{2,1,0:T(8,128)(2,1)S(1)} all-to-all(bf16[8,128,128]{2,1,0:T(8,128)(2,1)S(1)} %get-tuple-element.19), channel_id=1, replica_groups={{0,1,4,5,8,9,12,13},{2,3,6,7,10,11,14,15},{16,17,20,21,24,25,28,29},{18..., dimensions={0} | all-to-all | bytes 524288 | tf_op jit(solution)/shard_map/all_to_all | solution.py:341
  72.8 0.0 copy-done.1
  72.8 0.0 copy-done.2
  72.8 0.0 copy-done.3
  72.8 0.4 image.1
  73.2 16.1 %all_to_all.16.got = f32[128,1,384]{2,1,0:T(1,128)S(1)} all-to-all(f32[128,1,384]{2,1,0:T(1,128)S(1)} %image.1), channel_id=1, replica_groups=mesh['row'=8,'col'=16] {'row','col'}, dimensions={0} | all-to-all | bytes 393216 | tf_op jit(solution)/shard_map/all_to_all | solution.py:413
  89.3 1.7 %final.1 = (f32[32,512]{1,0:T(8,128)}, f32[32,512]{1,0:T(8,128)}, f32[1,32]{1,0:T(1,128)}, f32[1,32]{1,0:T(1,128)}) custom-call(f32[128,1,384]{2,1,0:T(1,128)S(1)} %all_to_all.16.got), custom_call_target="tpu_custom_call" | custom-call | tf_op jit(solution)/shard_map/final/pallas_call | solution.py:414
  (2 shorter events, 0.1 us)
Async XLA Ops:
  3.7 6.3 %copy-start = (bf16[512,128]{1,0:T(8,128)(2,1)S(1)}, bf16[512,128]{1,0:T(8,128)(2,1)}, u32[]{:S(2)}) copy-start(bf16[512,128]{1,0:T(8,128)(2,1)} %get-tuple-element.18.refs_0_) | copy-start | bytes 393220
  3.7 23.0 %all-to-all-start = ((bf16[8,272,128]{2,1,0:T(8,128)(2,1)}), bf16[8,272,128]{2,1,0:T(8,128)(2,1)S(1)}, u32[]{:S(2)}, u32[]{:S(2)}) async-start(bf16[8,272,128]{2,1,0:T(8,128)(2,1)} %get-tuple-element.17), calls=%async_computation | async-start | bytes 1114112 | tf_op jit(solution)/shard_map/all_to_all | solution.py:341
  10.0 7.6 %collective-permute-start.2 = (bf16[512,128]{1,0:T(8,128)(2,1)S(1)}, bf16[512,128]{1,0:T(8,128)(2,1)S(1)}, u32[]{:S(2)}, u32[]{:S(2)}) collective-permute-start(bf16[512,128]{1,0:T(8,128)(2,1)S(1)} %copy-done), channel_id=1, source_target_pairs={{0,96},{16,112},{32,0},{48,16},{64,32},{80,48},{96,64},{112,80},{1... | collective-permute-start | bytes 393224 | tf_op jit(solution)/shard_map/ppermute | solution.py:379
  12.9 6.5 %collective-permute-start.1 = (bf16[512,128]{1,0:T(8,128)(2,1)S(1)}, bf16[512,128]{1,0:T(8,128)(2,1)S(1)}, u32[]{:S(2)}, u32[]{:S(2)}) collective-permute-start(bf16[512,128]{1,0:T(8,128)(2,1)S(1)} %copy-done), channel_id=1, source_target_pairs={{0,64},{16,80},{32,96},{48,112},{64,0},{80,16},{96,32},{112,48},{1... | collective-permute-start | bytes 393224 | tf_op jit(solution)/shard_map/ppermute | solution.py:379
  13.2 8.9 %collective-permute-start = (bf16[512,128]{1,0:T(8,128)(2,1)S(1)}, bf16[512,128]{1,0:T(8,128)(2,1)S(1)}, u32[]{:S(2)}, u32[]{:S(2)}) collective-permute-start(bf16[512,128]{1,0:T(8,128)(2,1)S(1)} %copy-done), channel_id=1, source_target_pairs={{0,32},{16,48},{32,64},{48,80},{64,96},{80,112},{96,0},{112,16},{1... | collective-permute-start | bytes 393224 | tf_op jit(solution)/shard_map/ppermute | solution.py:379
  13.9 12.8 %collective-permute-start.4 = (bf16[512,128]{1,0:T(8,128)(2,1)S(1)}, bf16[512,128]{1,0:T(8,128)(2,1)S(1)}, u32[]{:S(2)}, u32[]{:S(2)}) collective-permute-start(bf16[512,128]{1,0:T(8,128)(2,1)S(1)} %copy-done), channel_id=1, source_target_pairs={{0,16},{16,0},{32,48},{48,32},{64,80},{80,64},{96,112},{112,96},{1... | collective-permute-start | bytes 393224 | tf_op jit(solution)/shard_map/ppermute | solution.py:346
  17.7 9.0 %collective-permute-start.7 = (bf16[512,128]{1,0:T(8,128)(2,1)S(1)}, bf16[512,128]{1,0:T(8,128)(2,1)S(1)}, u32[]{:S(2)}, u32[]{:S(2)}) collective-permute-start(bf16[512,128]{1,0:T(8,128)(2,1)S(1)} %collective-permute-done.2.refs_3_), channel_id=1, source_target_pairs={{0,16},{16,0},{32,48},{48,32},{64,80},{80,64},{96,112},{112,96},{1... | collective-permute-start | bytes 393224 | tf_op jit(solution)/shard_map/ppermute | solution.py:346
  19.4 7.3 %collective-permute-start.6 = (bf16[512,128]{1,0:T(8,128)(2,1)S(1)}, bf16[512,128]{1,0:T(8,128)(2,1)S(1)}, u32[]{:S(2)}, u32[]{:S(2)}) collective-permute-start(bf16[512,128]{1,0:T(8,128)(2,1)S(1)} %collective-permute-done.1.refs_2_), channel_id=1, source_target_pairs={{0,16},{16,0},{32,48},{48,32},{64,80},{80,64},{96,112},{112,96},{1... | collective-permute-start | bytes 393224 | tf_op jit(solution)/shard_map/ppermute | solution.py:346
  22.1 4.6 %collective-permute-start.5 = (bf16[512,128]{1,0:T(8,128)(2,1)S(1)}, bf16[512,128]{1,0:T(8,128)(2,1)S(1)}, u32[]{:S(2)}, u32[]{:S(2)}) collective-permute-start(bf16[512,128]{1,0:T(8,128)(2,1)S(1)} %collective-permute-done.refs_1_), channel_id=1, source_target_pairs={{0,16},{16,0},{32,48},{48,32},{64,80},{80,64},{96,112},{112,96},{1... | collective-permute-start | bytes 393224 | tf_op jit(solution)/shard_map/ppermute | solution.py:346
  23.1 3.7 %copy-start.4 = (f32[8,256]{1,0:T(8,128)S(1)}, f32[8,256]{1,0:T(8,128)}, u32[]{:S(2)}) copy-start(f32[8,256]{1,0:T(8,128)} %get-tuple-element.16.table) | copy-start | bytes 24580
  23.1 20.6 %collective-permute-start.3 = (bf16[4,512,128]{2,1,0:T(8,128)(2,1)S(1)}, bf16[4,512,128]{2,1,0:T(8,128)(2,1)S(1)}, u32[]{:S(2)}, u32[]{:S(2)}) collective-permute-start(bf16[4,512,128]{2,1,0:T(8,128)(2,1)S(1)} %stack.1), channel_id=1, source_target_pairs={{0,3},{1,2},{2,1},{3,0},{4,7},{5,6},{6,5},{7,4},{8,11},{9,10},{10,... | collective-permute-start | bytes 1572872 | tf_op jit(solution)/shard_map/ppermute | solution.py:393
  43.8 2.2 %collective-permute-start.8 = (bf16[4,512,128]{2,1,0:T(8,128)(2,1)S(1)}, bf16[4,512,128]{2,1,0:T(8,128)(2,1)S(1)}, u32[]{:S(2)}, u32[]{:S(2)}) collective-permute-start(bf16[4,512,128]{2,1,0:T(8,128)(2,1)S(1)} %gate.1.refs_0_), channel_id=1, source_target_pairs={{0,16},{16,0},{32,48},{48,32},{64,80},{80,64},{96,112},{112,96},{1... | collective-permute-start | bytes 1572872 | tf_op jit(solution)/shard_map/ppermute | solution.py:346
  62.9 9.9 %copy-start.1 = (f32[128,128]{1,0:T(8,128)S(1)}, f32[128,128]{1,0:T(8,128)}, u32[]{:S(2)}) copy-start(f32[128,128]{1,0:T(8,128)} %get-tuple-element.21.vq) | copy-start | bytes 196612
  62.9 9.9 %copy-start.2 = (f32[128,128]{1,0:T(8,128)S(1)}, f32[128,128]{1,0:T(8,128)}, u32[]{:S(2)}) copy-start(f32[128,128]{1,0:T(8,128)} %get-tuple-element.22.nv) | copy-start | bytes 196612
  62.9 9.9 %copy-start.3 = (f32[128,128]{1,0:T(8,128)S(1)}, f32[128,128]{1,0:T(8,128)}, u32[]{:S(2)}) copy-start(f32[128,128]{1,0:T(8,128)} %get-tuple-element.23.pos) | copy-start | bytes 196612
